TPU v7x, 32 devices: a whole 2x2x4 slice. The times are simulated.
32 devices in a mesh: groups: 2 (over x), gx: 8 (over z, y), gy: 2 (over core).
Axes of the slice: x: 2, y: 2, z: 4, core: 2. Of those that a mesh axis runs over, the one named last changes fastest.
Arguments:
- tokens: bfloat16 [64, 16384], P('groups', 'gx'), parts along dimension 0, may hold values from -6 to 6
- w_query: bfloat16 [16384, 8192], P('gx', 'gy'), may hold values from -0.046875 to 0.046875
- w_key: bfloat16 [16384, 512], P('gx', 'gy'), may hold values from -0.046875 to 0.046875
- w_value: bfloat16 [16384, 512], P('gx', 'gy'), may hold values from -0.046875 to 0.046875
- w_out: bfloat16 [8192, 16384], P('gy', 'gx'), may hold values from -0.0625 to 0.0625
- key_cache: bfloat16 [64, 4, 1024, 128], P(('groups', 'gx'), 'gy'), parts along dimension 0, may hold values from -600 to 600
- value_cache: bfloat16 [64, 4, 1024, 128], P(('groups', 'gx'), 'gy'), parts along dimension 0, may hold values from -6 to 6
- lengths: int32 [64], P(('groups', 'gx')), parts along dimension 0, may hold values from 2 to 1024, as said below
Outputs:
- attended: bfloat16 [64, 16384], P(('groups', 'gy'), 'gx'), parts along dimension 0
There are 2 independent parts, one for each index of `groups`. A program takes and returns all parts, laid end to end along the dimension named above; an argument that names none is the same for every part. Nothing has to cross between parts.
Inputs may be any that keep to these rules, and one draw needn't show every extreme that they name: `lengths`: every row has 2 or more filled slots; some row has all 1024 slots filled.
All inputs are finite; a program needn't handle non-finite values.
Results may differ from a plain program's by a relative error of at most 0.011.
Values may be sent and summed in bfloat16 or wider, within the bound.
No kernel may reach another device: no remote copies, remote signals or barrier semaphores. Data moves between devices by JAX's collectives and lax.ppermute only.
A program may use at most 128 MiB of HBM per device.

v0:
```python
import jax
import jax.numpy as jnp
from jax import lax
from jax.sharding import PartitionSpec as P

rope_base = 500000.0


def rotate(vectors, positions):
    half = vectors.shape[-1] // 2
    freqs = rope_base ** (-2.0 * jnp.arange(half).astype(jnp.float32) / (2.0 * half))
    angles = positions[:, None] * freqs[None, :]
    cosine = jnp.cos(angles)[:, None, :]
    sine = jnp.sin(angles)[:, None, :]
    first = vectors[..., :half]
    second = vectors[..., half:]
    return jnp.concatenate(
        [first * cosine - second * sine, second * cosine + first * sine], axis=-1
    )


def on_device(tokens, w_query, w_key, w_value, w_out, key_cache, value_cache, lengths):
    rows_dev = key_cache.shape[0]
    kv_local = key_cache.shape[1]
    cache_slots = key_cache.shape[2]
    head_dim = key_cache.shape[3]
    query_cols = w_query.shape[1]
    kv_cols = w_key.shape[1]
    heads_local = query_cols // head_dim
    group = heads_local // kv_local

    def take_rows():
        return tokens

    queries = lax.psum_scatter(
        jnp.dot(take_rows(), w_query, preferred_element_type=jnp.float32),
        "gx",
        scatter_dimension=0,
        tiled=True,
    )
    picked = take_rows()
    key_values = lax.psum_scatter(
        jnp.concatenate(
            [
                jnp.dot(picked, w_key, preferred_element_type=jnp.float32),
                jnp.dot(picked, w_value, preferred_element_type=jnp.float32),
            ],
            axis=1,
        ),
        "gx",
        scatter_dimension=0,
        tiled=True,
    )
    keys_new = key_values[:, :kv_cols]
    values_new = key_values[:, kv_cols:]
    positions = lengths.astype(jnp.float32)
    queries_rot = rotate(queries.reshape(rows_dev, heads_local, head_dim), positions).astype(
        jnp.bfloat16
    )
    queries_rot = queries_rot.reshape(rows_dev, kv_local, group, head_dim)
    keys_rot = rotate(keys_new.reshape(rows_dev, kv_local, head_dim), positions).astype(
        jnp.bfloat16
    )
    values_b = values_new.astype(jnp.bfloat16).reshape(rows_dev, kv_local, head_dim)
    scaling = head_dim ** (-0.5)
    scores = (
        jnp.einsum("rkgd,rkcd->rkgc", queries_rot, key_cache, preferred_element_type=jnp.float32)
        * scaling
    )
    own_score = (
        jnp.einsum("rkgd,rkd->rkg", queries_rot, keys_rot, preferred_element_type=jnp.float32)
        * scaling
    )
    valid = jnp.arange(cache_slots)[None, :] < lengths[:, None]
    scores = jnp.where(valid[:, None, None, :], scores, jnp.float32(-1e30))
    highest = jnp.maximum(jnp.max(scores, axis=-1), own_score)
    weights = jnp.exp(scores - highest[..., None])
    own_weight = jnp.exp(own_score - highest)
    total = jnp.sum(weights, axis=-1) + own_weight
    probs = (weights / total[..., None]).astype(jnp.bfloat16)
    own_prob = (own_weight / total).astype(jnp.bfloat16)
    mixed = jnp.einsum("rkgc,rkcd->rkgd", probs, value_cache, preferred_element_type=jnp.float32)
    mixed = (
        mixed
        + own_prob.astype(jnp.float32)[..., None] * values_b.astype(jnp.float32)[:, :, None, :]
    )
    heads = mixed.astype(jnp.bfloat16).reshape(rows_dev, query_cols)
    terms = jnp.dot(
        lax.all_gather(heads, "gx", axis=0, tiled=True), w_out, preferred_element_type=jnp.float32
    )
    return lax.psum_scatter(terms, "gy", scatter_dimension=0, tiled=True).astype(jnp.bfloat16)


def solution(mesh):
    in_specs = (
        P("groups", "gx"),
        P("gx", "gy"),
        P("gx", "gy"),
        P("gx", "gy"),
        P("gy", "gx"),
        P(("groups", "gx"), "gy", None, None),
        P(("groups", "gx"), "gy", None, None),
        P(("groups", "gx")),
    )
    out_specs = P(("groups", "gy"), "gx")
    return jax.shard_map(
        on_device, mesh=mesh, in_specs=in_specs, out_specs=out_specs, check_vma=False
    )
```

profile of v0, /device:TPU:0, one launch (start us, length us, event | category | flops | bytes accessed | tf_op | source)
XLA Modules:
  0.0 155.1 jit_solution(17177970236067870084)
XLA Ops:
  6.5 0.0 copy-start
  6.5 0.0 all-reduce.5.cloned.1.call-start
  6.6 0.0 copy-start.3
  6.6 9.8 %fusion.13 = f32[32,4096]{1,0:T(8,128)} fusion(bf16[32,2048]{1,0:T(8,128)(2,1)} %param.8, bf16[2048,4096]{1,0:T(8,128)(2,1)} %param.9), kind=kOutput, calls=%fused_computation.35 | convolution fusion | flops 536870912 | bytes 17432576 | tf_op jit(solution)/shard_map/dot_general | solution.py:36
  16.4 0.3 fusion.14
  16.7 0.0 copy-done.3
  16.7 0.3 fusion.15
  17.0 0.6 pad_maximum_fusion
  17.6 0.0 all-reduce.5.cloned.1.call-update
  17.6 0.0 reduce-scatter.2.cloned.1.call-start
  17.7 0.0 copy-done.4
  17.7 0.0 copy-done.5
  17.7 0.6 dynamic-slice
  18.9 0.1 iota_compare_fusion
  19.0 0.1 multiply_cosine_fusion
  19.1 74.5 %all-reduce.5.cloned.1.call-done = (f32[32,4096]{1,0:T(8,128)}, f32[32,512]{1,0:T(8,128)}) async-done(((f32[32,4096]{1,0:T(8,128)}, f32[32,512]{1,0:T(8,128)}), (f32[32,4096]{1,0:T(8,128)}, f32[32,512]{1,0:T(8,128)})) %all-reduce.5.cloned.1.call-update) | async-done | bytes 589840
  93.5 0.7 constant_dynamic-slice_fusion
  94.3 0.9 dynamic-slice_bitcast_fusion
  95.2 0.1 subtract_convert_fusion.1
  95.3 0.1 subtract_convert_fusion
  95.4 0.1 maximum_bitcast_fusion
  95.4 0.2 fusion.5
  95.7 0.8 fusion.12
  96.4 0.2 fusion.2
  96.7 0.8 fusion.7
  97.5 2.0 %fusion.1 = bf16[4,2,16,128]{3,2,1,0:T(8,128)(2,1)S(1)} fusion(bf16[4,2,1024,128]{3,2,1,0:T(8,128)(2,1)} %param.14, f32[4,2,16,1024]{3,2,1,0:T(8,128)S(1)} %get-tuple-element.16, f32[4,2,16]{2,1,0:T(2,128)S(1)} %get-tuple-element.10, f32[4,2,16]{2,1,0:T(2,128)S(1)} %multiply_maximum_fusion, f32[4,2,128]{2,1,0:T(2,128)S(1)} %reshape.96, ...), kind=kOutput, calls=%fused_computation.3 | convolution fusion | flops 33996800 | bytes 2659840 | tf_op jit(solution)/shard_map/rkgc,rkcd->rkgd/dot_general | solution.py:82
  99.6 30.9 %all-gather = bf16[8,4,4096]{2,1,0:T(4,128)(2,1)S(1)} all-gather(bf16[1,4,4096]{2,1,0:T(4,128)(2,1)S(1)} %reshape.97), channel_id=1, replica_groups=mesh['groups'=2,'gx'=8,'gy'=2] {'gx'}, dimensions={0}, use_global_device_ids=true | all-gather | bytes 294912 | tf_op jit(solution)/shard_map/all_gather | solution.py:89
  130.5 0.1 reshape.98
  130.6 9.5 %fusion.16 = f32[32,2048]{1,0:T(8,128)} fusion(bf16[32,4096]{1,0:T(8,128)(2,1)S(1)} %reshape.98, bf16[4096,2048]{1,0:T(8,128)(2,1)} %param.12), kind=kOutput, calls=%fused_computation.38 | convolution fusion | flops 536870912 | bytes 17301504 | tf_op jit(solution)/shard_map/dot_general | solution.py:88
  140.0 0.0 reduce-scatter.2.cloned.1.call-update
  140.0 6.6 %reduce-scatter.2.cloned.1.call-done = f32[16,2048]{1,0:T(8,128)} async-done(((f32[32,2048]{1,0:T(8,128)}), f32[16,2048]{1,0:T(8,128)}) %reduce-scatter.2.cloned.1.call-update) | async-done | bytes 131088 | tf_op jit(solution)/shard_map/reduce_scatter | solution.py:91
  146.7 1.5 convert_element_type.48
  (15 shorter events, 0.1 us)
Async XLA Ops:
  6.5 89.1 %copy-start = (bf16[4,2,1024,128]{3,2,1,0:T(8,128)(2,1)S(1)}, bf16[4,2,1024,128]{3,2,1,0:T(8,128)(2,1)}, u32[]{:S(2)}) copy-start(bf16[4,2,1024,128]{3,2,1,0:T(8,128)(2,1)} %param.13) | copy-start | bytes 6291460
  6.5 11.2 %copy-start.5 = (u32[32]{0:T(128)S(1)}, u32[32]{0:T(128)}, u32[]{:S(2)}) copy-start(u32[32]{0:T(128)} %constant.21) | copy-start | bytes 388
  6.5 9.8 %copy-start.1 = (bf16[32,2048]{1,0:T(8,128)(2,1)S(1)}, bf16[32,2048]{1,0:T(8,128)(2,1)}, u32[]{:S(2)}) copy-start(bf16[32,2048]{1,0:T(8,128)(2,1)} %param.8) | copy-start | bytes 393220
  6.5 9.8 %copy-start.2 = (bf16[2048,256]{1,0:T(8,128)(2,1)S(1)}, bf16[2048,256]{1,0:T(8,128)(2,1)}, u32[]{:S(2)}) copy-start(bf16[2048,256]{1,0:T(8,128)(2,1)} %param.10) | copy-start | bytes 3145732
  6.5 11.1 %copy-start.4 = (s32[4]{0:T(128)S(1)}, s32[4]{0:T(128)}, u32[]{:S(2)}) copy-start(s32[4]{0:T(128)} %param.15) | copy-start | bytes 52
  6.5 87.0 %all-reduce.5.cloned.1.call-start = ((), (), s32[]{:S(2)}) async-start(), calls=%async_computation.2 | async-start | bytes 1179648
  6.6 10.1 %copy-start.3 = (bf16[2048,256]{1,0:T(8,128)(2,1)S(1)}, bf16[2048,256]{1,0:T(8,128)(2,1)}, u32[]{:S(2)}) copy-start(bf16[2048,256]{1,0:T(8,128)(2,1)} %param.11) | copy-start | bytes 3145732
  17.6 129.1 %reduce-scatter.2.cloned.1.call-start = ((), (), s32[]{:S(2)}) async-start(), calls=%async_computation.1 | async-start | bytes 393216 | tf_op jit(solution)/shard_map/reduce_scatter | solution.py:91
Sparse Core Ops, SparseCore 0:
  17.7 75.7 all-reduce.4
  140.2 6.4 reduce-scatter.1
where the time goes:
time: 155 us
  waiting for transfers between devices  81.1 us (52%)
  blocking collectives  30.9 us (20%)
  matrix products  22.8 us (15%)
  between operations  14.1 us (9%)
  other arithmetic  3.67 us (2%)
  local copies, waits for them, and re-layouts  2.35 us (2%)
    unnamed x3, waiting for transfers between devices  74.5 us
    all_gather x1, blocking collectives, on_device(): lax.all_gather(heads, 'gx', axis=0, tiled=True)  30.9 us
    dot_general x1, matrix products, on_device(): jnp.dot(take_rows(), w_query, preferred_element_type=jnp.float32)  9.76 us
    dot_general x1, matrix products, on_device(): jnp.dot(lax.all_gather(heads, 'gx', axis=0, tiled=True), w_out, preferred...  9.45 us
    reduce_scatter x1, waiting for transfers between devices, on_device(): lax.psum_scatter(terms, 'gy', scatter_dimension=0, tiled=True)  6.65 us
  transfers between devices with their start and end apart: 2, of which 2 were waited for; matrix products, arithmetic and copies ran while one was open for 0% of the time, Pallas kernels for 0%

commit v1 on v0

v1 whole, which is shorter than its diff:
```python
import functools

import jax
import jax.numpy as jnp
from jax import lax
from jax.experimental import pallas as pl
from jax.experimental.pallas import tpu as pltpu
from jax.sharding import PartitionSpec as P

rope_base = 500000.0
MIB = 1024 * 1024


def project_kernel(
    n,
    head_dim,
    tokens_ref,
    wq_ref,
    wk_ref,
    wv_ref,
    out_ref,
    t_buf,
    q_buf,
    k_buf,
    v_buf,
    by_head,
    k_rows,
    v_rows,
    sems,
):
    rows = tokens_ref.shape[0]
    chunks, _, width = q_buf.shape
    heads = chunks * width // head_dim
    kv_heads = wk_ref.shape[1] // head_dim
    t_copy = pltpu.make_async_copy(tokens_ref, t_buf, sems.at[2 + chunks])
    k_copy = pltpu.make_async_copy(wk_ref, k_buf, sems.at[0])
    v_copy = pltpu.make_async_copy(wv_ref, v_buf, sems.at[1])
    t_copy.start()
    k_copy.start()
    v_copy.start()
    q_copies = []
    for c in range(chunks):
        copy = pltpu.make_async_copy(
            wq_ref.at[:, c * width : (c + 1) * width], q_buf.at[c], sems.at[2 + c]
        )
        copy.start()
        q_copies.append(copy)
    t_copy.wait()
    tokens = t_buf[...]

    def spread(dest, part, first, count):
        for j in range(part.shape[1] // head_dim):
            dest[pl.ds(first + j, rows, stride=count), :] = part[:, j * head_dim : (j + 1) * head_dim]

    k_copy.wait()
    spread(k_rows, jnp.dot(tokens, k_buf[...], preferred_element_type=jnp.float32), 0, kv_heads)
    v_copy.wait()
    spread(v_rows, jnp.dot(tokens, v_buf[...], preferred_element_type=jnp.float32), 0, kv_heads)
    for c in range(chunks):
        q_copies[c].wait()
        part = jnp.dot(tokens, q_buf[c], preferred_element_type=jnp.float32)
        spread(by_head, part, c * (width // head_dim), heads)
    own = rows // n
    for d in range(n):
        out_ref[d, : own * heads] = by_head[d * own * heads : (d + 1) * own * heads].astype(out_ref.dtype)
        kv = jnp.concatenate(
            [
                k_rows[d * own * kv_heads : (d + 1) * own * kv_heads],
                v_rows[d * own * kv_heads : (d + 1) * own * kv_heads],
            ],
            axis=0,
        )
        out_ref[d, own * heads :] = kv.astype(out_ref.dtype)


def attend_kernel(n, lengths_ref, parts_ref, cos_ref, sin_ref, key_ref, value_ref, out_ref, keys, values, sems):
    rows, kv_heads, slots, head_dim = key_ref.shape
    heads = out_ref.shape[1] // rows
    group = heads // kv_heads
    pairs = [(r, k) for r in range(rows) for k in range(kv_heads)]
    copies = {}
    for i, (r, k) in enumerate(pairs):
        copies["k", i] = pltpu.make_async_copy(key_ref.at[r, k], keys.at[i], sems.at[0, i])
        copies["k", i].start()
    for i, (r, k) in enumerate(pairs):
        copies["v", i] = pltpu.make_async_copy(value_ref.at[r, k], values.at[i], sems.at[1, i])
        copies["v", i].start()

    total = parts_ref[0].astype(jnp.float32)
    for d in range(1, n):
        total = total + parts_ref[d].astype(jnp.float32)
    cosine = cos_ref[...]
    sine = sin_ref[...]

    def rotated(vectors, count):
        per_row = (rows, count, head_dim)
        c = jnp.broadcast_to(cosine[:, None, :], per_row).reshape(rows * count, head_dim)
        s = jnp.broadcast_to(sine[:, None, :], per_row).reshape(rows * count, head_dim)
        return (vectors * c + pltpu.roll(vectors, head_dim // 2, 1) * s).astype(jnp.bfloat16)

    q_count = rows * heads
    kv_count = rows * kv_heads
    queries = rotated(total[:q_count], heads)
    new_keys = rotated(total[q_count : q_count + kv_count], kv_heads).astype(jnp.float32)
    new_values = total[q_count + kv_count :].astype(jnp.bfloat16).astype(jnp.float32)
    scaling = head_dim ** (-0.5)
    slot = lax.broadcasted_iota(jnp.int32, (group, slots), 1)
    scores = []
    own_scores = []
    for i, (r, k) in enumerate(pairs):
        q = queries[i * group : (i + 1) * group]
        copies["k", i].wait()
        score = lax.dot_general(
            q, keys[i], (((1,), (1,)), ((), ())), preferred_element_type=jnp.float32
        )
        scores.append(jnp.where(slot < lengths_ref[r], score * scaling, jnp.float32(-1e30)))
        own_scores.append(
            jnp.sum(q.astype(jnp.float32) * new_keys[i : i + 1], axis=1, keepdims=True) * scaling
        )
    highest = [
        jnp.maximum(jnp.max(score, axis=1, keepdims=True), own)
        for score, own in zip(scores, own_scores)
    ]
    weights = [jnp.exp(score - high) for score, high in zip(scores, highest)]
    own_weights = [jnp.exp(own - high) for own, high in zip(own_scores, highest)]
    norms = [
        jnp.sum(weight, axis=1, keepdims=True) + own for weight, own in zip(weights, own_weights)
    ]
    mixed = []
    for i in range(len(pairs)):
        copies["v", i].wait()
        head = jnp.dot(weights[i].astype(jnp.bfloat16), values[i], preferred_element_type=jnp.float32)
        mixed.append((head + own_weights[i] * new_values[i : i + 1]) / norms[i])
    block = jnp.concatenate(mixed, axis=0).astype(jnp.bfloat16)
    for d in range(n):
        out_ref[d] = block


def output_kernel(n, gy, me_ref, heads_ref, w_ref, own_ref, other_ref, w_buf, wide, lhs, sems):
    chunks, _, width = w_buf.shape
    copies = []
    for c in range(chunks):
        copy = pltpu.make_async_copy(
            w_ref.at[:, c * width : (c + 1) * width], w_buf.at[c], sems.at[c]
        )
        copy.start()
        copies.append(copy)
    own = n // gy
    per_dev, head_dim = heads_ref.shape[1:]
    heads = w_ref.shape[0] // head_dim
    rows = n * per_dev // heads
    for j in range(gy):
        first = lax.rem(me_ref[0] + j, gy) * own
        for d in range(own):
            at = (j * own + d) * per_dev
            wide[at : at + per_dev, :] = heads_ref[first + d].astype(jnp.float32)
    for h in range(heads):
        lhs[:, h * head_dim : (h + 1) * head_dim] = wide[pl.ds(h, rows, stride=heads), :].astype(lhs.dtype)
    for c in range(chunks):
        copies[c].wait()
        part = jnp.dot(lhs[...], w_buf[c], preferred_element_type=jnp.float32)
        own_ref[:, c * width : (c + 1) * width] = part[: rows // gy]
        for j in range(1, gy):
            other_ref[j - 1, :, c * width : (c + 1) * width] = part[j * (rows // gy) : (j + 1) * (rows // gy)]


def in_hbm(x):
    return pltpu.with_memory_space_constraint(x, pltpu.HBM)


def on_device(n, gy, tokens, w_query, w_key, w_value, w_out, key_cache, value_cache, lengths):
    own_rows, kv_heads, slots, head_dim = key_cache.shape
    rows, depth = tokens.shape
    q_cols = w_query.shape[1]
    kv_cols = w_key.shape[1]
    heads = q_cols // head_dim
    out_cols = w_out.shape[1]
    vmem = pl.BlockSpec(memory_space=pltpu.VMEM)
    smem = pl.BlockSpec(memory_space=pltpu.SMEM)
    anywhere = pl.BlockSpec(memory_space=pl.ANY)
    width = min(512, q_cols)
    chunks = q_cols // width
    block = own_rows * (heads + 2 * kv_heads)

    parts = pl.pallas_call(
        functools.partial(project_kernel, n, head_dim),
        out_shape=jax.ShapeDtypeStruct((n, block, head_dim), jnp.bfloat16),
        in_specs=[anywhere, anywhere, anywhere, anywhere],
        out_specs=vmem,
        scratch_shapes=[
            pltpu.VMEM((rows, depth), jnp.bfloat16),
            pltpu.VMEM((chunks, depth, width), jnp.bfloat16),
            pltpu.VMEM((depth, kv_cols), jnp.bfloat16),
            pltpu.VMEM((depth, kv_cols), jnp.bfloat16),
            pltpu.VMEM((rows * heads, head_dim), jnp.float32),
            pltpu.VMEM((rows * kv_heads, head_dim), jnp.float32),
            pltpu.VMEM((rows * kv_heads, head_dim), jnp.float32),
            pltpu.SemaphoreType.DMA((3 + chunks,)),
        ],
        compiler_params=pltpu.CompilerParams(vmem_limit_bytes=26 * MIB),
        cost_estimate=pl.CostEstimate(
            flops=2 * rows * depth * (q_cols + 2 * kv_cols),
            bytes_accessed=2 * depth * (q_cols + 2 * kv_cols),
            transcendentals=0,
        ),
        name="project",
    )(in_hbm(tokens), in_hbm(w_query), in_hbm(w_key), in_hbm(w_value))

    parts = lax.all_to_all(parts, "gx", 0, 0, tiled=True)

    half = head_dim // 2
    freqs = rope_base ** (-2.0 * jnp.arange(half).astype(jnp.float32) / (2.0 * half))
    angles = lengths.astype(jnp.float32)[:, None] * freqs[None, :]
    cosine = jnp.cos(angles)
    sine = jnp.sin(angles)
    cosine = jnp.concatenate([cosine, cosine], axis=1)
    sine = jnp.concatenate([-sine, sine], axis=1)

    mixed = pl.pallas_call(
        functools.partial(attend_kernel, n),
        out_shape=jax.ShapeDtypeStruct((n, own_rows * heads, head_dim), jnp.bfloat16),
        in_specs=[smem, vmem, vmem, vmem, anywhere, anywhere],
        out_specs=vmem,
        scratch_shapes=[
            pltpu.VMEM((own_rows * kv_heads, slots, head_dim), jnp.bfloat16),
            pltpu.VMEM((own_rows * kv_heads, slots, head_dim), jnp.bfloat16),
            pltpu.SemaphoreType.DMA((2, own_rows * kv_heads)),
        ],
        compiler_params=pltpu.CompilerParams(vmem_limit_bytes=16 * MIB),
        cost_estimate=pl.CostEstimate(
            flops=4 * own_rows * heads * slots * head_dim,
            bytes_accessed=4 * own_rows * kv_heads * slots * head_dim,
            transcendentals=own_rows * heads * slots,
        ),
        name="attend",
    )(
        lengths,
        parts,
        cosine,
        sine,
        in_hbm(key_cache),
        in_hbm(value_cache),
    )

    mixed = lax.all_to_all(mixed, "gx", 0, 0, tiled=True)

    me = lax.axis_index("gy").astype(jnp.int32).reshape(1)
    out_width = min(256, out_cols)
    out_chunks = out_cols // out_width
    own, other = pl.pallas_call(
        functools.partial(output_kernel, n, gy),
        out_shape=(
            jax.ShapeDtypeStruct((rows // gy, out_cols), jnp.float32),
            jax.ShapeDtypeStruct((gy - 1, rows // gy, out_cols), jnp.float32),
        ),
        in_specs=[smem, vmem, anywhere],
        out_specs=(vmem, vmem),
        scratch_shapes=[
            pltpu.VMEM((out_chunks, q_cols, out_width), jnp.bfloat16),
            pltpu.VMEM((rows * heads, head_dim), jnp.float32),
            pltpu.VMEM((rows, q_cols), jnp.bfloat16),
            pltpu.SemaphoreType.DMA((out_chunks,)),
        ],
        compiler_params=pltpu.CompilerParams(vmem_limit_bytes=26 * MIB),
        cost_estimate=pl.CostEstimate(
            flops=2 * rows * q_cols * out_cols,
            bytes_accessed=2 * q_cols * out_cols,
            transcendentals=0,
        ),
        name="output",
    )(me, mixed, in_hbm(w_out))

    total = own
    for j in range(1, gy):
        total = total + lax.ppermute(other[j - 1], "gy", [(i, (i + j) % gy) for i in range(gy)])
    return total.astype(jnp.bfloat16)


def solution(mesh):
    in_specs = (
        P("groups", "gx"),
        P("gx", "gy"),
        P("gx", "gy"),
        P("gx", "gy"),
        P("gy", "gx"),
        P(("groups", "gx"), "gy", None, None),
        P(("groups", "gx"), "gy", None, None),
        P(("groups", "gx")),
    )
    out_specs = P(("groups", "gy"), "gx")
    body = functools.partial(on_device, mesh.shape["gx"], mesh.shape["gy"])
    return jax.shard_map(body, mesh=mesh, in_specs=in_specs, out_specs=out_specs, check_vma=False)
```

time: 155 us -> 51.6 us (0.33)
  waiting for transfers between devices: 81.1 us -> 19.3 us
  blocking collectives: 30.9 us -> 0 us
  matrix products: 22.8 us -> 0 us
  Pallas kernels: 0 us -> 20.2 us
  between operations: 14.1 us -> 0.05 us
  starting transfers between devices: 0.08 us -> 11 us
  other arithmetic: 3.67 us -> 0.84 us
  local copies, waits for them, and re-layouts: 2.35 us -> 0.01 us
    unnamed x3 -> x0, waiting for transfers between devices: 74.5 us -> none
    all_gather x1 -> x0, blocking collectives: 30.9 us -> none  [on_device(): lax.all_gather(heads, 'gx', axis=0, tiled=True)]
    dot_general x7 -> x0, matrix products: 22.8 us -> none  [the longest x1 9.76 us: on_device(): jnp.dot(take_rows(), w_query, preferred_element_type=jnp.float32)]
    pallas_call x0 -> x3, Pallas kernels: none -> 20.2 us  [the longest x1 7.97 us: on_device(): pl.pallas_call(functools.partial(project_kernel, n, head_dim), out_shape=...]
    all_to_all x0 -> x2, waiting for transfers between devices: none -> 17.9 us  [the longest x1 9.4 us: on_device(): parts = lax.all_to_all(parts, 'gx', 0, 0, tiled=True)]
    all_to_all x0 -> x2, starting transfers between devices: none -> 10.9 us  [the longest x1 7.29 us: on_device(): parts = lax.all_to_all(parts, 'gx', 0, 0, tiled=True)]
    reduce_scatter x1 -> x0, waiting for transfers between devices: 6.65 us -> none  [on_device(): lax.psum_scatter(terms, 'gy', scatter_dimension=0, tiled=True)]
    convert_element_type x4 -> x2, other arithmetic: 2.34 us -> 0.65 us  [the longest x1 0.64 us: on_device(): return total.astype(jnp.bfloat16)]
  transfers between devices with their start and end apart: 2 -> 3, of which waited for: 2 -> 3; matrix products, arithmetic and copies ran while one was open for 0% -> 0% of each run, Pallas kernels for 0% -> 0%
where the time goes in v1:
time: 51.6 us; the launch traced here: 51.3 us
  Pallas kernels  20.2 us (39%)
  waiting for transfers between devices  19.3 us (37%)
  starting transfers between devices  11 us (21%)
  other arithmetic  0.84 us (2%)
    all_to_all x1, waiting for transfers between devices, on_device(): parts = lax.all_to_all(parts, 'gx', 0, 0, tiled=True)  9.4 us
    all_to_all x1, waiting for transfers between devices, on_device(): mixed = lax.all_to_all(mixed, 'gx', 0, 0, tiled=True)  8.53 us
    pallas_call x1, Pallas kernels, on_device(): pl.pallas_call(functools.partial(project_kernel, n, head_dim), out_shape=...  7.97 us
    all_to_all x1, starting transfers between devices, on_device(): parts = lax.all_to_all(parts, 'gx', 0, 0, tiled=True)  7.29 us
    pallas_call x1, Pallas kernels, on_device(): pl.pallas_call(functools.partial(output_kernel, n, gy), out_shape=(jax.Sh...  6.94 us
    pallas_call x1, Pallas kernels, on_device(): pl.pallas_call(functools.partial(attend_kernel, n), out_shape=jax.ShapeDt...  5.24 us
    all_to_all x1, starting transfers between devices, on_device(): mixed = lax.all_to_all(mixed, 'gx', 0, 0, tiled=True)  3.6 us
    ppermute x1, waiting for transfers between devices, on_device(): lax.ppermute(other[j - 1], 'gy', [(i, (i + j) % gy) for i in range(gy)])  1.33 us
  transfers between devices with their start and end apart: 3, of which 3 were waited for; matrix products, arithmetic and copies ran while one was open for 0% of the time, Pallas kernels for 0%

profile of v1, /device:TPU:0, one launch (start us, length us, event | category | flops | bytes accessed | tf_op | source)
XLA Modules:
  0.0 51.3 jit_solution(1657219760273070409)
XLA Ops:
  0.0 0.0 copy-start
  0.0 8.0 %project.1 = bf16[8,144,128]{2,1,0:T(8,128)(2,1)} custom-call(bf16[32,2048]{1,0:T(8,128)(2,1)} %tokens_ref.1, bf16[2048,4096]{1,0:T(8,128)(2,1)} %wq_ref.1, bf16[2048,256]{1,0:T(8,128)(2,1)} %wk_ref.1, bf16[2048,256]{1,0:T(8,128)(2,1)} %wv_ref.1), custom_call_target="tpu_custom_call" | custom-call | flops 603979776 | bytes 18874368 | tf_op jit(solution)/shard_map/project/pallas_call | solution.py:185
  8.0 7.3 %all-to-all-start = ((bf16[8,144,128]{2,1,0:T(8,128)(2,1)}), bf16[8,144,128]{2,1,0:T(8,128)(2,1)S(1)}, u32[]{:S(2)}, u32[]{:S(2)}) async-start(bf16[8,144,128]{2,1,0:T(8,128)(2,1)} %project.1), calls=%async_computation | async-start | bytes 589824 | tf_op jit(solution)/shard_map/all_to_all | solution.py:209
  15.3 0.0 copy-done
  15.3 0.1 fusion
  15.4 0.1 pad_maximum_fusion
  15.5 9.4 %all-to-all-done.parts_ref = bf16[8,144,128]{2,1,0:T(8,128)(2,1)S(1)} async-done(((bf16[8,144,128]{2,1,0:T(8,128)(2,1)}), bf16[8,144,128]{2,1,0:T(8,128)(2,1)S(1)}, u32[]{:S(2)}, u32[]{:S(2)}) %all-to-all-start) | async-done | bytes 294944 | tf_op jit(solution)/shard_map/all_to_all | solution.py:209
  24.9 5.2 %attend.1 = bf16[8,128,128]{2,1,0:T(8,128)(2,1)} custom-call(s32[4]{0:T(128)S(1)} %copy-done, bf16[8,144,128]{2,1,0:T(8,128)(2,1)S(1)} %all-to-all-done.parts_ref, f32[4,128]{1,0:T(4,128)S(1)} %get-tuple-element.12.cos_ref, f32[4,128]{1,0:T(4,128)S(1)} %get-tuple-element.13.sin_ref, bf16[4,2,1024,128]{3,2,1,0:T(8,128)(2,1)} %key_ref.1, ...), custom_call_target="tpu_custom_call" | custom-call | flops 67108864 | bytes 4194304 | tf_op jit(solution)/shard_map/attend/pallas_call | solution.py:219
  30.1 3.6 %all-to-all-start.1 = ((bf16[8,128,128]{2,1,0:T(8,128)(2,1)}), bf16[8,128,128]{2,1,0:T(8,128)(2,1)S(1)}, u32[]{:S(2)}, u32[]{:S(2)}) async-start(bf16[8,128,128]{2,1,0:T(8,128)(2,1)} %attend.1), calls=%async_computation.1 | async-start | bytes 524288 | tf_op jit(solution)/shard_map/all_to_all | solution.py:245
  33.8 8.5 %all-to-all-done.1.heads_ref = bf16[8,128,128]{2,1,0:T(8,128)(2,1)S(1)} async-done(((bf16[8,128,128]{2,1,0:T(8,128)(2,1)}), bf16[8,128,128]{2,1,0:T(8,128)(2,1)S(1)}, u32[]{:S(2)}, u32[]{:S(2)}) %all-to-all-start.1) | async-done | bytes 262176 | tf_op jit(solution)/shard_map/all_to_all | solution.py:245
  42.3 6.9 %output.1 = (f32[16,2048]{1,0:T(8,128)S(1)}, f32[1,16,2048]{2,1,0:T(8,128)S(1)}) custom-call(s32[1]{0:T(128)} %bitcast.me_ref, bf16[8,128,128]{2,1,0:T(8,128)(2,1)S(1)} %all-to-all-done.1.heads_ref, bf16[4096,2048]{1,0:T(8,128)(2,1)} %w_ref.1), custom_call_target="tpu_custom_call" | custom-call | flops 536870912 | bytes 16777216 | tf_op jit(solution)/shard_map/output/pallas_call | solution.py:250
  49.2 0.1 collective-permute-start
  49.3 1.3 %collective-permute-done = f32[16,2048]{1,0:T(8,128)S(1)} collective-permute-done((f32[16,2048]{1,0:T(8,128)S(1)}, f32[16,2048]{1,0:T(8,128)S(1)}, u32[]{:S(2)}, u32[]{:S(2)}) %collective-permute-start) | collective-permute-done | bytes 131104 | tf_op jit(solution)/shard_map/ppermute | solution.py:275
  50.6 0.6 %add_convert_fusion = bf16[16,2048]{1,0:T(8,128)(2,1)} fusion(f32[16,2048]{1,0:T(8,128)S(1)} %get-tuple-element.7, f32[16,2048]{1,0:T(8,128)S(1)} %collective-permute-done), kind=kLoop, calls=%fused_computation | loop fusion | flops 65536 | bytes 327680 | tf_op jit(solution)/shard_map/convert_element_type | solution.py:276
  (2 shorter events, 0.0 us)
Async XLA Ops:
  0.0 15.3 %copy-start = (s32[4]{0:T(128)S(1)}, s32[4]{0:T(128)}, u32[]{:S(2)}) copy-start(s32[4]{0:T(128)} %lengths_ref.1) | copy-start | bytes 52
  8.0 16.9 %all-to-all-start = ((bf16[8,144,128]{2,1,0:T(8,128)(2,1)}), bf16[8,144,128]{2,1,0:T(8,128)(2,1)S(1)}, u32[]{:S(2)}, u32[]{:S(2)}) async-start(bf16[8,144,128]{2,1,0:T(8,128)(2,1)} %project.1), calls=%async_computation | async-start | bytes 589824 | tf_op jit(solution)/shard_map/all_to_all | solution.py:209
  30.1 12.1 %all-to-all-start.1 = ((bf16[8,128,128]{2,1,0:T(8,128)(2,1)}), bf16[8,128,128]{2,1,0:T(8,128)(2,1)S(1)}, u32[]{:S(2)}, u32[]{:S(2)}) async-start(bf16[8,128,128]{2,1,0:T(8,128)(2,1)} %attend.1), calls=%async_computation.1 | async-start | bytes 524288 | tf_op jit(solution)/shard_map/all_to_all | solution.py:245
  49.2 1.4 %collective-permute-start = (f32[16,2048]{1,0:T(8,128)S(1)}, f32[16,2048]{1,0:T(8,128)S(1)}, u32[]{:S(2)}, u32[]{:S(2)}) collective-permute-start(f32[16,2048]{1,0:T(8,128)S(1)} %bitcast.2), channel_id=1, source_target_pairs={{0,1},{1,0},{2,3},{3,2},{4,5},{5,4},{6,7},{7,6},{8,9},{9,8},{10,11... | collective-permute-start | bytes 393224 | tf_op jit(solution)/shard_map/ppermute | solution.py:275

commit v2 on v1

--- a/solution.py
+++ b/solution.py
@@ -12,13 +12,14 @@
 
 
 def project_kernel(
-    n,
     head_dim,
+    me_ref,
     tokens_ref,
     wq_ref,
     wk_ref,
     wv_ref,
-    out_ref,
+    keep_ref,
+    send_ref,
     t_buf,
     q_buf,
     k_buf,
@@ -60,35 +61,53 @@
         q_copies[c].wait()
         part = jnp.dot(tokens, q_buf[c], preferred_element_type=jnp.float32)
         spread(by_head, part, c * (width // head_dim), heads)
-    own = rows // n
-    for d in range(n):
-        out_ref[d, : own * heads] = by_head[d * own * heads : (d + 1) * own * heads].astype(out_ref.dtype)
-        kv = jnp.concatenate(
-            [
-                k_rows[d * own * kv_heads : (d + 1) * own * kv_heads],
-                v_rows[d * own * kv_heads : (d + 1) * own * kv_heads],
-            ],
-            axis=0,
-        )
-        out_ref[d, own * heads :] = kv.astype(out_ref.dtype)
-
-
-def attend_kernel(n, lengths_ref, parts_ref, cos_ref, sin_ref, key_ref, value_ref, out_ref, keys, values, sems):
-    rows, kv_heads, slots, head_dim = key_ref.shape
-    heads = out_ref.shape[1] // rows
+    far, block, _ = keep_ref.shape
+    near = rows * (heads + 2 * kv_heads) // (far * block)
+    own = rows // (far * near)
+
+    def of_device(d):
+        def pick(source, count):
+            size = own * count
+            return source[pl.ds(pl.multiple_of(d * size, size), size), :]
+
+        return jnp.concatenate([pick(by_head, heads), pick(k_rows, kv_heads), pick(v_rows, kv_heads)], axis=0)
+
+    mine = lax.rem(me_ref[0], near)
+    for f in range(far):
+        keep_ref[f] = of_device(f * near + mine)
+        for j in range(1, near):
+            send_ref[j - 1, f] = of_device(f * near + lax.rem(mine + j, near)).astype(send_ref.dtype)
+
+
+def partner(f, k, far):
+    return f ^ k if far & (far - 1) == 0 else (f + k) % far
+
+
+def source(f, k, far):
+    return f ^ k if far & (far - 1) == 0 else (f + far - k) % far
+
+
+def combine_kernel(near, me_ref, cache_ref, keep_ref, *refs):
+    far = keep_ref.shape[0]
+    mine = lax.div(me_ref[0], near)
+    received, outs = refs[:-far], refs[-far:]
+    for k in range(far):
+        f = partner(mine, k, far)
+        total = keep_ref[f]
+        for part in received:
+            total = total + part[f].astype(jnp.float32)
+        outs[k][...] = total.astype(outs[k].dtype)
+
+
+def attend_kernel(lengths_ref, cos_ref, sin_ref, keys, values, *refs):
+    parts, out_ref = refs[:-1], refs[-1]
+    rows, kv_heads, slots, head_dim = keys.shape
+    heads = out_ref.shape[0] // rows
     group = heads // kv_heads
     pairs = [(r, k) for r in range(rows) for k in range(kv_heads)]
-    copies = {}
-    for i, (r, k) in enumerate(pairs):
-        copies["k", i] = pltpu.make_async_copy(key_ref.at[r, k], keys.at[i], sems.at[0, i])
-        copies["k", i].start()
-    for i, (r, k) in enumerate(pairs):
-        copies["v", i] = pltpu.make_async_copy(value_ref.at[r, k], values.at[i], sems.at[1, i])
-        copies["v", i].start()
-
-    total = parts_ref[0].astype(jnp.float32)
-    for d in range(1, n):
-        total = total + parts_ref[d].astype(jnp.float32)
+    total = parts[0][...].astype(jnp.float32)
+    for part in parts[1:]:
+        total = total + part[...].astype(jnp.float32)
     cosine = cos_ref[...]
     sine = sin_ref[...]
 
@@ -109,9 +128,8 @@
     own_scores = []
     for i, (r, k) in enumerate(pairs):
         q = queries[i * group : (i + 1) * group]
-        copies["k", i].wait()
         score = lax.dot_general(
-            q, keys[i], (((1,), (1,)), ((), ())), preferred_element_type=jnp.float32
+            q, keys[r, k], (((1,), (1,)), ((), ())), preferred_element_type=jnp.float32
         )
         scores.append(jnp.where(slot < lengths_ref[r], score * scaling, jnp.float32(-1e30)))
         own_scores.append(
@@ -127,38 +145,33 @@
         jnp.sum(weight, axis=1, keepdims=True) + own for weight, own in zip(weights, own_weights)
     ]
     mixed = []
-    for i in range(len(pairs)):
-        copies["v", i].wait()
-        head = jnp.dot(weights[i].astype(jnp.bfloat16), values[i], preferred_element_type=jnp.float32)
+    for i, (r, k) in enumerate(pairs):
+        head = jnp.dot(weights[i].astype(jnp.bfloat16), values[r, k], preferred_element_type=jnp.float32)
         mixed.append((head + own_weights[i] * new_values[i : i + 1]) / norms[i])
-    block = jnp.concatenate(mixed, axis=0).astype(jnp.bfloat16)
-    for d in range(n):
-        out_ref[d] = block
-
-
-def output_kernel(n, gy, me_ref, heads_ref, w_ref, own_ref, other_ref, w_buf, wide, lhs, sems):
-    chunks, _, width = w_buf.shape
-    copies = []
-    for c in range(chunks):
-        copy = pltpu.make_async_copy(
-            w_ref.at[:, c * width : (c + 1) * width], w_buf.at[c], sems.at[c]
-        )
-        copy.start()
-        copies.append(copy)
-    own = n // gy
-    per_dev, head_dim = heads_ref.shape[1:]
+    out_ref[...] = jnp.concatenate(mixed, axis=0).astype(jnp.bfloat16)
+
+
+def output_kernel(n, gy, far, me_ref, w_ref, *refs):
+    blocks = refs[:far]
+    own_ref, other_ref, wide, lhs = refs[far:]
+    near, per_dev, head_dim = blocks[0].shape
     heads = w_ref.shape[0] // head_dim
     rows = n * per_dev // heads
-    for j in range(gy):
-        first = lax.rem(me_ref[0] + j, gy) * own
-        for d in range(own):
-            at = (j * own + d) * per_dev
-            wide[at : at + per_dev, :] = heads_ref[first + d].astype(jnp.float32)
+    out_cols = w_ref.shape[1]
+    width = min(512, out_cols)
+    half = n // gy
+    mine = lax.rem(me_ref[0], near)
+    for k in range(far):
+        for j in range(near):
+            d = source(lax.div(me_ref[0], near), k, far) * near + lax.rem(mine + near - j, near)
+            place = lax.rem(lax.div(d, half) + gy - me_ref[1], gy) * half + lax.rem(d, half)
+            wide[pl.ds(pl.multiple_of(place * per_dev, per_dev), per_dev), :] = blocks[k][j].astype(jnp.float32)
     for h in range(heads):
         lhs[:, h * head_dim : (h + 1) * head_dim] = wide[pl.ds(h, rows, stride=heads), :].astype(lhs.dtype)
-    for c in range(chunks):
-        copies[c].wait()
-        part = jnp.dot(lhs[...], w_buf[c], preferred_element_type=jnp.float32)
+    for c in range(out_cols // width):
+        part = jnp.dot(
+            lhs[...], w_ref[:, c * width : (c + 1) * width], preferred_element_type=jnp.float32
+        )
         own_ref[:, c * width : (c + 1) * width] = part[: rows // gy]
         for j in range(1, gy):
             other_ref[j - 1, :, c * width : (c + 1) * width] = part[j * (rows // gy) : (j + 1) * (rows // gy)]
@@ -166,6 +179,10 @@
 
 def in_hbm(x):
     return pltpu.with_memory_space_constraint(x, pltpu.HBM)
+
+
+def in_vmem(x):
+    return pltpu.with_memory_space_constraint(x, pltpu.VMEM)
 
 
 def on_device(n, gy, tokens, w_query, w_key, w_value, w_out, key_cache, value_cache, lengths):
@@ -182,11 +199,28 @@
     chunks = q_cols // width
     block = own_rows * (heads + 2 * kv_heads)
 
-    parts = pl.pallas_call(
-        functools.partial(project_kernel, n, head_dim),
-        out_shape=jax.ShapeDtypeStruct((n, block, head_dim), jnp.bfloat16),
-        in_specs=[anywhere, anywhere, anywhere, anywhere],
-        out_specs=vmem,
+    near = 2 if n % 2 == 0 else 1
+    far = n // near
+    def to_near(x, j):
+        return lax.ppermute(
+            x, "gx", [(f * near + i, f * near + (i + j) % near) for f in range(far) for i in range(near)]
+        )
+
+    def to_far(x, k):
+        return lax.ppermute(
+            x, "gx", [(f * near + i, int(partner(f, k, far)) * near + i) for f in range(far) for i in range(near)]
+        )
+
+    me = jnp.stack([lax.axis_index("gx"), lax.axis_index("gy")]).astype(jnp.int32)
+
+    keep, send = pl.pallas_call(
+        functools.partial(project_kernel, head_dim),
+        out_shape=(
+            jax.ShapeDtypeStruct((far, block, head_dim), jnp.float32),
+            jax.ShapeDtypeStruct((near - 1, far, block, head_dim), jnp.bfloat16),
+        ),
+        in_specs=[smem, anywhere, anywhere, anywhere, anywhere],
+        out_specs=(vmem, vmem),
         scratch_shapes=[
             pltpu.VMEM((rows, depth), jnp.bfloat16),
             pltpu.VMEM((chunks, depth, width), jnp.bfloat16),
@@ -204,9 +238,24 @@
             transcendentals=0,
         ),
         name="project",
-    )(in_hbm(tokens), in_hbm(w_query), in_hbm(w_key), in_hbm(w_value))
-
-    parts = lax.all_to_all(parts, "gx", 0, 0, tiled=True)
+    )(me, in_hbm(tokens), in_hbm(w_query), in_hbm(w_key), in_hbm(w_value))
+
+    received = [to_near(send[j - 1], j) for j in range(1, near)]
+
+    summed = pl.pallas_call(
+        functools.partial(combine_kernel, near),
+        out_shape=[
+            jax.ShapeDtypeStruct((block, head_dim), jnp.float32 if k == 0 else jnp.bfloat16)
+            for k in range(far)
+        ],
+        in_specs=[smem] + [vmem] * (2 + len(received)),
+        out_specs=[vmem] * far,
+        compiler_params=pltpu.CompilerParams(vmem_limit_bytes=12 * MIB),
+        cost_estimate=pl.CostEstimate(flops=0, bytes_accessed=16 * MIB, transcendentals=0),
+        name="combine",
+    )(me, in_vmem(value_cache), keep, *received)
+
+    parts = [summed[0]] + [to_far(summed[k], k) for k in range(1, far)]
 
     half = head_dim // 2
     freqs = rope_base ** (-2.0 * jnp.arange(half).astype(jnp.float32) / (2.0 * half))
@@ -217,58 +266,42 @@
     sine = jnp.concatenate([-sine, sine], axis=1)
 
     mixed = pl.pallas_call(
-        functools.partial(attend_kernel, n),
-        out_shape=jax.ShapeDtypeStruct((n, own_rows * heads, head_dim), jnp.bfloat16),
-        in_specs=[smem, vmem, vmem, vmem, anywhere, anywhere],
+        attend_kernel,
+        out_shape=jax.ShapeDtypeStruct((own_rows * heads, head_dim), jnp.bfloat16),
+        in_specs=[smem] + [vmem] * (4 + far),
         out_specs=vmem,
-        scratch_shapes=[
-            pltpu.VMEM((own_rows * kv_heads, slots, head_dim), jnp.bfloat16),
-            pltpu.VMEM((own_rows * kv_heads, slots, head_dim), jnp.bfloat16),
-            pltpu.SemaphoreType.DMA((2, own_rows * kv_heads)),
-        ],
-        compiler_params=pltpu.CompilerParams(vmem_limit_bytes=16 * MIB),
+        compiler_params=pltpu.CompilerParams(vmem_limit_bytes=12 * MIB),
         cost_estimate=pl.CostEstimate(
             flops=4 * own_rows * heads * slots * head_dim,
             bytes_accessed=4 * own_rows * kv_heads * slots * head_dim,
             transcendentals=own_rows * heads * slots,
         ),
         name="attend",
-    )(
-        lengths,
-        parts,
-        cosine,
-        sine,
-        in_hbm(key_cache),
-        in_hbm(value_cache),
-    )
-
-    mixed = lax.all_to_all(mixed, "gx", 0, 0, tiled=True)
-
-    me = lax.axis_index("gy").astype(jnp.int32).reshape(1)
-    out_width = min(256, out_cols)
-    out_chunks = out_cols // out_width
+    )(lengths, cosine, sine, in_vmem(key_cache), in_vmem(value_cache), *parts)
+
+    pair = jnp.stack([mixed] + [to_near(mixed, j) for j in range(1, near)])
+    blocks = [pair] + [to_far(pair, k) for k in range(1, far)]
+
     own, other = pl.pallas_call(
-        functools.partial(output_kernel, n, gy),
+        functools.partial(output_kernel, n, gy, far),
         out_shape=(
             jax.ShapeDtypeStruct((rows // gy, out_cols), jnp.float32),
             jax.ShapeDtypeStruct((gy - 1, rows // gy, out_cols), jnp.float32),
         ),
-        in_specs=[smem, vmem, anywhere],
+        in_specs=[smem] + [vmem] * (1 + far),
         out_specs=(vmem, vmem),
         scratch_shapes=[
-            pltpu.VMEM((out_chunks, q_cols, out_width), jnp.bfloat16),
             pltpu.VMEM((rows * heads, head_dim), jnp.float32),
             pltpu.VMEM((rows, q_cols), jnp.bfloat16),
-            pltpu.SemaphoreType.DMA((out_chunks,)),
         ],
-        compiler_params=pltpu.CompilerParams(vmem_limit_bytes=26 * MIB),
+        compiler_params=pltpu.CompilerParams(vmem_limit_bytes=12 * MIB),
         cost_estimate=pl.CostEstimate(
             flops=2 * rows * q_cols * out_cols,
             bytes_accessed=2 * q_cols * out_cols,
             transcendentals=0,
         ),
         name="output",
-    )(me, mixed, in_hbm(w_out))
+    )(me, in_vmem(w_out), *blocks)
 
     total = own
     for j in range(1, gy):

time: 51.6 us -> 44.5 us (0.86)
  Pallas kernels: 20.2 us -> 13.7 us
  waiting for transfers between devices: 19.3 us -> 16.1 us
  starting transfers between devices: 11 us -> 13.6 us
    all_to_all x2 -> x0, waiting for transfers between devices: 17.9 us -> none  [the longest x1 9.4 us: on_device(): parts = lax.all_to_all(parts, 'gx', 0, 0, tiled=True)]
    ppermute x0 -> x8, waiting for transfers between devices: none -> 14.7 us  [the longest x6 8.64 us: to_far(): lax.ppermute(x, 'gx', [(f * near + i, int(partner(f, k, far)) * near + i)...]
    ppermute x0 -> x8, starting transfers between devices: none -> 13.5 us  [the longest x6 8.9 us: to_far(): lax.ppermute(x, 'gx', [(f * near + i, int(partner(f, k, far)) * near + i)...]
    all_to_all x2 -> x0, starting transfers between devices: 10.9 us -> none  [the longest x1 7.29 us: on_device(): parts = lax.all_to_all(parts, 'gx', 0, 0, tiled=True)]
    pallas_call x3 -> x4, Pallas kernels: 20.2 us -> 13.7 us  [the longest x1 8.1 us: on_device(): pl.pallas_call(functools.partial(project_kernel, head_dim), out_shape=(ja...]
  transfers between devices with their start and end apart: 3 -> 9, of which waited for: 3 -> 7; matrix products, arithmetic and copies ran while one was open for 0% -> 0% of each run, Pallas kernels for 0% -> 0%
where the time goes in v2:
time: 44.5 us; the launch traced here: 44.4 us
  waiting for transfers between devices  16.1 us (36%)
  Pallas kernels  13.7 us (31%)
  starting transfers between devices  13.6 us (31%)
  other arithmetic  0.92 us (2%)
    ppermute x6, starting transfers between devices, to_far(): lax.ppermute(x, 'gx', [(f * near + i, int(partner(f, k, far)) * near + i)...  8.9 us
    ppermute x6, waiting for transfers between devices, to_far(): lax.ppermute(x, 'gx', [(f * near + i, int(partner(f, k, far)) * near + i)...  8.64 us
    pallas_call x1, Pallas kernels, on_device(): pl.pallas_call(functools.partial(project_kernel, head_dim), out_shape=(ja...  8.1 us
    ppermute x2, waiting for transfers between devices, to_near(): lax.ppermute(x, 'gx', [(f * near + i, f * near + (i + j) % near) for f in...  6.11 us
    ppermute x2, starting transfers between devices, to_near(): lax.ppermute(x, 'gx', [(f * near + i, f * near + (i + j) % near) for f in...  4.64 us
    pallas_call x1, Pallas kernels, on_device(): pl.pallas_call(functools.partial(output_kernel, n, gy, far), out_shape=(j...  3.53 us
    pallas_call x1, Pallas kernels, on_device(): pl.pallas_call(attend_kernel, out_shape=jax.ShapeDtypeStruct((own_rows *...  1.51 us
    ppermute x1, waiting for transfers between devices, on_device(): lax.ppermute(other[j - 1], 'gy', [(i, (i + j) % gy) for i in range(gy)])  1.33 us
  transfers between devices with their start and end apart: 9, of which 7 were waited for; matrix products, arithmetic and copies ran while one was open for 0% of the time, Pallas kernels for 0%

profile of v2, /device:TPU:0, one launch (start us, length us, event | category | flops | bytes accessed | tf_op | source)
XLA Modules:
  0.0 44.4 jit_solution(9345685881958523356)
XLA Ops:
  0.0 0.0 copy-start.3
  0.0 0.0 copy-start.1
  0.0 0.1 pad_add_fusion.me_ref
  0.1 8.1 %project.1 = (f32[4,144,128]{2,1,0:T(8,128)S(1)}, bf16[1,4,144,128]{3,2,1,0:T(8,128)(2,1)S(1)}) custom-call(s32[2]{0:T(128)S(1)} %pad_add_fusion.me_ref, bf16[32,2048]{1,0:T(8,128)(2,1)} %tokens_ref.1, bf16[2048,4096]{1,0:T(8,128)(2,1)} %wq_ref.1, bf16[2048,256]{1,0:T(8,128)(2,1)} %wk_ref.1, bf16[2048,256]{1,0:T(8,128)(2,1)} %wv_ref.1), custom_call_target="tpu_custom_call" | custom-call | flops 603979776 | bytes 18874368 | tf_op jit(solution)/shard_map/project/pallas_call | solution.py:216
  8.2 3.0 %collective-permute-start = (bf16[4,144,128]{2,1,0:T(8,128)(2,1)S(1)}, bf16[4,144,128]{2,1,0:T(8,128)(2,1)S(1)}, u32[]{:S(2)}, u32[]{:S(2)}) collective-permute-start(bf16[4,144,128]{2,1,0:T(8,128)(2,1)S(1)} %bitcast.7), channel_id=1, source_target_pairs={{0,2},{2,0},{4,6},{6,4},{8,10},{10,8},{12,14},{14,12},{1,3},{3,1},... | collective-permute-start | bytes 442376 | tf_op jit(solution)/shard_map/ppermute | solution.py:205
  11.2 0.0 copy-done.3
  11.3 0.1 fusion
  11.4 3.7 %collective-permute-done.refs_0_ = bf16[4,144,128]{2,1,0:T(8,128)(2,1)S(1)} collective-permute-done((bf16[4,144,128]{2,1,0:T(8,128)(2,1)S(1)}, bf16[4,144,128]{2,1,0:T(8,128)(2,1)S(1)}, u32[]{:S(2)}, u32[]{:S(2)}) %collective-permute-start) | collective-permute-done | bytes 147488 | tf_op jit(solution)/shard_map/ppermute | solution.py:205
  15.1 0.0 copy-done.1
  15.1 0.6 %combine.1 = (f32[144,128]{1,0:T(8,128)S(1)}, bf16[144,128]{1,0:T(8,128)(2,1)S(1)}, bf16[144,128]{1,0:T(8,128)(2,1)S(1)}, bf16[144,128]{1,0:T(8,128)(2,1)S(1)}) custom-call(s32[2]{0:T(128)S(1)} %pad_add_fusion.me_ref, bf16[4,2,1024,128]{3,2,1,0:T(8,128)(2,1)S(1)} %copy-done.1, f32[4,144,128]{2,1,0:T(8,128)S(1)} %get-tuple-element.13.keep_ref, ...), custom_call_target="tpu_custom_call" | custom-call | bytes 16777216 | tf_op jit(solution)/shard_map/combine/pallas_call | solution.py:245
  15.7 1.9 %collective-permute-start.1 = (bf16[144,128]{1,0:T(8,128)(2,1)S(1)}, bf16[144,128]{1,0:T(8,128)(2,1)S(1)}, u32[]{:S(2)}, u32[]{:S(2)}) collective-permute-start(bf16[144,128]{1,0:T(8,128)(2,1)S(1)} %get-tuple-element.16), channel_id=1, source_target_pairs={{0,4},{2,6},{4,0},{6,2},{8,12},{10,14},{12,8},{14,10},{1,5},{3,7},... | collective-permute-start | bytes 110600 | tf_op jit(solution)/shard_map/ppermute | solution.py:210
  17.5 2.6 %collective-permute-start.2 = (bf16[144,128]{1,0:T(8,128)(2,1)S(1)}, bf16[144,128]{1,0:T(8,128)(2,1)S(1)}, u32[]{:S(2)}, u32[]{:S(2)}) collective-permute-start(bf16[144,128]{1,0:T(8,128)(2,1)S(1)} %get-tuple-element.17), channel_id=1, source_target_pairs={{0,8},{2,10},{4,12},{6,14},{8,0},{10,2},{12,4},{14,6},{1,9},{3,11}... | collective-permute-start | bytes 110600 | tf_op jit(solution)/shard_map/ppermute | solution.py:210
  20.1 0.0 collective-permute-start.3
  20.1 0.1 pad_maximum_fusion.1
  20.2 0.0 collective-permute-done.1.refs_1_
  20.2 2.5 %collective-permute-done.2.refs_2_ = bf16[144,128]{1,0:T(8,128)(2,1)S(1)} collective-permute-done((bf16[144,128]{1,0:T(8,128)(2,1)S(1)}, bf16[144,128]{1,0:T(8,128)(2,1)S(1)}, u32[]{:S(2)}, u32[]{:S(2)}) %collective-permute-start.2) | collective-permute-done | bytes 36896 | tf_op jit(solution)/shard_map/ppermute | solution.py:210
  22.7 3.2 %collective-permute-done.3.refs_3_ = bf16[144,128]{1,0:T(8,128)(2,1)S(1)} collective-permute-done((bf16[144,128]{1,0:T(8,128)(2,1)S(1)}, bf16[144,128]{1,0:T(8,128)(2,1)S(1)}, u32[]{:S(2)}, u32[]{:S(2)}) %collective-permute-start.3) | collective-permute-done | bytes 36896 | tf_op jit(solution)/shard_map/ppermute | solution.py:210
  25.9 0.0 copy-done.2
  25.9 1.5 %attend.1 = bf16[128,128]{1,0:T(8,128)(2,1)S(1)} custom-call(s32[4]{0:T(128)S(1)} %copy-done.3, f32[4,128]{1,0:T(4,128)S(1)} %get-tuple-element.24.cos_ref, f32[4,128]{1,0:T(4,128)S(1)} %get-tuple-element.25.sin_ref, bf16[4,2,1024,128]{3,2,1,0:T(8,128)(2,1)S(1)} %copy-done.2, bf16[4,2,1024,128]{3,2,1,0:T(8,128)(2,1)S(1)} %copy-done.1, ...), custom_call_target="tpu_custom_call" | custom-call | flops 67108864 | bytes 4194304 | tf_op jit(solution)/shard_map/attend/pallas_call | solution.py:268
  27.4 1.6 %collective-permute-start.4 = (bf16[128,128]{1,0:T(8,128)(2,1)S(1)}, bf16[128,128]{1,0:T(8,128)(2,1)S(1)}, u32[]{:S(2)}, u32[]{:S(2)}) collective-permute-start(bf16[128,128]{1,0:T(8,128)(2,1)S(1)} %attend.1), channel_id=1, source_target_pairs={{0,2},{2,0},{4,6},{6,4},{8,10},{10,8},{12,14},{14,12},{1,3},{3,1},... | collective-permute-start | bytes 98312 | tf_op jit(solution)/shard_map/ppermute | solution.py:205
  29.0 2.4 %collective-permute-done.4 = bf16[128,128]{1,0:T(8,128)(2,1)S(1)} collective-permute-done((bf16[128,128]{1,0:T(8,128)(2,1)S(1)}, bf16[128,128]{1,0:T(8,128)(2,1)S(1)}, u32[]{:S(2)}, u32[]{:S(2)}) %collective-permute-start.4) | collective-permute-done | bytes 32800 | tf_op jit(solution)/shard_map/ppermute | solution.py:205
  31.4 0.1 collective-permute-start.5
  31.5 0.9 %collective-permute-start.6 = (bf16[2,128,128]{2,1,0:T(8,128)(2,1)S(1)}, bf16[2,128,128]{2,1,0:T(8,128)(2,1)S(1)}, u32[]{:S(2)}, u32[]{:S(2)}) collective-permute-start(bf16[2,128,128]{2,1,0:T(8,128)(2,1)S(1)} %pad_maximum_fusion.refs_0_), channel_id=1, source_target_pairs={{0,8},{2,10},{4,12},{6,14},{8,0},{10,2},{12,4},{14,6},{1,9},{3,11}... | collective-permute-start | bytes 196616 | tf_op jit(solution)/shard_map/ppermute | solution.py:210
  32.4 3.4 %collective-permute-start.7 = (bf16[2,128,128]{2,1,0:T(8,128)(2,1)S(1)}, bf16[2,128,128]{2,1,0:T(8,128)(2,1)S(1)}, u32[]{:S(2)}, u32[]{:S(2)}) collective-permute-start(bf16[2,128,128]{2,1,0:T(8,128)(2,1)S(1)} %pad_maximum_fusion.refs_0_), channel_id=1, source_target_pairs={{0,12},{2,14},{4,8},{6,10},{8,4},{10,6},{12,0},{14,2},{1,13},{3,15... | collective-permute-start | bytes 196616 | tf_op jit(solution)/shard_map/ppermute | solution.py:210
  35.8 0.0 collective-permute-done.5.refs_1_
  35.9 0.9 %collective-permute-done.6.refs_2_ = bf16[2,128,128]{2,1,0:T(8,128)(2,1)S(1)} collective-permute-done((bf16[2,128,128]{2,1,0:T(8,128)(2,1)S(1)}, bf16[2,128,128]{2,1,0:T(8,128)(2,1)S(1)}, u32[]{:S(2)}, u32[]{:S(2)}) %collective-permute-start.6) | collective-permute-done | bytes 65568 | tf_op jit(solution)/shard_map/ppermute | solution.py:210
  36.7 2.1 %collective-permute-done.7.refs_3_ = bf16[2,128,128]{2,1,0:T(8,128)(2,1)S(1)} collective-permute-done((bf16[2,128,128]{2,1,0:T(8,128)(2,1)S(1)}, bf16[2,128,128]{2,1,0:T(8,128)(2,1)S(1)}, u32[]{:S(2)}, u32[]{:S(2)}) %collective-permute-start.7) | collective-permute-done | bytes 65568 | tf_op jit(solution)/shard_map/ppermute | solution.py:210
  38.8 0.0 copy-done
  38.8 3.5 %output.1 = (f32[16,2048]{1,0:T(8,128)S(1)}, f32[1,16,2048]{2,1,0:T(8,128)S(1)}) custom-call(s32[2]{0:T(128)S(1)} %pad_add_fusion.me_ref, bf16[4096,2048]{1,0:T(8,128)(2,1)S(1)} %copy-done, bf16[2,128,128]{2,1,0:T(8,128)(2,1)S(1)} %pad_maximum_fusion.refs_0_, bf16[2,128,128]{2,1,0:T(8,128)(2,1)S(1)} %collective-permute-done.5.refs_1_, ...), custom_call_target="tpu_custom_call" | custom-call | flops 536870912 | bytes 16777216 | tf_op jit(solution)/shard_map/output/pallas_call | solution.py:285
  42.3 0.1 collective-permute-start.8
  42.4 1.3 %collective-permute-done.8 = f32[16,2048]{1,0:T(8,128)S(1)} collective-permute-done((f32[16,2048]{1,0:T(8,128)S(1)}, f32[16,2048]{1,0:T(8,128)S(1)}, u32[]{:S(2)}, u32[]{:S(2)}) %collective-permute-start.8) | collective-permute-done | bytes 131104 | tf_op jit(solution)/shard_map/ppermute | solution.py:308
  43.8 0.6 %add_convert_fusion = bf16[16,2048]{1,0:T(8,128)(2,1)} fusion(f32[16,2048]{1,0:T(8,128)S(1)} %get-tuple-element.19, f32[16,2048]{1,0:T(8,128)S(1)} %collective-permute-done.8), kind=kLoop, calls=%fused_computation | loop fusion | flops 65536 | bytes 327680 | tf_op jit(solution)/shard_map/convert_element_type | solution.py:309
  (5 shorter events, 0.0 us)
Async XLA Ops:
  0.0 11.2 %copy-start.3 = (s32[4]{0:T(128)S(1)}, s32[4]{0:T(128)}, u32[]{:S(2)}) copy-start(s32[4]{0:T(128)} %lengths_ref.1) | copy-start | bytes 52
  0.0 15.1 %copy-start.1 = (bf16[4,2,1024,128]{3,2,1,0:T(8,128)(2,1)S(1)}, bf16[4,2,1024,128]{3,2,1,0:T(8,128)(2,1)}, u32[]{:S(2)}) copy-start(bf16[4,2,1024,128]{3,2,1,0:T(8,128)(2,1)} %values.1) | copy-start | bytes 6291460
  0.0 25.9 %copy-start.2 = (bf16[4,2,1024,128]{3,2,1,0:T(8,128)(2,1)S(1)}, bf16[4,2,1024,128]{3,2,1,0:T(8,128)(2,1)}, u32[]{:S(2)}) copy-start(bf16[4,2,1024,128]{3,2,1,0:T(8,128)(2,1)} %keys.1) | copy-start | bytes 6291460
  0.0 38.8 %copy-start = (bf16[4096,2048]{1,0:T(8,128)(2,1)S(1)}, bf16[4096,2048]{1,0:T(8,128)(2,1)}, u32[]{:S(2)}) copy-start(bf16[4096,2048]{1,0:T(8,128)(2,1)} %w_ref.1) | copy-start | bytes 50331652
  8.2 6.9 %collective-permute-start = (bf16[4,144,128]{2,1,0:T(8,128)(2,1)S(1)}, bf16[4,144,128]{2,1,0:T(8,128)(2,1)S(1)}, u32[]{:S(2)}, u32[]{:S(2)}) collective-permute-start(bf16[4,144,128]{2,1,0:T(8,128)(2,1)S(1)} %bitcast.7), channel_id=1, source_target_pairs={{0,2},{2,0},{4,6},{6,4},{8,10},{10,8},{12,14},{14,12},{1,3},{3,1},... | collective-permute-start | bytes 442376 | tf_op jit(solution)/shard_map/ppermute | solution.py:205
  15.7 4.5 %collective-permute-start.1 = (bf16[144,128]{1,0:T(8,128)(2,1)S(1)}, bf16[144,128]{1,0:T(8,128)(2,1)S(1)}, u32[]{:S(2)}, u32[]{:S(2)}) collective-permute-start(bf16[144,128]{1,0:T(8,128)(2,1)S(1)} %get-tuple-element.16), channel_id=1, source_target_pairs={{0,4},{2,6},{4,0},{6,2},{8,12},{10,14},{12,8},{14,10},{1,5},{3,7},... | collective-permute-start | bytes 110600 | tf_op jit(solution)/shard_map/ppermute | solution.py:210
  17.5 5.2 %collective-permute-start.2 = (bf16[144,128]{1,0:T(8,128)(2,1)S(1)}, bf16[144,128]{1,0:T(8,128)(2,1)S(1)}, u32[]{:S(2)}, u32[]{:S(2)}) collective-permute-start(bf16[144,128]{1,0:T(8,128)(2,1)S(1)} %get-tuple-element.17), channel_id=1, source_target_pairs={{0,8},{2,10},{4,12},{6,14},{8,0},{10,2},{12,4},{14,6},{1,9},{3,11}... | collective-permute-start | bytes 110600 | tf_op jit(solution)/shard_map/ppermute | solution.py:210
  20.1 5.8 %collective-permute-start.3 = (bf16[144,128]{1,0:T(8,128)(2,1)S(1)}, bf16[144,128]{1,0:T(8,128)(2,1)S(1)}, u32[]{:S(2)}, u32[]{:S(2)}) collective-permute-start(bf16[144,128]{1,0:T(8,128)(2,1)S(1)} %get-tuple-element.18), channel_id=1, source_target_pairs={{0,12},{2,14},{4,8},{6,10},{8,4},{10,6},{12,0},{14,2},{1,13},{3,15... | collective-permute-start | bytes 110600 | tf_op jit(solution)/shard_map/ppermute | solution.py:210
  27.4 4.0 %collective-permute-start.4 = (bf16[128,128]{1,0:T(8,128)(2,1)S(1)}, bf16[128,128]{1,0:T(8,128)(2,1)S(1)}, u32[]{:S(2)}, u32[]{:S(2)}) collective-permute-start(bf16[128,128]{1,0:T(8,128)(2,1)S(1)} %attend.1), channel_id=1, source_target_pairs={{0,2},{2,0},{4,6},{6,4},{8,10},{10,8},{12,14},{14,12},{1,3},{3,1},... | collective-permute-start | bytes 98312 | tf_op jit(solution)/shard_map/ppermute | solution.py:205
  31.4 4.5 %collective-permute-start.5 = (bf16[2,128,128]{2,1,0:T(8,128)(2,1)S(1)}, bf16[2,128,128]{2,1,0:T(8,128)(2,1)S(1)}, u32[]{:S(2)}, u32[]{:S(2)}) collective-permute-start(bf16[2,128,128]{2,1,0:T(8,128)(2,1)S(1)} %pad_maximum_fusion.refs_0_), channel_id=1, source_target_pairs={{0,4},{2,6},{4,0},{6,2},{8,12},{10,14},{12,8},{14,10},{1,5},{3,7},... | collective-permute-start | bytes 196616 | tf_op jit(solution)/shard_map/ppermute | solution.py:210
  31.5 5.2 %collective-permute-start.6 = (bf16[2,128,128]{2,1,0:T(8,128)(2,1)S(1)}, bf16[2,128,128]{2,1,0:T(8,128)(2,1)S(1)}, u32[]{:S(2)}, u32[]{:S(2)}) collective-permute-start(bf16[2,128,128]{2,1,0:T(8,128)(2,1)S(1)} %pad_maximum_fusion.refs_0_), channel_id=1, source_target_pairs={{0,8},{2,10},{4,12},{6,14},{8,0},{10,2},{12,4},{14,6},{1,9},{3,11}... | collective-permute-start | bytes 196616 | tf_op jit(solution)/shard_map/ppermute | solution.py:210
  32.4 6.4 %collective-permute-start.7 = (bf16[2,128,128]{2,1,0:T(8,128)(2,1)S(1)}, bf16[2,128,128]{2,1,0:T(8,128)(2,1)S(1)}, u32[]{:S(2)}, u32[]{:S(2)}) collective-permute-start(bf16[2,128,128]{2,1,0:T(8,128)(2,1)S(1)} %pad_maximum_fusion.refs_0_), channel_id=1, source_target_pairs={{0,12},{2,14},{4,8},{6,10},{8,4},{10,6},{12,0},{14,2},{1,13},{3,15... | collective-permute-start | bytes 196616 | tf_op jit(solution)/shard_map/ppermute | solution.py:210
  42.3 1.4 %collective-permute-start.8 = (f32[16,2048]{1,0:T(8,128)S(1)}, f32[16,2048]{1,0:T(8,128)S(1)}, u32[]{:S(2)}, u32[]{:S(2)}) collective-permute-start(f32[16,2048]{1,0:T(8,128)S(1)} %bitcast.8), channel_id=1, source_target_pairs={{0,1},{1,0},{2,3},{3,2},{4,5},{5,4},{6,7},{7,6},{8,9},{9,8},{10,11... | collective-permute-start | bytes 393224 | tf_op jit(solution)/shard_map/ppermute | solution.py:308

commit v3 on v2

v3 whole, which is shorter than its diff:
```python
import functools

import jax
import jax.numpy as jnp
from jax import lax
from jax.experimental import pallas as pl
from jax.experimental.pallas import tpu as pltpu
from jax.sharding import PartitionSpec as P

rope_base = 500000.0
MIB = 1024 * 1024


def chunk_widths(cols, head_dim):
    unit = cols // 16
    if cols % 16 or unit % head_dim:
        return (cols,)
    return (4 * unit, 4 * unit, 4 * unit, 2 * unit, unit, unit)


def project_kernel(
    near,
    widths,
    head_dim,
    tokens_ref,
    wq_ref,
    wk_ref,
    wv_ref,
    keep_ref,
    send_ref,
    t_buf,
    q_buf,
    k_buf,
    v_buf,
    by_head,
    k_rows,
    v_rows,
    sems,
):
    rows = tokens_ref.shape[0]
    heads = q_buf.shape[1] // head_dim
    kv_heads = wk_ref.shape[1] // head_dim
    t_copy = pltpu.make_async_copy(tokens_ref, t_buf, sems.at[0])
    k_copy = pltpu.make_async_copy(wk_ref, k_buf, sems.at[1])
    v_copy = pltpu.make_async_copy(wv_ref, v_buf, sems.at[2])
    t_copy.start()
    k_copy.start()
    v_copy.start()
    q_copies = []
    first = 0
    for c, width in enumerate(widths):
        at = slice(first, first + width)
        copy = pltpu.make_async_copy(wq_ref.at[:, at], q_buf.at[:, at], sems.at[3 + c])
        copy.start()
        q_copies.append((copy, at))
        first += width

    far, block, _ = keep_ref.shape
    own = rows // (far * near)
    q_count = own * heads
    me = lax.axis_index("gx")
    mine, mine_far = lax.rem(me, near), lax.div(me, near)

    def devices():
        for f in range(far):
            other = partner(mine_far, f, far) * near
            yield keep_ref, (f,), other + mine
            for j in range(1, near):
                yield send_ref, (j - 1, f), other + lax.rem(mine + j, near)

    def spread(dest, part, first, count):
        for j in range(part.shape[1] // head_dim):
            dest[pl.ds(first + j, rows, stride=count), :] = part[:, j * head_dim : (j + 1) * head_dim]

    def put_kv():
        for ref, at, d in devices():
            size = own * kv_heads
            rows_of = pl.ds(pl.multiple_of(d * size, size), size)
            kv = jnp.concatenate([k_rows[rows_of, :], v_rows[rows_of, :]], axis=0)
            ref[*at, q_count:, :] = kv.astype(ref.dtype)

    def put_heads(first, count):
        for ref, at, d in devices():
            start = pl.multiple_of(d * q_count, q_count)
            for r in range(own):
                to = r * heads + first
                ref[*at, to : to + count, :] = by_head[pl.ds(start + to, count), :].astype(ref.dtype)

    t_copy.wait()
    tokens = t_buf[...]
    k_copy.wait()
    spread(k_rows, jnp.dot(tokens, k_buf[...], preferred_element_type=jnp.float32), 0, kv_heads)
    v_copy.wait()
    spread(v_rows, jnp.dot(tokens, v_buf[...], preferred_element_type=jnp.float32), 0, kv_heads)
    put_kv()
    step = 16 if heads % 16 == 0 else heads
    done = 0
    for copy, at in q_copies:
        copy.wait()
        part = jnp.dot(tokens, q_buf[:, at], preferred_element_type=jnp.float32)
        spread(by_head, part, at.start // head_dim, heads)
        while done + step <= at.stop // head_dim:
            put_heads(done, step)
            done += step


def partner(f, k, far):
    return f ^ k if far & (far - 1) == 0 else (f + k) % far


def source(f, k, far):
    return f ^ k if far & (far - 1) == 0 else (f + far - k) % far


def combine_kernel(cache_ref, keep_ref, *refs):
    far = keep_ref.shape[0]
    received, outs = refs[:-far], refs[-far:]
    for k in range(far):
        total = keep_ref[k]
        for part in received:
            total = total + part[k].astype(jnp.float32)
        outs[k][...] = total.astype(outs[k].dtype)


def attend_kernel(table_ref, keys, values, *refs):
    parts, out_ref = refs[:-1], refs[-1]
    rows, kv_heads, slots, head_dim = keys.shape
    heads = out_ref.shape[0] // rows
    group = heads // kv_heads
    pairs = [(r, k) for r in range(rows) for k in range(kv_heads)]
    total = parts[0][...].astype(jnp.float32)
    for part in parts[1:]:
        total = total + part[...].astype(jnp.float32)
    cosine = table_ref[:rows]
    sine = table_ref[rows : 2 * rows]
    filled = table_ref[2 * rows :]

    def rotated(vectors, count):
        per_row = (rows, count, head_dim)
        c = jnp.broadcast_to(cosine[:, None, :], per_row).reshape(rows * count, head_dim)
        s = jnp.broadcast_to(sine[:, None, :], per_row).reshape(rows * count, head_dim)
        return (vectors * c + pltpu.roll(vectors, head_dim // 2, 1) * s).astype(jnp.bfloat16)

    q_count = rows * heads
    kv_count = rows * kv_heads
    queries = rotated(total[:q_count], heads)
    new_keys = rotated(total[q_count : q_count + kv_count], kv_heads).astype(jnp.float32)
    new_values = total[q_count + kv_count :].astype(jnp.bfloat16).astype(jnp.float32)
    scaling = head_dim ** (-0.5)
    slot = lax.broadcasted_iota(jnp.int32, (group, slots), 1).astype(jnp.float32)
    scores = []
    own_scores = []
    for i, (r, k) in enumerate(pairs):
        q = queries[i * group : (i + 1) * group]
        score = lax.dot_general(
            q, keys[r, k], (((1,), (1,)), ((), ())), preferred_element_type=jnp.float32
        )
        scores.append(jnp.where(slot < filled[r : r + 1, :1], score * scaling, jnp.float32(-1e30)))
        own_scores.append(
            jnp.sum(q.astype(jnp.float32) * new_keys[i : i + 1], axis=1, keepdims=True) * scaling
        )
    highest = [
        jnp.maximum(jnp.max(score, axis=1, keepdims=True), own)
        for score, own in zip(scores, own_scores)
    ]
    weights = [jnp.exp(score - high) for score, high in zip(scores, highest)]
    own_weights = [jnp.exp(own - high) for own, high in zip(own_scores, highest)]
    norms = [
        jnp.sum(weight, axis=1, keepdims=True) + own for weight, own in zip(weights, own_weights)
    ]
    mixed = []
    for i, (r, k) in enumerate(pairs):
        head = jnp.dot(weights[i].astype(jnp.bfloat16), values[r, k], preferred_element_type=jnp.float32)
        mixed.append((head + own_weights[i] * new_values[i : i + 1]) / norms[i])
    out_ref[...] = jnp.concatenate(mixed, axis=0).astype(jnp.bfloat16)


def output_kernel(n, gy, far, w_ref, *refs):
    blocks = refs[:far]
    own_ref, other_ref, wide, lhs = refs[far:]
    near, per_dev, head_dim = blocks[0].shape
    heads = w_ref.shape[0] // head_dim
    rows = n * per_dev // heads
    out_cols = w_ref.shape[1]
    width = min(512, out_cols)
    half = n // gy
    me, me_gy = lax.axis_index("gx"), lax.axis_index("gy")
    mine, mine_far = lax.rem(me, near), lax.div(me, near)
    for k in range(far):
        for j in range(near):
            d = source(mine_far, k, far) * near + lax.rem(mine + near - j, near)
            place = lax.rem(lax.div(d, half) + gy - me_gy, gy) * half + lax.rem(d, half)
            wide[pl.ds(pl.multiple_of(place * per_dev, per_dev), per_dev), :] = blocks[k][j].astype(jnp.float32)
    for h in range(heads):
        lhs[:, h * head_dim : (h + 1) * head_dim] = wide[pl.ds(h, rows, stride=heads), :].astype(lhs.dtype)
    for c in range(out_cols // width):
        part = jnp.dot(
            lhs[...], w_ref[:, c * width : (c + 1) * width], preferred_element_type=jnp.float32
        )
        own_ref[:, c * width : (c + 1) * width] = part[: rows // gy]
        for j in range(1, gy):
            other = part[j * (rows // gy) : (j + 1) * (rows // gy)]
            other_ref[j - 1, :, c * width : (c + 1) * width] = other.astype(other_ref.dtype)


def in_hbm(x):
    return pltpu.with_memory_space_constraint(x, pltpu.HBM)


def in_vmem(x):
    return pltpu.with_memory_space_constraint(x, pltpu.VMEM)


def on_device(n, gy, tokens, w_query, w_key, w_value, w_out, key_cache, value_cache, lengths):
    own_rows, kv_heads, slots, head_dim = key_cache.shape
    rows, depth = tokens.shape
    q_cols = w_query.shape[1]
    kv_cols = w_key.shape[1]
    heads = q_cols // head_dim
    out_cols = w_out.shape[1]
    vmem = pl.BlockSpec(memory_space=pltpu.VMEM)
    anywhere = pl.BlockSpec(memory_space=pl.ANY)
    block = own_rows * (heads + 2 * kv_heads)

    near = 2 if n % 2 == 0 else 1
    far = n // near
    def to_near(x, j):
        return lax.ppermute(
            x, "gx", [(f * near + i, f * near + (i + j) % near) for f in range(far) for i in range(near)]
        )

    def to_far(x, k):
        return lax.ppermute(
            x, "gx", [(f * near + i, int(partner(f, k, far)) * near + i) for f in range(far) for i in range(near)]
        )

    widths = chunk_widths(q_cols, head_dim)
    keep, send = pl.pallas_call(
        functools.partial(project_kernel, near, widths, head_dim),
        out_shape=(
            jax.ShapeDtypeStruct((far, block, head_dim), jnp.float32),
            jax.ShapeDtypeStruct((near - 1, far, block, head_dim), jnp.bfloat16),
        ),
        in_specs=[anywhere, anywhere, anywhere, anywhere],
        out_specs=(vmem, vmem),
        scratch_shapes=[
            pltpu.VMEM((rows, depth), jnp.bfloat16),
            pltpu.VMEM((depth, q_cols), jnp.bfloat16),
            pltpu.VMEM((depth, kv_cols), jnp.bfloat16),
            pltpu.VMEM((depth, kv_cols), jnp.bfloat16),
            pltpu.VMEM((rows * heads, head_dim), jnp.float32),
            pltpu.VMEM((rows * kv_heads, head_dim), jnp.float32),
            pltpu.VMEM((rows * kv_heads, head_dim), jnp.float32),
            pltpu.SemaphoreType.DMA((3 + len(widths),)),
        ],
        compiler_params=pltpu.CompilerParams(vmem_limit_bytes=26 * MIB),
        cost_estimate=pl.CostEstimate(
            flops=2 * rows * depth * (q_cols + 2 * kv_cols),
            bytes_accessed=2 * depth * (q_cols + 2 * kv_cols),
            transcendentals=0,
        ),
        name="project",
    )(in_hbm(tokens), in_hbm(w_query), in_hbm(w_key), in_hbm(w_value))

    received = [to_near(send[j - 1], j) for j in range(1, near)]

    summed = pl.pallas_call(
        combine_kernel,
        out_shape=[
            jax.ShapeDtypeStruct((block, head_dim), jnp.float32 if k == 0 else jnp.bfloat16)
            for k in range(far)
        ],
        in_specs=[vmem] * (2 + len(received)),
        out_specs=[vmem] * far,
        compiler_params=pltpu.CompilerParams(vmem_limit_bytes=12 * MIB),
        cost_estimate=pl.CostEstimate(flops=0, bytes_accessed=16 * MIB, transcendentals=0),
        name="combine",
    )(in_vmem(value_cache), keep, *received)

    parts = [summed[0]] + [to_far(summed[k], k) for k in range(1, far)]

    half = head_dim // 2
    freqs = rope_base ** (-2.0 * jnp.arange(half).astype(jnp.float32) / (2.0 * half))
    positions = lengths.astype(jnp.float32)[:, None]
    angles = positions * freqs[None, :]
    cosine = jnp.cos(angles)
    sine = jnp.sin(angles)
    table = jnp.concatenate(
        [
            jnp.concatenate([cosine, cosine], axis=1),
            jnp.concatenate([-sine, sine], axis=1),
            jnp.broadcast_to(positions, (own_rows, head_dim)),
        ],
        axis=0,
    )

    mixed = pl.pallas_call(
        attend_kernel,
        out_shape=jax.ShapeDtypeStruct((own_rows * heads, head_dim), jnp.bfloat16),
        in_specs=[vmem] * (3 + far),
        out_specs=vmem,
        compiler_params=pltpu.CompilerParams(vmem_limit_bytes=12 * MIB),
        cost_estimate=pl.CostEstimate(
            flops=4 * own_rows * heads * slots * head_dim,
            bytes_accessed=4 * own_rows * kv_heads * slots * head_dim,
            transcendentals=own_rows * heads * slots,
        ),
        name="attend",
    )(table, in_vmem(key_cache), in_vmem(value_cache), *parts)

    pair = jnp.stack([mixed] + [to_near(mixed, j) for j in range(1, near)])
    blocks = [pair] + [to_far(pair, k) for k in range(1, far)]

    own, other = pl.pallas_call(
        functools.partial(output_kernel, n, gy, far),
        out_shape=(
            jax.ShapeDtypeStruct((rows // gy, out_cols), jnp.float32),
            jax.ShapeDtypeStruct((gy - 1, rows // gy, out_cols), jnp.bfloat16),
        ),
        in_specs=[vmem] * (1 + far),
        out_specs=(vmem, vmem),
        scratch_shapes=[
            pltpu.VMEM((rows * heads, head_dim), jnp.float32),
            pltpu.VMEM((rows, q_cols), jnp.bfloat16),
        ],
        compiler_params=pltpu.CompilerParams(vmem_limit_bytes=12 * MIB),
        cost_estimate=pl.CostEstimate(
            flops=2 * rows * q_cols * out_cols,
            bytes_accessed=2 * q_cols * out_cols,
            transcendentals=0,
        ),
        name="output",
    )(in_vmem(w_out), *blocks)

    total = own
    for j in range(1, gy):
        part = lax.ppermute(other[j - 1], "gy", [(i, (i + j) % gy) for i in range(gy)])
        total = total + part.astype(jnp.float32)
    return total.astype(jnp.bfloat16)


def solution(mesh):
    in_specs = (
        P("groups", "gx"),
        P("gx", "gy"),
        P("gx", "gy"),
        P("gx", "gy"),
        P("gy", "gx"),
        P(("groups", "gx"), "gy", None, None),
        P(("groups", "gx"), "gy", None, None),
        P(("groups", "gx")),
    )
    out_specs = P(("groups", "gy"), "gx")
    body = functools.partial(on_device, mesh.shape["gx"], mesh.shape["gy"])
    return jax.shard_map(body, mesh=mesh, in_specs=in_specs, out_specs=out_specs, check_vma=False)
```

time: 44.5 us -> 41.9 us (0.942)
  Pallas kernels: 13.7 us -> 11.7 us
  waiting for transfers between devices: 16.1 us -> 15.5 us
    pallas_call x2, Pallas kernels: 8.68 us -> 7.77 us  [the longest x1 7.75 us: on_device(): pl.pallas_call(functools.partial(project_kernel, near, widths, head_dim),...]
    pallas_call x1, Pallas kernels: 3.53 us -> 2.89 us  [on_device(): pl.pallas_call(functools.partial(output_kernel, n, gy, far), out_shape=(j...]
    pallas_call x1, Pallas kernels: 1.51 us -> 0.99 us  [on_device(): pl.pallas_call(attend_kernel, out_shape=jax.ShapeDtypeStruct((own_rows *...]
  transfers between devices with their start and end apart: 9 -> 9, of which waited for: 7 -> 7; matrix products, arithmetic and copies ran while one was open for 0% -> 1% of each run, Pallas kernels for 0% -> 0%
where the time goes in v3:
time: 41.9 us; the launch traced here: 41.8 us
  waiting for transfers between devices  15.5 us (37%)
  starting transfers between devices  13.6 us (32%)
  Pallas kernels  11.7 us (28%)
  other arithmetic  0.85 us (2%)
    ppermute x6, starting transfers between devices, to_far(): lax.ppermute(x, 'gx', [(f * near + i, int(partner(f, k, far)) * near + i)...  8.91 us
    ppermute x6, waiting for transfers between devices, to_far(): lax.ppermute(x, 'gx', [(f * near + i, int(partner(f, k, far)) * near + i)...  8.25 us
    pallas_call x1, Pallas kernels, on_device(): pl.pallas_call(functools.partial(project_kernel, near, widths, head_dim),...  7.75 us
    ppermute x2, waiting for transfers between devices, to_near(): lax.ppermute(x, 'gx', [(f * near + i, f * near + (i + j) % near) for f in...  6.04 us
    ppermute x2, starting transfers between devices, to_near(): lax.ppermute(x, 'gx', [(f * near + i, f * near + (i + j) % near) for f in...  4.63 us
    pallas_call x1, Pallas kernels, on_device(): pl.pallas_call(functools.partial(output_kernel, n, gy, far), out_shape=(j...  2.89 us
    ppermute x1, waiting for transfers between devices, on_device(): lax.ppermute(other[j - 1], 'gy', [(i, (i + j) % gy) for i in range(gy)])  1.24 us
    pallas_call x1, Pallas kernels, on_device(): pl.pallas_call(attend_kernel, out_shape=jax.ShapeDtypeStruct((own_rows *...  0.99 us
  transfers between devices with their start and end apart: 9, of which 7 were waited for; matrix products, arithmetic and copies ran while one was open for 1% of the time, Pallas kernels for 0%

profile of v3, /device:TPU:0, one launch (start us, length us, event | category | flops | bytes accessed | tf_op | source)
XLA Modules:
  0.0 41.8 jit_solution(4074513738601999114)
XLA Ops:
  0.0 0.0 copy-start.3
  0.0 0.0 copy-start.1
  0.0 0.0 copy-start.2
  0.0 7.7 %project.1 = (f32[4,144,128]{2,1,0:T(8,128)S(1)}, bf16[1,4,144,128]{3,2,1,0:T(8,128)(2,1)S(1)}) custom-call(bf16[32,2048]{1,0:T(8,128)(2,1)} %tokens_ref.1, bf16[2048,4096]{1,0:T(8,128)(2,1)} %wq_ref.1, bf16[2048,256]{1,0:T(8,128)(2,1)} %wk_ref.1, bf16[2048,256]{1,0:T(8,128)(2,1)} %wv_ref.1), custom_call_target="tpu_custom_call" | custom-call | flops 603979776 | bytes 18874368 | tf_op jit(solution)/shard_map/project/pallas_call | solution.py:238
  7.8 3.0 %collective-permute-start = (bf16[4,144,128]{2,1,0:T(8,128)(2,1)S(1)}, bf16[4,144,128]{2,1,0:T(8,128)(2,1)S(1)}, u32[]{:S(2)}, u32[]{:S(2)}) collective-permute-start(bf16[4,144,128]{2,1,0:T(8,128)(2,1)S(1)} %bitcast.5), channel_id=1, source_target_pairs={{0,2},{2,0},{4,6},{6,4},{8,10},{10,8},{12,14},{14,12},{1,3},{3,1},... | collective-permute-start | bytes 442376 | tf_op jit(solution)/shard_map/ppermute | solution.py:228
  10.8 0.0 copy-done.3
  10.8 0.1 pad.6.clone
  10.9 0.1 multiply_cosine_fusion
  11.0 3.6 %collective-permute-done.refs_0_ = bf16[4,144,128]{2,1,0:T(8,128)(2,1)S(1)} collective-permute-done((bf16[4,144,128]{2,1,0:T(8,128)(2,1)S(1)}, bf16[4,144,128]{2,1,0:T(8,128)(2,1)S(1)}, u32[]{:S(2)}, u32[]{:S(2)}) %collective-permute-start) | collective-permute-done | bytes 147488 | tf_op jit(solution)/shard_map/ppermute | solution.py:228
  14.7 0.0 copy-done.1
  14.7 1.9 %collective-permute-start.1 = (bf16[144,128]{1,0:T(8,128)(2,1)S(1)}, bf16[144,128]{1,0:T(8,128)(2,1)S(1)}, u32[]{:S(2)}, u32[]{:S(2)}) collective-permute-start(bf16[144,128]{1,0:T(8,128)(2,1)S(1)} %get-tuple-element.16), channel_id=1, source_target_pairs={{0,4},{2,6},{4,0},{6,2},{8,12},{10,14},{12,8},{14,10},{1,5},{3,7},... | collective-permute-start | bytes 110600 | tf_op jit(solution)/shard_map/ppermute | solution.py:233
  16.6 2.6 %collective-permute-start.2 = (bf16[144,128]{1,0:T(8,128)(2,1)S(1)}, bf16[144,128]{1,0:T(8,128)(2,1)S(1)}, u32[]{:S(2)}, u32[]{:S(2)}) collective-permute-start(bf16[144,128]{1,0:T(8,128)(2,1)S(1)} %get-tuple-element.17), channel_id=1, source_target_pairs={{0,8},{2,10},{4,12},{6,14},{8,0},{10,2},{12,4},{14,6},{1,9},{3,11}... | collective-permute-start | bytes 110600 | tf_op jit(solution)/shard_map/ppermute | solution.py:233
  19.1 0.0 collective-permute-start.3
  19.1 0.1 maximum_maximum_fusion.table_ref
  19.2 0.0 collective-permute-done.1.refs_1_
  19.2 2.5 %collective-permute-done.2.refs_2_ = bf16[144,128]{1,0:T(8,128)(2,1)S(1)} collective-permute-done((bf16[144,128]{1,0:T(8,128)(2,1)S(1)}, bf16[144,128]{1,0:T(8,128)(2,1)S(1)}, u32[]{:S(2)}, u32[]{:S(2)}) %collective-permute-start.2) | collective-permute-done | bytes 36896 | tf_op jit(solution)/shard_map/ppermute | solution.py:233
  21.8 3.2 %collective-permute-done.3.refs_3_ = bf16[144,128]{1,0:T(8,128)(2,1)S(1)} collective-permute-done((bf16[144,128]{1,0:T(8,128)(2,1)S(1)}, bf16[144,128]{1,0:T(8,128)(2,1)S(1)}, u32[]{:S(2)}, u32[]{:S(2)}) %collective-permute-start.3) | collective-permute-done | bytes 36896 | tf_op jit(solution)/shard_map/ppermute | solution.py:233
  24.9 0.0 copy-done.2
  24.9 1.0 %attend.1 = bf16[128,128]{1,0:T(8,128)(2,1)S(1)} custom-call(f32[12,128]{1,0:T(8,128)S(1)} %maximum_maximum_fusion.table_ref, bf16[4,2,1024,128]{3,2,1,0:T(8,128)(2,1)S(1)} %copy-done.2, bf16[4,2,1024,128]{3,2,1,0:T(8,128)(2,1)S(1)} %copy-done.1, f32[144,128]{1,0:T(8,128)S(1)} %get-tuple-element.15.refs_0_, ...), custom_call_target="tpu_custom_call" | custom-call | flops 67108864 | bytes 4194304 | tf_op jit(solution)/shard_map/attend/pallas_call | solution.py:297
  25.9 1.6 %collective-permute-start.4 = (bf16[128,128]{1,0:T(8,128)(2,1)S(1)}, bf16[128,128]{1,0:T(8,128)(2,1)S(1)}, u32[]{:S(2)}, u32[]{:S(2)}) collective-permute-start(bf16[128,128]{1,0:T(8,128)(2,1)S(1)} %attend.1), channel_id=1, source_target_pairs={{0,2},{2,0},{4,6},{6,4},{8,10},{10,8},{12,14},{14,12},{1,3},{3,1},... | collective-permute-start | bytes 98312 | tf_op jit(solution)/shard_map/ppermute | solution.py:228
  27.5 2.4 %collective-permute-done.4 = bf16[128,128]{1,0:T(8,128)(2,1)S(1)} collective-permute-done((bf16[128,128]{1,0:T(8,128)(2,1)S(1)}, bf16[128,128]{1,0:T(8,128)(2,1)S(1)}, u32[]{:S(2)}, u32[]{:S(2)}) %collective-permute-start.4) | collective-permute-done | bytes 32800 | tf_op jit(solution)/shard_map/ppermute | solution.py:228
  29.9 0.5 %collective-permute-start.7 = (bf16[2,128,128]{2,1,0:T(8,128)(2,1)S(1)}, bf16[2,128,128]{2,1,0:T(8,128)(2,1)S(1)}, u32[]{:S(2)}, u32[]{:S(2)}) collective-permute-start(bf16[2,128,128]{2,1,0:T(8,128)(2,1)S(1)} %pad_maximum_fusion.refs_0_), channel_id=1, source_target_pairs={{0,12},{2,14},{4,8},{6,10},{8,4},{10,6},{12,0},{14,2},{1,13},{3,15... | collective-permute-start | bytes 196616 | tf_op jit(solution)/shard_map/ppermute | solution.py:233
  30.4 0.0 collective-permute-start.6
  30.4 4.0 %collective-permute-start.5 = (bf16[2,128,128]{2,1,0:T(8,128)(2,1)S(1)}, bf16[2,128,128]{2,1,0:T(8,128)(2,1)S(1)}, u32[]{:S(2)}, u32[]{:S(2)}) collective-permute-start(bf16[2,128,128]{2,1,0:T(8,128)(2,1)S(1)} %pad_maximum_fusion.refs_0_), channel_id=1, source_target_pairs={{0,4},{2,6},{4,0},{6,2},{8,12},{10,14},{12,8},{14,10},{1,5},{3,7},... | collective-permute-start | bytes 196616 | tf_op jit(solution)/shard_map/ppermute | solution.py:233
  34.3 1.8 %collective-permute-done.7.refs_3_ = bf16[2,128,128]{2,1,0:T(8,128)(2,1)S(1)} collective-permute-done((bf16[2,128,128]{2,1,0:T(8,128)(2,1)S(1)}, bf16[2,128,128]{2,1,0:T(8,128)(2,1)S(1)}, u32[]{:S(2)}, u32[]{:S(2)}) %collective-permute-start.7) | collective-permute-done | bytes 65568 | tf_op jit(solution)/shard_map/ppermute | solution.py:233
  36.1 0.8 %collective-permute-done.6.refs_2_ = bf16[2,128,128]{2,1,0:T(8,128)(2,1)S(1)} collective-permute-done((bf16[2,128,128]{2,1,0:T(8,128)(2,1)S(1)}, bf16[2,128,128]{2,1,0:T(8,128)(2,1)S(1)}, u32[]{:S(2)}, u32[]{:S(2)}) %collective-permute-start.6) | collective-permute-done | bytes 65568 | tf_op jit(solution)/shard_map/ppermute | solution.py:233
  36.9 0.0 collective-permute-done.5.refs_1_
  36.9 0.0 copy-done
  36.9 2.9 %output.1 = (f32[16,2048]{1,0:T(8,128)S(1)}, bf16[1,16,2048]{2,1,0:T(8,128)(2,1)S(1)}) custom-call(bf16[4096,2048]{1,0:T(8,128)(2,1)S(1)} %copy-done, bf16[2,128,128]{2,1,0:T(8,128)(2,1)S(1)} %pad_maximum_fusion.refs_0_, bf16[2,128,128]{2,1,0:T(8,128)(2,1)S(1)} %collective-permute-done.5.refs_1_, bf16[2,128,128]{2,1,0:T(8,128)(2,1)S(1)} %collective-permute-done.6.refs_2_, ...), custom_call_target="tpu_custom_call" | custom-call | flops 536870912 | bytes 16777216 | tf_op jit(solution)/shard_map/output/pallas_call | solution.py:314
  39.8 0.1 collective-permute-start.8
  39.9 1.2 %collective-permute-done.8 = bf16[16,2048]{1,0:T(8,128)(2,1)S(1)} collective-permute-done((bf16[16,2048]{1,0:T(8,128)(2,1)S(1)}, bf16[16,2048]{1,0:T(8,128)(2,1)S(1)}, u32[]{:S(2)}, u32[]{:S(2)}) %collective-permute-start.8) | collective-permute-done | bytes 65568 | tf_op jit(solution)/shard_map/ppermute | solution.py:337
  41.1 0.6 %add_convert_fusion = bf16[16,2048]{1,0:T(8,128)(2,1)} fusion(f32[16,2048]{1,0:T(8,128)S(1)} %get-tuple-element.19, bf16[16,2048]{1,0:T(8,128)(2,1)S(1)} %collective-permute-done.8), kind=kLoop, calls=%fused_computation | loop fusion | flops 98304 | bytes 262144 | tf_op jit(solution)/shard_map/convert_element_type | solution.py:339
  (5 shorter events, 0.0 us)
Async XLA Ops:
  0.0 10.8 %copy-start.3 = (s32[4]{0:T(128)S(1)}, s32[4]{0:T(128)}, u32[]{:S(2)}) copy-start(s32[4]{0:T(128)} %param.15) | copy-start | bytes 52
  0.0 14.7 %copy-start.1 = (bf16[4,2,1024,128]{3,2,1,0:T(8,128)(2,1)S(1)}, bf16[4,2,1024,128]{3,2,1,0:T(8,128)(2,1)}, u32[]{:S(2)}) copy-start(bf16[4,2,1024,128]{3,2,1,0:T(8,128)(2,1)} %values.1) | copy-start | bytes 6291460
  0.0 24.9 %copy-start.2 = (bf16[4,2,1024,128]{3,2,1,0:T(8,128)(2,1)S(1)}, bf16[4,2,1024,128]{3,2,1,0:T(8,128)(2,1)}, u32[]{:S(2)}) copy-start(bf16[4,2,1024,128]{3,2,1,0:T(8,128)(2,1)} %keys.1) | copy-start | bytes 6291460
  0.0 36.9 %copy-start = (bf16[4096,2048]{1,0:T(8,128)(2,1)S(1)}, bf16[4096,2048]{1,0:T(8,128)(2,1)}, u32[]{:S(2)}) copy-start(bf16[4096,2048]{1,0:T(8,128)(2,1)} %w_ref.1) | copy-start | bytes 50331652
  7.8 6.9 %collective-permute-start = (bf16[4,144,128]{2,1,0:T(8,128)(2,1)S(1)}, bf16[4,144,128]{2,1,0:T(8,128)(2,1)S(1)}, u32[]{:S(2)}, u32[]{:S(2)}) collective-permute-start(bf16[4,144,128]{2,1,0:T(8,128)(2,1)S(1)} %bitcast.5), channel_id=1, source_target_pairs={{0,2},{2,0},{4,6},{6,4},{8,10},{10,8},{12,14},{14,12},{1,3},{3,1},... | collective-permute-start | bytes 442376 | tf_op jit(solution)/shard_map/ppermute | solution.py:228
  14.7 4.5 %collective-permute-start.1 = (bf16[144,128]{1,0:T(8,128)(2,1)S(1)}, bf16[144,128]{1,0:T(8,128)(2,1)S(1)}, u32[]{:S(2)}, u32[]{:S(2)}) collective-permute-start(bf16[144,128]{1,0:T(8,128)(2,1)S(1)} %get-tuple-element.16), channel_id=1, source_target_pairs={{0,4},{2,6},{4,0},{6,2},{8,12},{10,14},{12,8},{14,10},{1,5},{3,7},... | collective-permute-start | bytes 110600 | tf_op jit(solution)/shard_map/ppermute | solution.py:233
  16.6 5.2 %collective-permute-start.2 = (bf16[144,128]{1,0:T(8,128)(2,1)S(1)}, bf16[144,128]{1,0:T(8,128)(2,1)S(1)}, u32[]{:S(2)}, u32[]{:S(2)}) collective-permute-start(bf16[144,128]{1,0:T(8,128)(2,1)S(1)} %get-tuple-element.17), channel_id=1, source_target_pairs={{0,8},{2,10},{4,12},{6,14},{8,0},{10,2},{12,4},{14,6},{1,9},{3,11}... | collective-permute-start | bytes 110600 | tf_op jit(solution)/shard_map/ppermute | solution.py:233
  19.1 5.8 %collective-permute-start.3 = (bf16[144,128]{1,0:T(8,128)(2,1)S(1)}, bf16[144,128]{1,0:T(8,128)(2,1)S(1)}, u32[]{:S(2)}, u32[]{:S(2)}) collective-permute-start(bf16[144,128]{1,0:T(8,128)(2,1)S(1)} %get-tuple-element.18), channel_id=1, source_target_pairs={{0,12},{2,14},{4,8},{6,10},{8,4},{10,6},{12,0},{14,2},{1,13},{3,15... | collective-permute-start | bytes 110600 | tf_op jit(solution)/shard_map/ppermute | solution.py:233
  25.9 4.0 %collective-permute-start.4 = (bf16[128,128]{1,0:T(8,128)(2,1)S(1)}, bf16[128,128]{1,0:T(8,128)(2,1)S(1)}, u32[]{:S(2)}, u32[]{:S(2)}) collective-permute-start(bf16[128,128]{1,0:T(8,128)(2,1)S(1)} %attend.1), channel_id=1, source_target_pairs={{0,2},{2,0},{4,6},{6,4},{8,10},{10,8},{12,14},{14,12},{1,3},{3,1},... | collective-permute-start | bytes 98312 | tf_op jit(solution)/shard_map/ppermute | solution.py:228
  29.9 6.2 %collective-permute-start.7 = (bf16[2,128,128]{2,1,0:T(8,128)(2,1)S(1)}, bf16[2,128,128]{2,1,0:T(8,128)(2,1)S(1)}, u32[]{:S(2)}, u32[]{:S(2)}) collective-permute-start(bf16[2,128,128]{2,1,0:T(8,128)(2,1)S(1)} %pad_maximum_fusion.refs_0_), channel_id=1, source_target_pairs={{0,12},{2,14},{4,8},{6,10},{8,4},{10,6},{12,0},{14,2},{1,13},{3,15... | collective-permute-start | bytes 196616 | tf_op jit(solution)/shard_map/ppermute | solution.py:233
  30.4 6.6 %collective-permute-start.6 = (bf16[2,128,128]{2,1,0:T(8,128)(2,1)S(1)}, bf16[2,128,128]{2,1,0:T(8,128)(2,1)S(1)}, u32[]{:S(2)}, u32[]{:S(2)}) collective-permute-start(bf16[2,128,128]{2,1,0:T(8,128)(2,1)S(1)} %pad_maximum_fusion.refs_0_), channel_id=1, source_target_pairs={{0,8},{2,10},{4,12},{6,14},{8,0},{10,2},{12,4},{14,6},{1,9},{3,11}... | collective-permute-start | bytes 196616 | tf_op jit(solution)/shard_map/ppermute | solution.py:233
  30.4 6.6 %collective-permute-start.5 = (bf16[2,128,128]{2,1,0:T(8,128)(2,1)S(1)}, bf16[2,128,128]{2,1,0:T(8,128)(2,1)S(1)}, u32[]{:S(2)}, u32[]{:S(2)}) collective-permute-start(bf16[2,128,128]{2,1,0:T(8,128)(2,1)S(1)} %pad_maximum_fusion.refs_0_), channel_id=1, source_target_pairs={{0,4},{2,6},{4,0},{6,2},{8,12},{10,14},{12,8},{14,10},{1,5},{3,7},... | collective-permute-start | bytes 196616 | tf_op jit(solution)/shard_map/ppermute | solution.py:233
  39.8 1.3 %collective-permute-start.8 = (bf16[16,2048]{1,0:T(8,128)(2,1)S(1)}, bf16[16,2048]{1,0:T(8,128)(2,1)S(1)}, u32[]{:S(2)}, u32[]{:S(2)}) collective-permute-start(bf16[16,2048]{1,0:T(8,128)(2,1)S(1)} %bitcast.6), channel_id=1, source_target_pairs={{0,1},{1,0},{2,3},{3,2},{4,5},{5,4},{6,7},{7,6},{8,9},{9,8},{10,11... | collective-permute-start | bytes 196616 | tf_op jit(solution)/shard_map/ppermute | solution.py:337

commit v4 on v3

--- a/solution.py
+++ b/solution.py
@@ -11,33 +11,12 @@
 MIB = 1024 * 1024
 
 
-def chunk_widths(cols, head_dim):
-    unit = cols // 16
-    if cols % 16 or unit % head_dim:
-        return (cols,)
-    return (4 * unit, 4 * unit, 4 * unit, 2 * unit, unit, unit)
-
-
 def project_kernel(
-    near,
-    widths,
-    head_dim,
-    tokens_ref,
-    wq_ref,
-    wk_ref,
-    wv_ref,
-    keep_ref,
-    send_ref,
-    t_buf,
-    q_buf,
-    k_buf,
-    v_buf,
-    by_head,
-    k_rows,
-    v_rows,
-    sems,
+    near, far, device_at, own, slab, head_dim, tokens_ref, wq_ref, wk_ref, wv_ref, keep_ref, *refs
 ):
-    rows = tokens_ref.shape[0]
+    send_refs = refs[: near - 1]
+    t_buf, q_buf, k_buf, v_buf, partial, sems = refs[near - 1 :]
+    rows, depth = tokens_ref.shape
     heads = q_buf.shape[1] // head_dim
     kv_heads = wk_ref.shape[1] // head_dim
     t_copy = pltpu.make_async_copy(tokens_ref, t_buf, sems.at[0])
@@ -47,61 +26,53 @@
     k_copy.start()
     v_copy.start()
     q_copies = []
-    first = 0
-    for c, width in enumerate(widths):
-        at = slice(first, first + width)
-        copy = pltpu.make_async_copy(wq_ref.at[:, at], q_buf.at[:, at], sems.at[3 + c])
-        copy.start()
-        q_copies.append((copy, at))
-        first += width
-
-    far, block, _ = keep_ref.shape
-    own = rows // (far * near)
-    q_count = own * heads
-    me = lax.axis_index("gx")
-    mine, mine_far = lax.rem(me, near), lax.div(me, near)
-
-    def devices():
-        for f in range(far):
-            other = partner(mine_far, f, far) * near
-            yield keep_ref, (f,), other + mine
-            for j in range(1, near):
-                yield send_ref, (j - 1, f), other + lax.rem(mine + j, near)
-
-    def spread(dest, part, first, count):
-        for j in range(part.shape[1] // head_dim):
-            dest[pl.ds(first + j, rows, stride=count), :] = part[:, j * head_dim : (j + 1) * head_dim]
-
-    def put_kv():
-        for ref, at, d in devices():
-            size = own * kv_heads
-            rows_of = pl.ds(pl.multiple_of(d * size, size), size)
-            kv = jnp.concatenate([k_rows[rows_of, :], v_rows[rows_of, :]], axis=0)
-            ref[*at, q_count:, :] = kv.astype(ref.dtype)
-
-    def put_heads(first, count):
-        for ref, at, d in devices():
-            start = pl.multiple_of(d * q_count, q_count)
-            for r in range(own):
-                to = r * heads + first
-                ref[*at, to : to + count, :] = by_head[pl.ds(start + to, count), :].astype(ref.dtype)
-
+    for c in range(depth // slab):
+        at = slice(c * slab, (c + 1) * slab)
+        q_copies.append((pltpu.make_async_copy(wq_ref.at[at, :], q_buf.at[at, :], sems.at[3 + c]), at))
+        q_copies[-1][0].start()
+
+    row = lax.broadcasted_iota(jnp.int32, (rows, rows), 0)
+    column = lax.broadcasted_iota(jnp.int32, (rows, rows), 1)
+    wanted = jnp.zeros((rows, rows), jnp.int32)
+    for p in range(near):
+        for q in range(far):
+            at = p * far + q
+            wanted = jnp.where(row >= at * own, row + (device_at(p, q) - at) * own, wanted)
+    pick = (column == wanted).astype(jnp.bfloat16)
     t_copy.wait()
-    tokens = t_buf[...]
+    tokens = jnp.dot(pick, t_buf[...], preferred_element_type=jnp.float32).astype(jnp.bfloat16)
+
+    group = far * own
+
+    def put(part, head):
+        count = part.shape[1] // head_dim
+        for p in range(near):
+            ref = send_refs[p - 1] if p else keep_ref
+            tiles = [
+                part[p * group : (p + 1) * group, h * head_dim : (h + 1) * head_dim] for h in range(count)
+            ]
+            ref[head * group : (head + count) * group, :] = jnp.concatenate(tiles, axis=0).astype(ref.dtype)
+
+    def times(part, weights):
+        return jnp.dot(part, weights, preferred_element_type=jnp.float32)
+
     k_copy.wait()
-    spread(k_rows, jnp.dot(tokens, k_buf[...], preferred_element_type=jnp.float32), 0, kv_heads)
+    put(times(tokens, k_buf[...]), heads)
     v_copy.wait()
-    spread(v_rows, jnp.dot(tokens, v_buf[...], preferred_element_type=jnp.float32), 0, kv_heads)
-    put_kv()
-    step = 16 if heads % 16 == 0 else heads
-    done = 0
-    for copy, at in q_copies:
+    put(times(tokens, v_buf[...]), heads + kv_heads)
+    q_cols = q_buf.shape[1]
+    width = q_cols // 4 if q_cols % (4 * head_dim) == 0 else q_cols
+    for c, (copy, at) in enumerate(q_copies):
         copy.wait()
-        part = jnp.dot(tokens, q_buf[:, at], preferred_element_type=jnp.float32)
-        spread(by_head, part, at.start // head_dim, heads)
-        while done + step <= at.stop // head_dim:
-            put_heads(done, step)
-            done += step
+        for first in range(0, q_cols, width):
+            columns = slice(first, first + width)
+            part = times(tokens[:, at], q_buf[at, columns])
+            if c > 0:
+                part = part + partial[:, columns]
+            if c < len(q_copies) - 1:
+                partial[:, columns] = part
+            else:
+                put(part, first // head_dim)
 
 
 def partner(f, k, far):
@@ -112,14 +83,25 @@
     return f ^ k if far & (far - 1) == 0 else (f + far - k) % far
 
 
-def combine_kernel(cache_ref, keep_ref, *refs):
-    far = keep_ref.shape[0]
-    received, outs = refs[:-far], refs[-far:]
-    for k in range(far):
-        total = keep_ref[k]
-        for part in received:
-            total = total + part[k].astype(jnp.float32)
-        outs[k][...] = total.astype(outs[k].dtype)
+def combine_kernel(steps, heads, kv_heads, cache_ref, keep_ref, *refs):
+    received, outs, total_ref = refs[: -steps - 1], refs[-steps - 1 : -1], refs[-1]
+    total = keep_ref[...]
+    for part in received:
+        total = total + part[...].astype(jnp.float32)
+    total_ref[...] = total
+    own = outs[0].shape[0] // (heads + 2 * kv_heads)
+    group = steps * own
+
+    def of_heads(j, first, count):
+        return [total_ref[pl.ds(first * group + j * own + r, count, stride=group), :] for r in range(own)]
+
+    for j in range(steps):
+        rows = (
+            of_heads(j, 0, heads)
+            + of_heads(j, heads, kv_heads)
+            + of_heads(j, heads + kv_heads, kv_heads)
+        )
+        outs[j][...] = jnp.concatenate(rows, axis=0).astype(outs[j].dtype)
 
 
 def attend_kernel(table_ref, keys, values, *refs):
@@ -175,7 +157,8 @@
     out_ref[...] = jnp.concatenate(mixed, axis=0).astype(jnp.bfloat16)
 
 
-def output_kernel(n, gy, far, w_ref, *refs):
+def output_kernel(n, gy, order, w_ref, *refs):
+    far = len(order)
     blocks = refs[:far]
     own_ref, other_ref, wide, lhs = refs[far:]
     near, per_dev, head_dim = blocks[0].shape
@@ -188,7 +171,7 @@
     mine, mine_far = lax.rem(me, near), lax.div(me, near)
     for k in range(far):
         for j in range(near):
-            d = source(mine_far, k, far) * near + lax.rem(mine + near - j, near)
+            d = source(mine_far, order[k], far) * near + lax.rem(mine + near - j, near)
             place = lax.rem(lax.div(d, half) + gy - me_gy, gy) * half + lax.rem(d, half)
             wide[pl.ds(pl.multiple_of(place * per_dev, per_dev), per_dev), :] = blocks[k][j].astype(jnp.float32)
     for h in range(heads):
@@ -224,6 +207,9 @@
 
     near = 2 if n % 2 == 0 else 1
     far = n // near
+    order_out = sorted(range(1, far), key=lambda k: -(k // 2))
+    order_back = sorted(range(1, far), key=lambda k: k % 2)
+
     def to_near(x, j):
         return lax.ppermute(
             x, "gx", [(f * near + i, f * near + (i + j) % near) for f in range(far) for i in range(near)]
@@ -234,24 +220,32 @@
             x, "gx", [(f * near + i, int(partner(f, k, far)) * near + i) for f in range(far) for i in range(near)]
         )
 
-    widths = chunk_widths(q_cols, head_dim)
-    keep, send = pl.pallas_call(
-        functools.partial(project_kernel, near, widths, head_dim),
-        out_shape=(
-            jax.ShapeDtypeStruct((far, block, head_dim), jnp.float32),
-            jax.ShapeDtypeStruct((near - 1, far, block, head_dim), jnp.bfloat16),
-        ),
+    slab = 256 if depth % 256 == 0 else depth
+
+    def device_at(j, k):
+        me = lax.axis_index("gx")
+        return partner(lax.div(me, near), k, far) * near + lax.rem(lax.rem(me, near) + j, near)
+
+    all_heads = heads + 2 * kv_heads
+    keep, *sends = pl.pallas_call(
+        functools.partial(
+            project_kernel, near, far, device_at, own_rows, slab, head_dim
+        ),
+        out_shape=[
+            jax.ShapeDtypeStruct(
+                (all_heads * far * own_rows, head_dim), jnp.bfloat16 if p else jnp.float32
+            )
+            for p in range(near)
+        ],
         in_specs=[anywhere, anywhere, anywhere, anywhere],
-        out_specs=(vmem, vmem),
+        out_specs=[vmem] * near,
         scratch_shapes=[
             pltpu.VMEM((rows, depth), jnp.bfloat16),
             pltpu.VMEM((depth, q_cols), jnp.bfloat16),
             pltpu.VMEM((depth, kv_cols), jnp.bfloat16),
             pltpu.VMEM((depth, kv_cols), jnp.bfloat16),
-            pltpu.VMEM((rows * heads, head_dim), jnp.float32),
-            pltpu.VMEM((rows * kv_heads, head_dim), jnp.float32),
-            pltpu.VMEM((rows * kv_heads, head_dim), jnp.float32),
-            pltpu.SemaphoreType.DMA((3 + len(widths),)),
+            pltpu.VMEM((rows, q_cols), jnp.float32),
+            pltpu.SemaphoreType.DMA((3 + depth // slab,)),
         ],
         compiler_params=pltpu.CompilerParams(vmem_limit_bytes=26 * MIB),
         cost_estimate=pl.CostEstimate(
@@ -262,22 +256,23 @@
         name="project",
     )(in_hbm(tokens), in_hbm(w_query), in_hbm(w_key), in_hbm(w_value))
 
-    received = [to_near(send[j - 1], j) for j in range(1, near)]
+    received = [to_near(sends[p - 1], p) for p in range(1, near)]
 
     summed = pl.pallas_call(
-        combine_kernel,
+        functools.partial(combine_kernel, far, heads, kv_heads),
         out_shape=[
-            jax.ShapeDtypeStruct((block, head_dim), jnp.float32 if k == 0 else jnp.bfloat16)
-            for k in range(far)
+            jax.ShapeDtypeStruct((block, head_dim), jnp.bfloat16 if q else jnp.float32)
+            for q in range(far)
         ],
         in_specs=[vmem] * (2 + len(received)),
         out_specs=[vmem] * far,
+        scratch_shapes=[pltpu.VMEM((all_heads * far * own_rows, head_dim), jnp.float32)],
         compiler_params=pltpu.CompilerParams(vmem_limit_bytes=12 * MIB),
         cost_estimate=pl.CostEstimate(flops=0, bytes_accessed=16 * MIB, transcendentals=0),
         name="combine",
     )(in_vmem(value_cache), keep, *received)
 
-    parts = [summed[0]] + [to_far(summed[k], k) for k in range(1, far)]
+    parts = [summed[0]] + [to_far(summed[q], q) for q in order_out]
 
     half = head_dim // 2
     freqs = rope_base ** (-2.0 * jnp.arange(half).astype(jnp.float32) / (2.0 * half))
@@ -297,7 +292,7 @@
     mixed = pl.pallas_call(
         attend_kernel,
         out_shape=jax.ShapeDtypeStruct((own_rows * heads, head_dim), jnp.bfloat16),
-        in_specs=[vmem] * (3 + far),
+        in_specs=[vmem] * (3 + len(parts)),
         out_specs=vmem,
         compiler_params=pltpu.CompilerParams(vmem_limit_bytes=12 * MIB),
         cost_estimate=pl.CostEstimate(
@@ -309,10 +304,10 @@
     )(table, in_vmem(key_cache), in_vmem(value_cache), *parts)
 
     pair = jnp.stack([mixed] + [to_near(mixed, j) for j in range(1, near)])
-    blocks = [pair] + [to_far(pair, k) for k in range(1, far)]
+    blocks = [pair] + [to_far(pair, k) for k in order_back]
 
     own, other = pl.pallas_call(
-        functools.partial(output_kernel, n, gy, far),
+        functools.partial(output_kernel, n, gy, (0, *order_back)),
         out_shape=(
             jax.ShapeDtypeStruct((rows // gy, out_cols), jnp.float32),
             jax.ShapeDtypeStruct((gy - 1, rows // gy, out_cols), jnp.bfloat16),

time: 41.9 us -> 40.4 us (0.964)
  waiting for transfers between devices: 15.5 us -> 14.5 us
  Pallas kernels: 11.7 us -> 11.2 us
    ppermute x6, waiting for transfers between devices: 8.25 us -> 7.18 us  [to_far(): lax.ppermute(x, 'gx', [(f * near + i, int(partner(f, k, far)) * near + i)...]
    pallas_call x3, Pallas kernels: 10.7 us -> 10.2 us  [the longest x1 7.22 us: on_device(): pl.pallas_call(functools.partial(project_kernel, near, far, device_at, ow...]
where the time goes in v4:
time: 40.4 us; the launch traced here: 40.3 us
  waiting for transfers between devices  14.5 us (36%)
  starting transfers between devices  13.6 us (34%)
  Pallas kernels  11.2 us (28%)
  other arithmetic  0.85 us (2%)
    ppermute x6, starting transfers between devices, to_far(): lax.ppermute(x, 'gx', [(f * near + i, int(partner(f, k, far)) * near + i)...  8.91 us
    pallas_call x1, Pallas kernels, on_device(): pl.pallas_call(functools.partial(project_kernel, near, far, device_at, ow...  7.22 us
    ppermute x6, waiting for transfers between devices, to_far(): lax.ppermute(x, 'gx', [(f * near + i, int(partner(f, k, far)) * near + i)...  7.18 us
    ppermute x2, waiting for transfers between devices, to_near(): lax.ppermute(x, 'gx', [(f * near + i, f * near + (i + j) % near) for f in...  6.04 us
    ppermute x2, starting transfers between devices, to_near(): lax.ppermute(x, 'gx', [(f * near + i, f * near + (i + j) % near) for f in...  4.63 us
    pallas_call x1, Pallas kernels, on_device(): pl.pallas_call(functools.partial(output_kernel, n, gy, (0, *order_back)),...  2.88 us
    ppermute x1, waiting for transfers between devices, on_device(): lax.ppermute(other[j - 1], 'gy', [(i, (i + j) % gy) for i in range(gy)])  1.24 us
    pallas_call x1, Pallas kernels, on_device(): pl.pallas_call(attend_kernel, out_shape=jax.ShapeDtypeStruct((own_rows *...  0.99 us
  transfers between devices with their start and end apart: 9, of which 7 were waited for; matrix products, arithmetic and copies ran while one was open for 1% of the time, Pallas kernels for 0%

profile of v4, /device:TPU:0, one launch (start us, length us, event | category | flops | bytes accessed | tf_op | source)
XLA Modules:
  0.0 40.3 jit_solution(18201043948518998073)
XLA Ops:
  0.0 0.0 copy-start.3
  0.0 0.0 copy-start.1
  0.0 7.2 %project.1 = (f32[576,128]{1,0:T(8,128)S(1)}, bf16[576,128]{1,0:T(8,128)(2,1)S(1)}) custom-call(bf16[32,2048]{1,0:T(8,128)(2,1)} %tokens_ref.1, bf16[2048,4096]{1,0:T(8,128)(2,1)} %wq_ref.1, bf16[2048,256]{1,0:T(8,128)(2,1)} %wk_ref.1, bf16[2048,256]{1,0:T(8,128)(2,1)} %wv_ref.1), custom_call_target="tpu_custom_call" | custom-call | flops 603979776 | bytes 18874368 | tf_op jit(solution)/shard_map/project/pallas_call | solution.py:230
  7.2 3.0 %collective-permute-start = (bf16[576,128]{1,0:T(8,128)(2,1)S(1)}, bf16[576,128]{1,0:T(8,128)(2,1)S(1)}, u32[]{:S(2)}, u32[]{:S(2)}) collective-permute-start(bf16[576,128]{1,0:T(8,128)(2,1)S(1)} %get-tuple-element.14), channel_id=1, source_target_pairs={{0,2},{2,0},{4,6},{6,4},{8,10},{10,8},{12,14},{14,12},{1,3},{3,1},... | collective-permute-start | bytes 442376 | tf_op jit(solution)/shard_map/ppermute | solution.py:214
  10.3 0.0 copy-done.3
  10.3 0.1 pad.6.clone
  10.4 0.1 multiply_cosine_fusion
  10.5 3.6 %collective-permute-done.refs_0_ = bf16[576,128]{1,0:T(8,128)(2,1)S(1)} collective-permute-done((bf16[576,128]{1,0:T(8,128)(2,1)S(1)}, bf16[576,128]{1,0:T(8,128)(2,1)S(1)}, u32[]{:S(2)}, u32[]{:S(2)}) %collective-permute-start) | collective-permute-done | bytes 147488 | tf_op jit(solution)/shard_map/ppermute | solution.py:214
  14.1 0.0 copy-done.1
  14.1 0.1 combine.1
  14.3 2.9 %collective-permute-start.1 = (bf16[144,128]{1,0:T(8,128)(2,1)S(1)}, bf16[144,128]{1,0:T(8,128)(2,1)S(1)}, u32[]{:S(2)}, u32[]{:S(2)}) collective-permute-start(bf16[144,128]{1,0:T(8,128)(2,1)S(1)} %get-tuple-element.16), channel_id=1, source_target_pairs={{0,8},{2,10},{4,12},{6,14},{8,0},{10,2},{12,4},{14,6},{1,9},{3,11}... | collective-permute-start | bytes 110600 | tf_op jit(solution)/shard_map/ppermute | solution.py:219
  17.1 1.3 %collective-permute-start.2 = (bf16[144,128]{1,0:T(8,128)(2,1)S(1)}, bf16[144,128]{1,0:T(8,128)(2,1)S(1)}, u32[]{:S(2)}, u32[]{:S(2)}) collective-permute-start(bf16[144,128]{1,0:T(8,128)(2,1)S(1)} %get-tuple-element.17), channel_id=1, source_target_pairs={{0,12},{2,14},{4,8},{6,10},{8,4},{10,6},{12,0},{14,2},{1,13},{3,15... | collective-permute-start | bytes 110600 | tf_op jit(solution)/shard_map/ppermute | solution.py:219
  18.5 0.2 collective-permute-start.3
  18.7 0.1 maximum_maximum_fusion.table_ref
  18.8 0.4 collective-permute-done.1.refs_1_
  19.2 3.7 %collective-permute-done.2.refs_2_ = bf16[144,128]{1,0:T(8,128)(2,1)S(1)} collective-permute-done((bf16[144,128]{1,0:T(8,128)(2,1)S(1)}, bf16[144,128]{1,0:T(8,128)(2,1)S(1)}, u32[]{:S(2)}, u32[]{:S(2)}) %collective-permute-start.2) | collective-permute-done | bytes 36896 | tf_op jit(solution)/shard_map/ppermute | solution.py:219
  22.9 0.0 collective-permute-done.3.refs_3_
  22.9 0.0 copy-done.2
  22.9 1.0 %attend.1 = bf16[128,128]{1,0:T(8,128)(2,1)S(1)} custom-call(f32[12,128]{1,0:T(8,128)S(1)} %maximum_maximum_fusion.table_ref, bf16[4,2,1024,128]{3,2,1,0:T(8,128)(2,1)S(1)} %copy-done.2, bf16[4,2,1024,128]{3,2,1,0:T(8,128)(2,1)S(1)} %copy-done.1, f32[144,128]{1,0:T(8,128)S(1)} %get-tuple-element.15.refs_0_, ...), custom_call_target="tpu_custom_call" | custom-call | flops 67108864 | bytes 4194304 | tf_op jit(solution)/shard_map/attend/pallas_call | solution.py:292
  23.9 1.6 %collective-permute-start.4 = (bf16[128,128]{1,0:T(8,128)(2,1)S(1)}, bf16[128,128]{1,0:T(8,128)(2,1)S(1)}, u32[]{:S(2)}, u32[]{:S(2)}) collective-permute-start(bf16[128,128]{1,0:T(8,128)(2,1)S(1)} %attend.1), channel_id=1, source_target_pairs={{0,2},{2,0},{4,6},{6,4},{8,10},{10,8},{12,14},{14,12},{1,3},{3,1},... | collective-permute-start | bytes 98312 | tf_op jit(solution)/shard_map/ppermute | solution.py:214
  25.5 2.4 %collective-permute-done.4 = bf16[128,128]{1,0:T(8,128)(2,1)S(1)} collective-permute-done((bf16[128,128]{1,0:T(8,128)(2,1)S(1)}, bf16[128,128]{1,0:T(8,128)(2,1)S(1)}, u32[]{:S(2)}, u32[]{:S(2)}) %collective-permute-start.4) | collective-permute-done | bytes 32800 | tf_op jit(solution)/shard_map/ppermute | solution.py:214
  27.9 2.1 %collective-permute-start.7 = (bf16[2,128,128]{2,1,0:T(8,128)(2,1)S(1)}, bf16[2,128,128]{2,1,0:T(8,128)(2,1)S(1)}, u32[]{:S(2)}, u32[]{:S(2)}) collective-permute-start(bf16[2,128,128]{2,1,0:T(8,128)(2,1)S(1)} %pad_maximum_fusion.refs_0_), channel_id=1, source_target_pairs={{0,12},{2,14},{4,8},{6,10},{8,4},{10,6},{12,0},{14,2},{1,13},{3,15... | collective-permute-start | bytes 196616 | tf_op jit(solution)/shard_map/ppermute | solution.py:219
  30.0 0.0 collective-permute-start.6
  30.0 2.4 %collective-permute-start.5 = (bf16[2,128,128]{2,1,0:T(8,128)(2,1)S(1)}, bf16[2,128,128]{2,1,0:T(8,128)(2,1)S(1)}, u32[]{:S(2)}, u32[]{:S(2)}) collective-permute-start(bf16[2,128,128]{2,1,0:T(8,128)(2,1)S(1)} %pad_maximum_fusion.refs_0_), channel_id=1, source_target_pairs={{0,8},{2,10},{4,12},{6,14},{8,0},{10,2},{12,4},{14,6},{1,9},{3,11}... | collective-permute-start | bytes 196616 | tf_op jit(solution)/shard_map/ppermute | solution.py:219
  32.3 1.7 %collective-permute-done.7.refs_3_ = bf16[2,128,128]{2,1,0:T(8,128)(2,1)S(1)} collective-permute-done((bf16[2,128,128]{2,1,0:T(8,128)(2,1)S(1)}, bf16[2,128,128]{2,1,0:T(8,128)(2,1)S(1)}, u32[]{:S(2)}, u32[]{:S(2)}) %collective-permute-start.7) | collective-permute-done | bytes 65568 | tf_op jit(solution)/shard_map/ppermute | solution.py:219
  34.1 1.4 %collective-permute-done.6.refs_2_ = bf16[2,128,128]{2,1,0:T(8,128)(2,1)S(1)} collective-permute-done((bf16[2,128,128]{2,1,0:T(8,128)(2,1)S(1)}, bf16[2,128,128]{2,1,0:T(8,128)(2,1)S(1)}, u32[]{:S(2)}, u32[]{:S(2)}) %collective-permute-start.6) | collective-permute-done | bytes 65568 | tf_op jit(solution)/shard_map/ppermute | solution.py:219
  35.4 0.0 collective-permute-done.5.refs_1_
  35.4 0.0 copy-done
  35.4 2.9 %output.1 = (f32[16,2048]{1,0:T(8,128)S(1)}, bf16[1,16,2048]{2,1,0:T(8,128)(2,1)S(1)}) custom-call(bf16[4096,2048]{1,0:T(8,128)(2,1)S(1)} %copy-done, bf16[2,128,128]{2,1,0:T(8,128)(2,1)S(1)} %pad_maximum_fusion.refs_0_, bf16[2,128,128]{2,1,0:T(8,128)(2,1)S(1)} %collective-permute-done.5.refs_1_, bf16[2,128,128]{2,1,0:T(8,128)(2,1)S(1)} %collective-permute-done.6.refs_2_, ...), custom_call_target="tpu_custom_call" | custom-call | flops 536870912 | bytes 16777216 | tf_op jit(solution)/shard_map/output/pallas_call | solution.py:309
  38.3 0.1 collective-permute-start.8
  38.4 1.2 %collective-permute-done.8 = bf16[16,2048]{1,0:T(8,128)(2,1)S(1)} collective-permute-done((bf16[16,2048]{1,0:T(8,128)(2,1)S(1)}, bf16[16,2048]{1,0:T(8,128)(2,1)S(1)}, u32[]{:S(2)}, u32[]{:S(2)}) %collective-permute-start.8) | collective-permute-done | bytes 65568 | tf_op jit(solution)/shard_map/ppermute | solution.py:332
  39.6 0.6 %add_convert_fusion = bf16[16,2048]{1,0:T(8,128)(2,1)} fusion(f32[16,2048]{1,0:T(8,128)S(1)} %get-tuple-element.19, bf16[16,2048]{1,0:T(8,128)(2,1)S(1)} %collective-permute-done.8), kind=kLoop, calls=%fused_computation | loop fusion | flops 98304 | bytes 262144 | tf_op jit(solution)/shard_map/convert_element_type | solution.py:334
  (5 shorter events, 0.0 us)
Async XLA Ops:
  0.0 10.3 %copy-start.3 = (s32[4]{0:T(128)S(1)}, s32[4]{0:T(128)}, u32[]{:S(2)}) copy-start(s32[4]{0:T(128)} %param.15) | copy-start | bytes 52
  0.0 14.1 %copy-start.1 = (bf16[4,2,1024,128]{3,2,1,0:T(8,128)(2,1)S(1)}, bf16[4,2,1024,128]{3,2,1,0:T(8,128)(2,1)}, u32[]{:S(2)}) copy-start(bf16[4,2,1024,128]{3,2,1,0:T(8,128)(2,1)} %values.1) | copy-start | bytes 6291460
  0.0 22.9 %copy-start.2 = (bf16[4,2,1024,128]{3,2,1,0:T(8,128)(2,1)S(1)}, bf16[4,2,1024,128]{3,2,1,0:T(8,128)(2,1)}, u32[]{:S(2)}) copy-start(bf16[4,2,1024,128]{3,2,1,0:T(8,128)(2,1)} %keys.1) | copy-start | bytes 6291460
  0.0 35.4 %copy-start = (bf16[4096,2048]{1,0:T(8,128)(2,1)S(1)}, bf16[4096,2048]{1,0:T(8,128)(2,1)}, u32[]{:S(2)}) copy-start(bf16[4096,2048]{1,0:T(8,128)(2,1)} %w_ref.1) | copy-start | bytes 50331652
  7.2 6.9 %collective-permute-start = (bf16[576,128]{1,0:T(8,128)(2,1)S(1)}, bf16[576,128]{1,0:T(8,128)(2,1)S(1)}, u32[]{:S(2)}, u32[]{:S(2)}) collective-permute-start(bf16[576,128]{1,0:T(8,128)(2,1)S(1)} %get-tuple-element.14), channel_id=1, source_target_pairs={{0,2},{2,0},{4,6},{6,4},{8,10},{10,8},{12,14},{14,12},{1,3},{3,1},... | collective-permute-start | bytes 442376 | tf_op jit(solution)/shard_map/ppermute | solution.py:214
  14.3 4.9 %collective-permute-start.1 = (bf16[144,128]{1,0:T(8,128)(2,1)S(1)}, bf16[144,128]{1,0:T(8,128)(2,1)S(1)}, u32[]{:S(2)}, u32[]{:S(2)}) collective-permute-start(bf16[144,128]{1,0:T(8,128)(2,1)S(1)} %get-tuple-element.16), channel_id=1, source_target_pairs={{0,8},{2,10},{4,12},{6,14},{8,0},{10,2},{12,4},{14,6},{1,9},{3,11}... | collective-permute-start | bytes 110600 | tf_op jit(solution)/shard_map/ppermute | solution.py:219
  17.1 5.8 %collective-permute-start.2 = (bf16[144,128]{1,0:T(8,128)(2,1)S(1)}, bf16[144,128]{1,0:T(8,128)(2,1)S(1)}, u32[]{:S(2)}, u32[]{:S(2)}) collective-permute-start(bf16[144,128]{1,0:T(8,128)(2,1)S(1)} %get-tuple-element.17), channel_id=1, source_target_pairs={{0,12},{2,14},{4,8},{6,10},{8,4},{10,6},{12,0},{14,2},{1,13},{3,15... | collective-permute-start | bytes 110600 | tf_op jit(solution)/shard_map/ppermute | solution.py:219
  18.5 4.4 %collective-permute-start.3 = (bf16[144,128]{1,0:T(8,128)(2,1)S(1)}, bf16[144,128]{1,0:T(8,128)(2,1)S(1)}, u32[]{:S(2)}, u32[]{:S(2)}) collective-permute-start(bf16[144,128]{1,0:T(8,128)(2,1)S(1)} %get-tuple-element.18), channel_id=1, source_target_pairs={{0,4},{2,6},{4,0},{6,2},{8,12},{10,14},{12,8},{14,10},{1,5},{3,7},... | collective-permute-start | bytes 110600 | tf_op jit(solution)/shard_map/ppermute | solution.py:219
  23.9 4.0 %collective-permute-start.4 = (bf16[128,128]{1,0:T(8,128)(2,1)S(1)}, bf16[128,128]{1,0:T(8,128)(2,1)S(1)}, u32[]{:S(2)}, u32[]{:S(2)}) collective-permute-start(bf16[128,128]{1,0:T(8,128)(2,1)S(1)} %attend.1), channel_id=1, source_target_pairs={{0,2},{2,0},{4,6},{6,4},{8,10},{10,8},{12,14},{14,12},{1,3},{3,1},... | collective-permute-start | bytes 98312 | tf_op jit(solution)/shard_map/ppermute | solution.py:214
  27.9 6.2 %collective-permute-start.7 = (bf16[2,128,128]{2,1,0:T(8,128)(2,1)S(1)}, bf16[2,128,128]{2,1,0:T(8,128)(2,1)S(1)}, u32[]{:S(2)}, u32[]{:S(2)}) collective-permute-start(bf16[2,128,128]{2,1,0:T(8,128)(2,1)S(1)} %pad_maximum_fusion.refs_0_), channel_id=1, source_target_pairs={{0,12},{2,14},{4,8},{6,10},{8,4},{10,6},{12,0},{14,2},{1,13},{3,15... | collective-permute-start | bytes 196616 | tf_op jit(solution)/shard_map/ppermute | solution.py:219
  30.0 5.4 %collective-permute-start.6 = (bf16[2,128,128]{2,1,0:T(8,128)(2,1)S(1)}, bf16[2,128,128]{2,1,0:T(8,128)(2,1)S(1)}, u32[]{:S(2)}, u32[]{:S(2)}) collective-permute-start(bf16[2,128,128]{2,1,0:T(8,128)(2,1)S(1)} %pad_maximum_fusion.refs_0_), channel_id=1, source_target_pairs={{0,4},{2,6},{4,0},{6,2},{8,12},{10,14},{12,8},{14,10},{1,5},{3,7},... | collective-permute-start | bytes 196616 | tf_op jit(solution)/shard_map/ppermute | solution.py:219
  30.0 5.4 %collective-permute-start.5 = (bf16[2,128,128]{2,1,0:T(8,128)(2,1)S(1)}, bf16[2,128,128]{2,1,0:T(8,128)(2,1)S(1)}, u32[]{:S(2)}, u32[]{:S(2)}) collective-permute-start(bf16[2,128,128]{2,1,0:T(8,128)(2,1)S(1)} %pad_maximum_fusion.refs_0_), channel_id=1, source_target_pairs={{0,8},{2,10},{4,12},{6,14},{8,0},{10,2},{12,4},{14,6},{1,9},{3,11}... | collective-permute-start | bytes 196616 | tf_op jit(solution)/shard_map/ppermute | solution.py:219
  38.3 1.3 %collective-permute-start.8 = (bf16[16,2048]{1,0:T(8,128)(2,1)S(1)}, bf16[16,2048]{1,0:T(8,128)(2,1)S(1)}, u32[]{:S(2)}, u32[]{:S(2)}) collective-permute-start(bf16[16,2048]{1,0:T(8,128)(2,1)S(1)} %bitcast.4), channel_id=1, source_target_pairs={{0,1},{1,0},{2,3},{3,2},{4,5},{5,4},{6,7},{7,6},{8,9},{9,8},{10,11... | collective-permute-start | bytes 196616 | tf_op jit(solution)/shard_map/ppermute | solution.py:332

commit v5 on v4

--- a/solution.py
+++ b/solution.py
@@ -12,10 +12,10 @@
 
 
 def project_kernel(
-    near, far, device_at, own, slab, head_dim, tokens_ref, wq_ref, wk_ref, wv_ref, keep_ref, *refs
+    low, high, device_at, own, slab, head_dim, tokens_ref, wq_ref, wk_ref, wv_ref, keep_ref, *refs
 ):
-    send_refs = refs[: near - 1]
-    t_buf, q_buf, k_buf, v_buf, partial, sems = refs[near - 1 :]
+    send_refs = refs[: low - 1]
+    t_buf, q_buf, k_buf, v_buf, partial, sems = refs[low - 1 :]
     rows, depth = tokens_ref.shape
     heads = q_buf.shape[1] // head_dim
     kv_heads = wk_ref.shape[1] // head_dim
@@ -34,19 +34,19 @@
     row = lax.broadcasted_iota(jnp.int32, (rows, rows), 0)
     column = lax.broadcasted_iota(jnp.int32, (rows, rows), 1)
     wanted = jnp.zeros((rows, rows), jnp.int32)
-    for p in range(near):
-        for q in range(far):
-            at = p * far + q
+    for p in range(low):
+        for q in range(high):
+            at = p * high + q
             wanted = jnp.where(row >= at * own, row + (device_at(p, q) - at) * own, wanted)
     pick = (column == wanted).astype(jnp.bfloat16)
     t_copy.wait()
     tokens = jnp.dot(pick, t_buf[...], preferred_element_type=jnp.float32).astype(jnp.bfloat16)
 
-    group = far * own
+    group = high * own
 
     def put(part, head):
         count = part.shape[1] // head_dim
-        for p in range(near):
+        for p in range(low):
             ref = send_refs[p - 1] if p else keep_ref
             tiles = [
                 part[p * group : (p + 1) * group, h * head_dim : (h + 1) * head_dim] for h in range(count)
@@ -75,12 +75,12 @@
                 put(part, first // head_dim)
 
 
-def partner(f, k, far):
-    return f ^ k if far & (far - 1) == 0 else (f + k) % far
-
-
-def source(f, k, far):
-    return f ^ k if far & (far - 1) == 0 else (f + far - k) % far
+def partner(f, k, count):
+    return f ^ k if count & (count - 1) == 0 else (f + k) % count
+
+
+def source(f, k, count):
+    return f ^ k if count & (count - 1) == 0 else (f + count - k) % count
 
 
 def combine_kernel(steps, heads, kv_heads, cache_ref, keep_ref, *refs):
@@ -157,21 +157,20 @@
     out_ref[...] = jnp.concatenate(mixed, axis=0).astype(jnp.bfloat16)
 
 
-def output_kernel(n, gy, order, w_ref, *refs):
-    far = len(order)
-    blocks = refs[:far]
-    own_ref, other_ref, wide, lhs = refs[far:]
-    near, per_dev, head_dim = blocks[0].shape
+def output_kernel(gy, order, w_ref, *refs):
+    low = len(order)
+    blocks = refs[:low]
+    own_ref, other_ref, wide, lhs = refs[low:]
+    high, per_dev, head_dim = blocks[0].shape
     heads = w_ref.shape[0] // head_dim
-    rows = n * per_dev // heads
+    rows = high * low * per_dev // heads
     out_cols = w_ref.shape[1]
     width = min(512, out_cols)
-    half = n // gy
+    half = high * low // gy
     me, me_gy = lax.axis_index("gx"), lax.axis_index("gy")
-    mine, mine_far = lax.rem(me, near), lax.div(me, near)
-    for k in range(far):
-        for j in range(near):
-            d = source(mine_far, order[k], far) * near + lax.rem(mine + near - j, near)
+    for k in range(low):
+        for j in range(high):
+            d = source(lax.div(me, low), j, high) * low + source(lax.rem(me, low), order[k], low)
             place = lax.rem(lax.div(d, half) + gy - me_gy, gy) * half + lax.rem(d, half)
             wide[pl.ds(pl.multiple_of(place * per_dev, per_dev), per_dev), :] = blocks[k][j].astype(jnp.float32)
     for h in range(heads):
@@ -205,40 +204,39 @@
     anywhere = pl.BlockSpec(memory_space=pl.ANY)
     block = own_rows * (heads + 2 * kv_heads)
 
-    near = 2 if n % 2 == 0 else 1
-    far = n // near
-    order_out = sorted(range(1, far), key=lambda k: -(k // 2))
-    order_back = sorted(range(1, far), key=lambda k: k % 2)
-
-    def to_near(x, j):
+    low = n
+    while low * low >= 4 * n and low % 2 == 0:
+        low //= 2
+    high = n // low
+    order = range(low - 1, 0, -1)
+
+    def to_low(x, k):
         return lax.ppermute(
-            x, "gx", [(f * near + i, f * near + (i + j) % near) for f in range(far) for i in range(near)]
-        )
-
-    def to_far(x, k):
+            x, "gx", [(h * low + i, h * low + int(partner(i, k, low))) for h in range(high) for i in range(low)]
+        )
+
+    def to_high(x, k):
         return lax.ppermute(
-            x, "gx", [(f * near + i, int(partner(f, k, far)) * near + i) for f in range(far) for i in range(near)]
+            x, "gx", [(h * low + i, int(partner(h, k, high)) * low + i) for h in range(high) for i in range(low)]
         )
 
     slab = 256 if depth % 256 == 0 else depth
 
-    def device_at(j, k):
+    def device_at(p, q):
         me = lax.axis_index("gx")
-        return partner(lax.div(me, near), k, far) * near + lax.rem(lax.rem(me, near) + j, near)
+        return partner(lax.div(me, low), q, high) * low + partner(lax.rem(me, low), p, low)
 
     all_heads = heads + 2 * kv_heads
     keep, *sends = pl.pallas_call(
-        functools.partial(
-            project_kernel, near, far, device_at, own_rows, slab, head_dim
-        ),
+        functools.partial(project_kernel, low, high, device_at, own_rows, slab, head_dim),
         out_shape=[
             jax.ShapeDtypeStruct(
-                (all_heads * far * own_rows, head_dim), jnp.bfloat16 if p else jnp.float32
+                (all_heads * high * own_rows, head_dim), jnp.bfloat16 if p else jnp.float32
             )
-            for p in range(near)
+            for p in range(low)
         ],
         in_specs=[anywhere, anywhere, anywhere, anywhere],
-        out_specs=[vmem] * near,
+        out_specs=[vmem] * low,
         scratch_shapes=[
             pltpu.VMEM((rows, depth), jnp.bfloat16),
             pltpu.VMEM((depth, q_cols), jnp.bfloat16),
@@ -256,23 +254,23 @@
         name="project",
     )(in_hbm(tokens), in_hbm(w_query), in_hbm(w_key), in_hbm(w_value))
 
-    received = [to_near(sends[p - 1], p) for p in range(1, near)]
+    received = [to_low(sends[p - 1], p) for p in order]
 
     summed = pl.pallas_call(
-        functools.partial(combine_kernel, far, heads, kv_heads),
+        functools.partial(combine_kernel, high, heads, kv_heads),
         out_shape=[
             jax.ShapeDtypeStruct((block, head_dim), jnp.bfloat16 if q else jnp.float32)
-            for q in range(far)
+            for q in range(high)
         ],
         in_specs=[vmem] * (2 + len(received)),
-        out_specs=[vmem] * far,
-        scratch_shapes=[pltpu.VMEM((all_heads * far * own_rows, head_dim), jnp.float32)],
+        out_specs=[vmem] * high,
+        scratch_shapes=[pltpu.VMEM((all_heads * high * own_rows, head_dim), jnp.float32)],
         compiler_params=pltpu.CompilerParams(vmem_limit_bytes=12 * MIB),
         cost_estimate=pl.CostEstimate(flops=0, bytes_accessed=16 * MIB, transcendentals=0),
         name="combine",
     )(in_vmem(value_cache), keep, *received)
 
-    parts = [summed[0]] + [to_far(summed[q], q) for q in order_out]
+    parts = [summed[0]] + [to_high(summed[q], q) for q in range(1, high)]
 
     half = head_dim // 2
     freqs = rope_base ** (-2.0 * jnp.arange(half).astype(jnp.float32) / (2.0 * half))
@@ -303,16 +301,16 @@
         name="attend",
     )(table, in_vmem(key_cache), in_vmem(value_cache), *parts)
 
-    pair = jnp.stack([mixed] + [to_near(mixed, j) for j in range(1, near)])
-    blocks = [pair] + [to_far(pair, k) for k in order_back]
+    column = jnp.stack([mixed] + [to_high(mixed, q) for q in range(1, high)])
+    blocks = [column] + [to_low(column, k) for k in order]
 
     own, other = pl.pallas_call(
-        functools.partial(output_kernel, n, gy, (0, *order_back)),
+        functools.partial(output_kernel, gy, (0, *order)),
         out_shape=(
             jax.ShapeDtypeStruct((rows // gy, out_cols), jnp.float32),
             jax.ShapeDtypeStruct((gy - 1, rows // gy, out_cols), jnp.bfloat16),
         ),
-        in_specs=[vmem] * (1 + far),
+        in_specs=[vmem] * (1 + low),
         out_specs=(vmem, vmem),
         scratch_shapes=[
             pltpu.VMEM((rows * heads, head_dim), jnp.float32),

time: 40.4 us -> 38.5 us (0.953)
  waiting for transfers between devices: 14.5 us -> 12.5 us
    ppermute x8, waiting for transfers between devices: 13.2 us -> 11.2 us  [the longest x6 6.84 us: to_low(): lax.ppermute(x, 'gx', [(h * low + i, h * low + int(partner(i, k, low))) f...]
  transfers between devices with their start and end apart: 9 -> 9, of which waited for: 7 -> 9; matrix products, arithmetic and copies ran while one was open for 1% -> 1% of each run, Pallas kernels for 0% -> 0%
where the time goes in v5:
time: 38.5 us; the launch traced here: 38.3 us
  starting transfers between devices  13.7 us (36%)
  waiting for transfers between devices  12.5 us (32%)
  Pallas kernels  11.2 us (29%)
  other arithmetic  0.85 us (2%)
    ppermute x6, starting transfers between devices, to_low(): lax.ppermute(x, 'gx', [(h * low + i, h * low + int(partner(i, k, low))) f...  8.25 us
    pallas_call x1, Pallas kernels, on_device(): pl.pallas_call(functools.partial(project_kernel, low, high, device_at, ow...  7.22 us
    ppermute x6, waiting for transfers between devices, to_low(): lax.ppermute(x, 'gx', [(h * low + i, h * low + int(partner(i, k, low))) f...  6.84 us
    ppermute x2, starting transfers between devices, to_high(): lax.ppermute(x, 'gx', [(h * low + i, int(partner(h, k, high)) * low + i)...  5.34 us
    ppermute x2, waiting for transfers between devices, to_high(): lax.ppermute(x, 'gx', [(h * low + i, int(partner(h, k, high)) * low + i)...  4.41 us
    pallas_call x1, Pallas kernels, on_device(): pl.pallas_call(functools.partial(output_kernel, gy, (0, *order)), out_sha...  2.87 us
    ppermute x1, waiting for transfers between devices, on_device(): lax.ppermute(other[j - 1], 'gy', [(i, (i + j) % gy) for i in range(gy)])  1.24 us
    pallas_call x1, Pallas kernels, on_device(): pl.pallas_call(attend_kernel, out_shape=jax.ShapeDtypeStruct((own_rows *...  1 us
  transfers between devices with their start and end apart: 9, of which 9 were waited for; matrix products, arithmetic and copies ran while one was open for 1% of the time, Pallas kernels for 0%

profile of v5, /device:TPU:0, one launch (start us, length us, event | category | flops | bytes accessed | tf_op | source)
XLA Modules:
  0.0 38.3 jit_solution(15361419386348078580)
XLA Ops:
  0.0 0.0 copy-start.3
  0.0 0.0 copy-start.1
  0.0 7.2 %project.1 = (f32[288,128]{1,0:T(8,128)S(1)}, bf16[288,128]{1,0:T(8,128)(2,1)S(1)}, bf16[288,128]{1,0:T(8,128)(2,1)S(1)}, bf16[288,128]{1,0:T(8,128)(2,1)S(1)}) custom-call(bf16[32,2048]{1,0:T(8,128)(2,1)} %tokens_ref.1, bf16[2048,4096]{1,0:T(8,128)(2,1)} %wq_ref.1, bf16[2048,256]{1,0:T(8,128)(2,1)} %wk_ref.1, bf16[2048,256]{1,0:T(8,128)(2,1)} %wv_ref.1), custom_call_target="tpu_custom_call" | custom-call | flops 603979776 | bytes 18874368 | tf_op jit(solution)/shard_map/project/pallas_call | solution.py:230
  7.2 4.1 %collective-permute-start = (bf16[288,128]{1,0:T(8,128)(2,1)S(1)}, bf16[288,128]{1,0:T(8,128)(2,1)S(1)}, u32[]{:S(2)}, u32[]{:S(2)}) collective-permute-start(bf16[288,128]{1,0:T(8,128)(2,1)S(1)} %get-tuple-element.14), channel_id=1, source_target_pairs={{0,6},{2,4},{4,2},{6,0},{8,14},{10,12},{12,10},{14,8},{1,7},{3,5},... | collective-permute-start | bytes 221192 | tf_op jit(solution)/shard_map/ppermute | solution.py:214
  11.3 0.5 %collective-permute-start.1 = (bf16[288,128]{1,0:T(8,128)(2,1)S(1)}, bf16[288,128]{1,0:T(8,128)(2,1)S(1)}, u32[]{:S(2)}, u32[]{:S(2)}) collective-permute-start(bf16[288,128]{1,0:T(8,128)(2,1)S(1)} %get-tuple-element.15), channel_id=1, source_target_pairs={{0,4},{2,6},{4,0},{6,2},{8,12},{10,14},{12,8},{14,10},{1,5},{3,7},... | collective-permute-start | bytes 221192 | tf_op jit(solution)/shard_map/ppermute | solution.py:214
  11.7 0.2 collective-permute-start.2
  11.9 0.0 copy-done.3
  12.0 0.1 multiply_cosine_fusion
  12.1 0.1 pad.6.clone
  12.1 1.8 %collective-permute-done.refs_0_ = bf16[288,128]{1,0:T(8,128)(2,1)S(1)} collective-permute-done((bf16[288,128]{1,0:T(8,128)(2,1)S(1)}, bf16[288,128]{1,0:T(8,128)(2,1)S(1)}, u32[]{:S(2)}, u32[]{:S(2)}) %collective-permute-start) | collective-permute-done | bytes 73760 | tf_op jit(solution)/shard_map/ppermute | solution.py:214
  13.9 1.7 %collective-permute-done.1.refs_1_ = bf16[288,128]{1,0:T(8,128)(2,1)S(1)} collective-permute-done((bf16[288,128]{1,0:T(8,128)(2,1)S(1)}, bf16[288,128]{1,0:T(8,128)(2,1)S(1)}, u32[]{:S(2)}, u32[]{:S(2)}) %collective-permute-start.1) | collective-permute-done | bytes 73760 | tf_op jit(solution)/shard_map/ppermute | solution.py:214
  15.7 0.4 %collective-permute-done.2.refs_2_ = bf16[288,128]{1,0:T(8,128)(2,1)S(1)} collective-permute-done((bf16[288,128]{1,0:T(8,128)(2,1)S(1)}, bf16[288,128]{1,0:T(8,128)(2,1)S(1)}, u32[]{:S(2)}, u32[]{:S(2)}) %collective-permute-start.2) | collective-permute-done | bytes 73760 | tf_op jit(solution)/shard_map/ppermute | solution.py:214
  16.1 0.0 copy-done.1
  16.1 0.1 combine.1
  16.2 2.7 %collective-permute-start.3 = (bf16[144,128]{1,0:T(8,128)(2,1)S(1)}, bf16[144,128]{1,0:T(8,128)(2,1)S(1)}, u32[]{:S(2)}, u32[]{:S(2)}) collective-permute-start(bf16[144,128]{1,0:T(8,128)(2,1)S(1)} %get-tuple-element.18), channel_id=1, source_target_pairs={{0,8},{2,10},{4,12},{6,14},{8,0},{10,2},{12,4},{14,6},{1,9},{3,11}... | collective-permute-start | bytes 110600 | tf_op jit(solution)/shard_map/ppermute | solution.py:219
  18.8 0.1 maximum_maximum_fusion.table_ref
  18.9 2.2 %collective-permute-done.3.refs_1_ = bf16[144,128]{1,0:T(8,128)(2,1)S(1)} collective-permute-done((bf16[144,128]{1,0:T(8,128)(2,1)S(1)}, bf16[144,128]{1,0:T(8,128)(2,1)S(1)}, u32[]{:S(2)}, u32[]{:S(2)}) %collective-permute-start.3) | collective-permute-done | bytes 36896 | tf_op jit(solution)/shard_map/ppermute | solution.py:219
  21.1 0.0 copy-done.2
  21.1 1.0 %attend.1 = bf16[128,128]{1,0:T(8,128)(2,1)S(1)} custom-call(f32[12,128]{1,0:T(8,128)S(1)} %maximum_maximum_fusion.table_ref, bf16[4,2,1024,128]{3,2,1,0:T(8,128)(2,1)S(1)} %copy-done.2, bf16[4,2,1024,128]{3,2,1,0:T(8,128)(2,1)S(1)} %copy-done.1, f32[144,128]{1,0:T(8,128)S(1)} %get-tuple-element.17.refs_0_, bf16[144,128]{1,0:T(8,128)(2,1)S(1)} %collective-permute-done.3.refs_1_), custom_call_target="tpu_custom_call" | custom-call | flops 67108864 | bytes 4194304 | tf_op jit(solution)/shard_map/attend/pallas_call | solution.py:290
  22.1 2.7 %collective-permute-start.4 = (bf16[128,128]{1,0:T(8,128)(2,1)S(1)}, bf16[128,128]{1,0:T(8,128)(2,1)S(1)}, u32[]{:S(2)}, u32[]{:S(2)}) collective-permute-start(bf16[128,128]{1,0:T(8,128)(2,1)S(1)} %attend.1), channel_id=1, source_target_pairs={{0,8},{2,10},{4,12},{6,14},{8,0},{10,2},{12,4},{14,6},{1,9},{3,11}... | collective-permute-start | bytes 98312 | tf_op jit(solution)/shard_map/ppermute | solution.py:219
  24.8 2.2 %collective-permute-done.4 = bf16[128,128]{1,0:T(8,128)(2,1)S(1)} collective-permute-done((bf16[128,128]{1,0:T(8,128)(2,1)S(1)}, bf16[128,128]{1,0:T(8,128)(2,1)S(1)}, u32[]{:S(2)}, u32[]{:S(2)}) %collective-permute-start.4) | collective-permute-done | bytes 32800 | tf_op jit(solution)/shard_map/ppermute | solution.py:219
  27.0 1.7 %collective-permute-start.5 = (bf16[2,128,128]{2,1,0:T(8,128)(2,1)S(1)}, bf16[2,128,128]{2,1,0:T(8,128)(2,1)S(1)}, u32[]{:S(2)}, u32[]{:S(2)}) collective-permute-start(bf16[2,128,128]{2,1,0:T(8,128)(2,1)S(1)} %pad_maximum_fusion.refs_0_), channel_id=1, source_target_pairs={{0,6},{2,4},{4,2},{6,0},{8,14},{10,12},{12,10},{14,8},{1,7},{3,5},... | collective-permute-start | bytes 196616 | tf_op jit(solution)/shard_map/ppermute | solution.py:214
  28.8 0.4 %collective-permute-start.6 = (bf16[2,128,128]{2,1,0:T(8,128)(2,1)S(1)}, bf16[2,128,128]{2,1,0:T(8,128)(2,1)S(1)}, u32[]{:S(2)}, u32[]{:S(2)}) collective-permute-start(bf16[2,128,128]{2,1,0:T(8,128)(2,1)S(1)} %pad_maximum_fusion.refs_0_), channel_id=1, source_target_pairs={{0,4},{2,6},{4,0},{6,2},{8,12},{10,14},{12,8},{14,10},{1,5},{3,7},... | collective-permute-start | bytes 196616 | tf_op jit(solution)/shard_map/ppermute | solution.py:214
  29.2 1.4 %collective-permute-start.7 = (bf16[2,128,128]{2,1,0:T(8,128)(2,1)S(1)}, bf16[2,128,128]{2,1,0:T(8,128)(2,1)S(1)}, u32[]{:S(2)}, u32[]{:S(2)}) collective-permute-start(bf16[2,128,128]{2,1,0:T(8,128)(2,1)S(1)} %pad_maximum_fusion.refs_0_), channel_id=1, source_target_pairs={{0,2},{2,0},{4,6},{6,4},{8,10},{10,8},{12,14},{14,12},{1,3},{3,1},... | collective-permute-start | bytes 196616 | tf_op jit(solution)/shard_map/ppermute | solution.py:214
  30.6 1.7 %collective-permute-done.5.refs_1_ = bf16[2,128,128]{2,1,0:T(8,128)(2,1)S(1)} collective-permute-done((bf16[2,128,128]{2,1,0:T(8,128)(2,1)S(1)}, bf16[2,128,128]{2,1,0:T(8,128)(2,1)S(1)}, u32[]{:S(2)}, u32[]{:S(2)}) %collective-permute-start.5) | collective-permute-done | bytes 65568 | tf_op jit(solution)/shard_map/ppermute | solution.py:214
  32.3 0.8 %collective-permute-done.6.refs_2_ = bf16[2,128,128]{2,1,0:T(8,128)(2,1)S(1)} collective-permute-done((bf16[2,128,128]{2,1,0:T(8,128)(2,1)S(1)}, bf16[2,128,128]{2,1,0:T(8,128)(2,1)S(1)}, u32[]{:S(2)}, u32[]{:S(2)}) %collective-permute-start.6) | collective-permute-done | bytes 65568 | tf_op jit(solution)/shard_map/ppermute | solution.py:214
  33.0 0.4 %collective-permute-done.7.refs_3_ = bf16[2,128,128]{2,1,0:T(8,128)(2,1)S(1)} collective-permute-done((bf16[2,128,128]{2,1,0:T(8,128)(2,1)S(1)}, bf16[2,128,128]{2,1,0:T(8,128)(2,1)S(1)}, u32[]{:S(2)}, u32[]{:S(2)}) %collective-permute-start.7) | collective-permute-done | bytes 65568 | tf_op jit(solution)/shard_map/ppermute | solution.py:214
  33.5 0.0 copy-done
  33.5 2.9 %output.1 = (f32[16,2048]{1,0:T(8,128)S(1)}, bf16[1,16,2048]{2,1,0:T(8,128)(2,1)S(1)}) custom-call(bf16[4096,2048]{1,0:T(8,128)(2,1)S(1)} %copy-done, bf16[2,128,128]{2,1,0:T(8,128)(2,1)S(1)} %pad_maximum_fusion.refs_0_, bf16[2,128,128]{2,1,0:T(8,128)(2,1)S(1)} %collective-permute-done.5.refs_1_, bf16[2,128,128]{2,1,0:T(8,128)(2,1)S(1)} %collective-permute-done.6.refs_2_, ...), custom_call_target="tpu_custom_call" | custom-call | flops 536870912 | bytes 16777216 | tf_op jit(solution)/shard_map/output/pallas_call | solution.py:307
  36.3 0.1 collective-permute-start.8
  36.4 1.2 %collective-permute-done.8 = bf16[16,2048]{1,0:T(8,128)(2,1)S(1)} collective-permute-done((bf16[16,2048]{1,0:T(8,128)(2,1)S(1)}, bf16[16,2048]{1,0:T(8,128)(2,1)S(1)}, u32[]{:S(2)}, u32[]{:S(2)}) %collective-permute-start.8) | collective-permute-done | bytes 65568 | tf_op jit(solution)/shard_map/ppermute | solution.py:330
  37.7 0.6 %add_convert_fusion = bf16[16,2048]{1,0:T(8,128)(2,1)} fusion(f32[16,2048]{1,0:T(8,128)S(1)} %get-tuple-element.19, bf16[16,2048]{1,0:T(8,128)(2,1)S(1)} %collective-permute-done.8), kind=kLoop, calls=%fused_computation | loop fusion | flops 98304 | bytes 262144 | tf_op jit(solution)/shard_map/convert_element_type | solution.py:332
  (5 shorter events, 0.0 us)
Async XLA Ops:
  0.0 12.0 %copy-start.3 = (s32[4]{0:T(128)S(1)}, s32[4]{0:T(128)}, u32[]{:S(2)}) copy-start(s32[4]{0:T(128)} %param.15) | copy-start | bytes 52
  0.0 16.1 %copy-start.1 = (bf16[4,2,1024,128]{3,2,1,0:T(8,128)(2,1)S(1)}, bf16[4,2,1024,128]{3,2,1,0:T(8,128)(2,1)}, u32[]{:S(2)}) copy-start(bf16[4,2,1024,128]{3,2,1,0:T(8,128)(2,1)} %values.1) | copy-start | bytes 6291460
  0.0 21.1 %copy-start.2 = (bf16[4,2,1024,128]{3,2,1,0:T(8,128)(2,1)S(1)}, bf16[4,2,1024,128]{3,2,1,0:T(8,128)(2,1)}, u32[]{:S(2)}) copy-start(bf16[4,2,1024,128]{3,2,1,0:T(8,128)(2,1)} %keys.1) | copy-start | bytes 6291460
  0.0 33.5 %copy-start = (bf16[4096,2048]{1,0:T(8,128)(2,1)S(1)}, bf16[4096,2048]{1,0:T(8,128)(2,1)}, u32[]{:S(2)}) copy-start(bf16[4096,2048]{1,0:T(8,128)(2,1)} %w_ref.1) | copy-start | bytes 50331652
  7.2 6.7 %collective-permute-start = (bf16[288,128]{1,0:T(8,128)(2,1)S(1)}, bf16[288,128]{1,0:T(8,128)(2,1)S(1)}, u32[]{:S(2)}, u32[]{:S(2)}) collective-permute-start(bf16[288,128]{1,0:T(8,128)(2,1)S(1)} %get-tuple-element.14), channel_id=1, source_target_pairs={{0,6},{2,4},{4,2},{6,0},{8,14},{10,12},{12,10},{14,8},{1,7},{3,5},... | collective-permute-start | bytes 221192 | tf_op jit(solution)/shard_map/ppermute | solution.py:214
  11.3 4.4 %collective-permute-start.1 = (bf16[288,128]{1,0:T(8,128)(2,1)S(1)}, bf16[288,128]{1,0:T(8,128)(2,1)S(1)}, u32[]{:S(2)}, u32[]{:S(2)}) collective-permute-start(bf16[288,128]{1,0:T(8,128)(2,1)S(1)} %get-tuple-element.15), channel_id=1, source_target_pairs={{0,4},{2,6},{4,0},{6,2},{8,12},{10,14},{12,8},{14,10},{1,5},{3,7},... | collective-permute-start | bytes 221192 | tf_op jit(solution)/shard_map/ppermute | solution.py:214
  11.7 4.4 %collective-permute-start.2 = (bf16[288,128]{1,0:T(8,128)(2,1)S(1)}, bf16[288,128]{1,0:T(8,128)(2,1)S(1)}, u32[]{:S(2)}, u32[]{:S(2)}) collective-permute-start(bf16[288,128]{1,0:T(8,128)(2,1)S(1)} %get-tuple-element.16), channel_id=1, source_target_pairs={{0,2},{2,0},{4,6},{6,4},{8,10},{10,8},{12,14},{14,12},{1,3},{3,1},... | collective-permute-start | bytes 221192 | tf_op jit(solution)/shard_map/ppermute | solution.py:214
  16.2 4.9 %collective-permute-start.3 = (bf16[144,128]{1,0:T(8,128)(2,1)S(1)}, bf16[144,128]{1,0:T(8,128)(2,1)S(1)}, u32[]{:S(2)}, u32[]{:S(2)}) collective-permute-start(bf16[144,128]{1,0:T(8,128)(2,1)S(1)} %get-tuple-element.18), channel_id=1, source_target_pairs={{0,8},{2,10},{4,12},{6,14},{8,0},{10,2},{12,4},{14,6},{1,9},{3,11}... | collective-permute-start | bytes 110600 | tf_op jit(solution)/shard_map/ppermute | solution.py:219
  22.1 4.9 %collective-permute-start.4 = (bf16[128,128]{1,0:T(8,128)(2,1)S(1)}, bf16[128,128]{1,0:T(8,128)(2,1)S(1)}, u32[]{:S(2)}, u32[]{:S(2)}) collective-permute-start(bf16[128,128]{1,0:T(8,128)(2,1)S(1)} %attend.1), channel_id=1, source_target_pairs={{0,8},{2,10},{4,12},{6,14},{8,0},{10,2},{12,4},{14,6},{1,9},{3,11}... | collective-permute-start | bytes 98312 | tf_op jit(solution)/shard_map/ppermute | solution.py:219
  27.0 5.2 %collective-permute-start.5 = (bf16[2,128,128]{2,1,0:T(8,128)(2,1)S(1)}, bf16[2,128,128]{2,1,0:T(8,128)(2,1)S(1)}, u32[]{:S(2)}, u32[]{:S(2)}) collective-permute-start(bf16[2,128,128]{2,1,0:T(8,128)(2,1)S(1)} %pad_maximum_fusion.refs_0_), channel_id=1, source_target_pairs={{0,6},{2,4},{4,2},{6,0},{8,14},{10,12},{12,10},{14,8},{1,7},{3,5},... | collective-permute-start | bytes 196616 | tf_op jit(solution)/shard_map/ppermute | solution.py:214
  28.8 4.3 %collective-permute-start.6 = (bf16[2,128,128]{2,1,0:T(8,128)(2,1)S(1)}, bf16[2,128,128]{2,1,0:T(8,128)(2,1)S(1)}, u32[]{:S(2)}, u32[]{:S(2)}) collective-permute-start(bf16[2,128,128]{2,1,0:T(8,128)(2,1)S(1)} %pad_maximum_fusion.refs_0_), channel_id=1, source_target_pairs={{0,4},{2,6},{4,0},{6,2},{8,12},{10,14},{12,8},{14,10},{1,5},{3,7},... | collective-permute-start | bytes 196616 | tf_op jit(solution)/shard_map/ppermute | solution.py:214
  29.2 4.3 %collective-permute-start.7 = (bf16[2,128,128]{2,1,0:T(8,128)(2,1)S(1)}, bf16[2,128,128]{2,1,0:T(8,128)(2,1)S(1)}, u32[]{:S(2)}, u32[]{:S(2)}) collective-permute-start(bf16[2,128,128]{2,1,0:T(8,128)(2,1)S(1)} %pad_maximum_fusion.refs_0_), channel_id=1, source_target_pairs={{0,2},{2,0},{4,6},{6,4},{8,10},{10,8},{12,14},{14,12},{1,3},{3,1},... | collective-permute-start | bytes 196616 | tf_op jit(solution)/shard_map/ppermute | solution.py:214
  36.3 1.3 %collective-permute-start.8 = (bf16[16,2048]{1,0:T(8,128)(2,1)S(1)}, bf16[16,2048]{1,0:T(8,128)(2,1)S(1)}, u32[]{:S(2)}, u32[]{:S(2)}) collective-permute-start(bf16[16,2048]{1,0:T(8,128)(2,1)S(1)} %bitcast.4), channel_id=1, source_target_pairs={{0,1},{1,0},{2,3},{3,2},{4,5},{5,4},{6,7},{7,6},{8,9},{9,8},{10,11... | collective-permute-start | bytes 196616 | tf_op jit(solution)/shard_map/ppermute | solution.py:330

commit v6 on v5

--- a/solution.py
+++ b/solution.py
@@ -157,6 +157,11 @@
     out_ref[...] = jnp.concatenate(mixed, axis=0).astype(jnp.bfloat16)
 
 
+def fill_rows(x):
+    rows = x.shape[0]
+    return jnp.concatenate([x] * (128 // rows), axis=0) if rows < 128 and 128 % rows == 0 else x
+
+
 def output_kernel(gy, order, w_ref, *refs):
     low = len(order)
     blocks = refs[:low]
@@ -175,9 +180,10 @@
             wide[pl.ds(pl.multiple_of(place * per_dev, per_dev), per_dev), :] = blocks[k][j].astype(jnp.float32)
     for h in range(heads):
         lhs[:, h * head_dim : (h + 1) * head_dim] = wide[pl.ds(h, rows, stride=heads), :].astype(lhs.dtype)
+    filled = fill_rows(lhs[...])
     for c in range(out_cols // width):
         part = jnp.dot(
-            lhs[...], w_ref[:, c * width : (c + 1) * width], preferred_element_type=jnp.float32
+            filled, w_ref[:, c * width : (c + 1) * width], preferred_element_type=jnp.float32
         )
         own_ref[:, c * width : (c + 1) * width] = part[: rows // gy]
         for j in range(1, gy):

time: 38.5 us -> 38 us (0.987)
  Pallas kernels: 11.2 us -> 10.7 us
    pallas_call x1, Pallas kernels: 2.87 us -> 2.43 us  [on_device(): pl.pallas_call(functools.partial(output_kernel, gy, (0, *order)), out_sha...]
where the time goes in v6:
time: 38 us; the launch traced here: 37.9 us
  starting transfers between devices  13.7 us (36%)
  waiting for transfers between devices  12.5 us (33%)
  Pallas kernels  10.7 us (28%)
  other arithmetic  0.85 us (2%)
    ppermute x6, starting transfers between devices, to_low(): lax.ppermute(x, 'gx', [(h * low + i, h * low + int(partner(i, k, low))) f...  8.25 us
    pallas_call x1, Pallas kernels, on_device(): pl.pallas_call(functools.partial(project_kernel, low, high, device_at, ow...  7.22 us
    ppermute x6, waiting for transfers between devices, to_low(): lax.ppermute(x, 'gx', [(h * low + i, h * low + int(partner(i, k, low))) f...  6.84 us
    ppermute x2, starting transfers between devices, to_high(): lax.ppermute(x, 'gx', [(h * low + i, int(partner(h, k, high)) * low + i)...  5.34 us
    ppermute x2, waiting for transfers between devices, to_high(): lax.ppermute(x, 'gx', [(h * low + i, int(partner(h, k, high)) * low + i)...  4.41 us
    pallas_call x1, Pallas kernels, on_device(): pl.pallas_call(functools.partial(output_kernel, gy, (0, *order)), out_sha...  2.43 us
    ppermute x1, waiting for transfers between devices, on_device(): lax.ppermute(other[j - 1], 'gy', [(i, (i + j) % gy) for i in range(gy)])  1.24 us
    pallas_call x1, Pallas kernels, on_device(): pl.pallas_call(attend_kernel, out_shape=jax.ShapeDtypeStruct((own_rows *...  1 us
  transfers between devices with their start and end apart: 9, of which 9 were waited for; matrix products, arithmetic and copies ran while one was open for 1% of the time, Pallas kernels for 0%

profile of v6, /device:TPU:0, one launch (start us, length us, event | category | flops | bytes accessed | tf_op | source)
XLA Modules:
  0.0 37.9 jit_solution(13955304726438503239)
XLA Ops:
  0.0 0.0 copy-start.3
  0.0 0.0 copy-start.1
  0.0 7.2 %project.1 = (f32[288,128]{1,0:T(8,128)S(1)}, bf16[288,128]{1,0:T(8,128)(2,1)S(1)}, bf16[288,128]{1,0:T(8,128)(2,1)S(1)}, bf16[288,128]{1,0:T(8,128)(2,1)S(1)}) custom-call(bf16[32,2048]{1,0:T(8,128)(2,1)} %tokens_ref.1, bf16[2048,4096]{1,0:T(8,128)(2,1)} %wq_ref.1, bf16[2048,256]{1,0:T(8,128)(2,1)} %wk_ref.1, bf16[2048,256]{1,0:T(8,128)(2,1)} %wv_ref.1), custom_call_target="tpu_custom_call" | custom-call | flops 603979776 | bytes 18874368 | tf_op jit(solution)/shard_map/project/pallas_call | solution.py:236
  7.2 4.1 %collective-permute-start = (bf16[288,128]{1,0:T(8,128)(2,1)S(1)}, bf16[288,128]{1,0:T(8,128)(2,1)S(1)}, u32[]{:S(2)}, u32[]{:S(2)}) collective-permute-start(bf16[288,128]{1,0:T(8,128)(2,1)S(1)} %get-tuple-element.14), channel_id=1, source_target_pairs={{0,6},{2,4},{4,2},{6,0},{8,14},{10,12},{12,10},{14,8},{1,7},{3,5},... | collective-permute-start | bytes 221192 | tf_op jit(solution)/shard_map/ppermute | solution.py:220
  11.3 0.5 %collective-permute-start.1 = (bf16[288,128]{1,0:T(8,128)(2,1)S(1)}, bf16[288,128]{1,0:T(8,128)(2,1)S(1)}, u32[]{:S(2)}, u32[]{:S(2)}) collective-permute-start(bf16[288,128]{1,0:T(8,128)(2,1)S(1)} %get-tuple-element.15), channel_id=1, source_target_pairs={{0,4},{2,6},{4,0},{6,2},{8,12},{10,14},{12,8},{14,10},{1,5},{3,7},... | collective-permute-start | bytes 221192 | tf_op jit(solution)/shard_map/ppermute | solution.py:220
  11.7 0.2 collective-permute-start.2
  11.9 0.0 copy-done.3
  12.0 0.1 multiply_cosine_fusion
  12.1 0.1 pad.6.clone
  12.1 1.8 %collective-permute-done.refs_0_ = bf16[288,128]{1,0:T(8,128)(2,1)S(1)} collective-permute-done((bf16[288,128]{1,0:T(8,128)(2,1)S(1)}, bf16[288,128]{1,0:T(8,128)(2,1)S(1)}, u32[]{:S(2)}, u32[]{:S(2)}) %collective-permute-start) | collective-permute-done | bytes 73760 | tf_op jit(solution)/shard_map/ppermute | solution.py:220
  13.9 1.7 %collective-permute-done.1.refs_1_ = bf16[288,128]{1,0:T(8,128)(2,1)S(1)} collective-permute-done((bf16[288,128]{1,0:T(8,128)(2,1)S(1)}, bf16[288,128]{1,0:T(8,128)(2,1)S(1)}, u32[]{:S(2)}, u32[]{:S(2)}) %collective-permute-start.1) | collective-permute-done | bytes 73760 | tf_op jit(solution)/shard_map/ppermute | solution.py:220
  15.7 0.4 %collective-permute-done.2.refs_2_ = bf16[288,128]{1,0:T(8,128)(2,1)S(1)} collective-permute-done((bf16[288,128]{1,0:T(8,128)(2,1)S(1)}, bf16[288,128]{1,0:T(8,128)(2,1)S(1)}, u32[]{:S(2)}, u32[]{:S(2)}) %collective-permute-start.2) | collective-permute-done | bytes 73760 | tf_op jit(solution)/shard_map/ppermute | solution.py:220
  16.1 0.0 copy-done.1
  16.1 0.1 combine.1
  16.2 2.7 %collective-permute-start.3 = (bf16[144,128]{1,0:T(8,128)(2,1)S(1)}, bf16[144,128]{1,0:T(8,128)(2,1)S(1)}, u32[]{:S(2)}, u32[]{:S(2)}) collective-permute-start(bf16[144,128]{1,0:T(8,128)(2,1)S(1)} %get-tuple-element.18), channel_id=1, source_target_pairs={{0,8},{2,10},{4,12},{6,14},{8,0},{10,2},{12,4},{14,6},{1,9},{3,11}... | collective-permute-start | bytes 110600 | tf_op jit(solution)/shard_map/ppermute | solution.py:225
  18.8 0.1 maximum_maximum_fusion.table_ref
  18.9 2.2 %collective-permute-done.3.refs_1_ = bf16[144,128]{1,0:T(8,128)(2,1)S(1)} collective-permute-done((bf16[144,128]{1,0:T(8,128)(2,1)S(1)}, bf16[144,128]{1,0:T(8,128)(2,1)S(1)}, u32[]{:S(2)}, u32[]{:S(2)}) %collective-permute-start.3) | collective-permute-done | bytes 36896 | tf_op jit(solution)/shard_map/ppermute | solution.py:225
  21.1 0.0 copy-done.2
  21.1 1.0 %attend.1 = bf16[128,128]{1,0:T(8,128)(2,1)S(1)} custom-call(f32[12,128]{1,0:T(8,128)S(1)} %maximum_maximum_fusion.table_ref, bf16[4,2,1024,128]{3,2,1,0:T(8,128)(2,1)S(1)} %copy-done.2, bf16[4,2,1024,128]{3,2,1,0:T(8,128)(2,1)S(1)} %copy-done.1, f32[144,128]{1,0:T(8,128)S(1)} %get-tuple-element.17.refs_0_, bf16[144,128]{1,0:T(8,128)(2,1)S(1)} %collective-permute-done.3.refs_1_), custom_call_target="tpu_custom_call" | custom-call | flops 67108864 | bytes 4194304 | tf_op jit(solution)/shard_map/attend/pallas_call | solution.py:296
  22.1 2.7 %collective-permute-start.4 = (bf16[128,128]{1,0:T(8,128)(2,1)S(1)}, bf16[128,128]{1,0:T(8,128)(2,1)S(1)}, u32[]{:S(2)}, u32[]{:S(2)}) collective-permute-start(bf16[128,128]{1,0:T(8,128)(2,1)S(1)} %attend.1), channel_id=1, source_target_pairs={{0,8},{2,10},{4,12},{6,14},{8,0},{10,2},{12,4},{14,6},{1,9},{3,11}... | collective-permute-start | bytes 98312 | tf_op jit(solution)/shard_map/ppermute | solution.py:225
  24.8 2.2 %collective-permute-done.4 = bf16[128,128]{1,0:T(8,128)(2,1)S(1)} collective-permute-done((bf16[128,128]{1,0:T(8,128)(2,1)S(1)}, bf16[128,128]{1,0:T(8,128)(2,1)S(1)}, u32[]{:S(2)}, u32[]{:S(2)}) %collective-permute-start.4) | collective-permute-done | bytes 32800 | tf_op jit(solution)/shard_map/ppermute | solution.py:225
  27.0 1.7 %collective-permute-start.5 = (bf16[2,128,128]{2,1,0:T(8,128)(2,1)S(1)}, bf16[2,128,128]{2,1,0:T(8,128)(2,1)S(1)}, u32[]{:S(2)}, u32[]{:S(2)}) collective-permute-start(bf16[2,128,128]{2,1,0:T(8,128)(2,1)S(1)} %pad_maximum_fusion.refs_0_), channel_id=1, source_target_pairs={{0,6},{2,4},{4,2},{6,0},{8,14},{10,12},{12,10},{14,8},{1,7},{3,5},... | collective-permute-start | bytes 196616 | tf_op jit(solution)/shard_map/ppermute | solution.py:220
  28.8 0.4 %collective-permute-start.6 = (bf16[2,128,128]{2,1,0:T(8,128)(2,1)S(1)}, bf16[2,128,128]{2,1,0:T(8,128)(2,1)S(1)}, u32[]{:S(2)}, u32[]{:S(2)}) collective-permute-start(bf16[2,128,128]{2,1,0:T(8,128)(2,1)S(1)} %pad_maximum_fusion.refs_0_), channel_id=1, source_target_pairs={{0,4},{2,6},{4,0},{6,2},{8,12},{10,14},{12,8},{14,10},{1,5},{3,7},... | collective-permute-start | bytes 196616 | tf_op jit(solution)/shard_map/ppermute | solution.py:220
  29.2 1.4 %collective-permute-start.7 = (bf16[2,128,128]{2,1,0:T(8,128)(2,1)S(1)}, bf16[2,128,128]{2,1,0:T(8,128)(2,1)S(1)}, u32[]{:S(2)}, u32[]{:S(2)}) collective-permute-start(bf16[2,128,128]{2,1,0:T(8,128)(2,1)S(1)} %pad_maximum_fusion.refs_0_), channel_id=1, source_target_pairs={{0,2},{2,0},{4,6},{6,4},{8,10},{10,8},{12,14},{14,12},{1,3},{3,1},... | collective-permute-start | bytes 196616 | tf_op jit(solution)/shard_map/ppermute | solution.py:220
  30.6 1.7 %collective-permute-done.5.refs_1_ = bf16[2,128,128]{2,1,0:T(8,128)(2,1)S(1)} collective-permute-done((bf16[2,128,128]{2,1,0:T(8,128)(2,1)S(1)}, bf16[2,128,128]{2,1,0:T(8,128)(2,1)S(1)}, u32[]{:S(2)}, u32[]{:S(2)}) %collective-permute-start.5) | collective-permute-done | bytes 65568 | tf_op jit(solution)/shard_map/ppermute | solution.py:220
  32.3 0.8 %collective-permute-done.6.refs_2_ = bf16[2,128,128]{2,1,0:T(8,128)(2,1)S(1)} collective-permute-done((bf16[2,128,128]{2,1,0:T(8,128)(2,1)S(1)}, bf16[2,128,128]{2,1,0:T(8,128)(2,1)S(1)}, u32[]{:S(2)}, u32[]{:S(2)}) %collective-permute-start.6) | collective-permute-done | bytes 65568 | tf_op jit(solution)/shard_map/ppermute | solution.py:220
  33.0 0.4 %collective-permute-done.7.refs_3_ = bf16[2,128,128]{2,1,0:T(8,128)(2,1)S(1)} collective-permute-done((bf16[2,128,128]{2,1,0:T(8,128)(2,1)S(1)}, bf16[2,128,128]{2,1,0:T(8,128)(2,1)S(1)}, u32[]{:S(2)}, u32[]{:S(2)}) %collective-permute-start.7) | collective-permute-done | bytes 65568 | tf_op jit(solution)/shard_map/ppermute | solution.py:220
  33.5 0.0 copy-done
  33.5 2.4 %output.1 = (f32[16,2048]{1,0:T(8,128)S(1)}, bf16[1,16,2048]{2,1,0:T(8,128)(2,1)S(1)}) custom-call(bf16[4096,2048]{1,0:T(8,128)(2,1)S(1)} %copy-done, bf16[2,128,128]{2,1,0:T(8,128)(2,1)S(1)} %pad_maximum_fusion.refs_0_, bf16[2,128,128]{2,1,0:T(8,128)(2,1)S(1)} %collective-permute-done.5.refs_1_, bf16[2,128,128]{2,1,0:T(8,128)(2,1)S(1)} %collective-permute-done.6.refs_2_, ...), custom_call_target="tpu_custom_call" | custom-call | flops 536870912 | bytes 16777216 | tf_op jit(solution)/shard_map/output/pallas_call | solution.py:313
  35.9 0.1 collective-permute-start.8
  36.0 1.2 %collective-permute-done.8 = bf16[16,2048]{1,0:T(8,128)(2,1)S(1)} collective-permute-done((bf16[16,2048]{1,0:T(8,128)(2,1)S(1)}, bf16[16,2048]{1,0:T(8,128)(2,1)S(1)}, u32[]{:S(2)}, u32[]{:S(2)}) %collective-permute-start.8) | collective-permute-done | bytes 65568 | tf_op jit(solution)/shard_map/ppermute | solution.py:336
  37.2 0.6 %add_convert_fusion = bf16[16,2048]{1,0:T(8,128)(2,1)} fusion(f32[16,2048]{1,0:T(8,128)S(1)} %get-tuple-element.19, bf16[16,2048]{1,0:T(8,128)(2,1)S(1)} %collective-permute-done.8), kind=kLoop, calls=%fused_computation | loop fusion | flops 98304 | bytes 262144 | tf_op jit(solution)/shard_map/convert_element_type | solution.py:338
  (5 shorter events, 0.0 us)
Async XLA Ops:
  0.0 12.0 %copy-start.3 = (s32[4]{0:T(128)S(1)}, s32[4]{0:T(128)}, u32[]{:S(2)}) copy-start(s32[4]{0:T(128)} %param.15) | copy-start | bytes 52
  0.0 16.1 %copy-start.1 = (bf16[4,2,1024,128]{3,2,1,0:T(8,128)(2,1)S(1)}, bf16[4,2,1024,128]{3,2,1,0:T(8,128)(2,1)}, u32[]{:S(2)}) copy-start(bf16[4,2,1024,128]{3,2,1,0:T(8,128)(2,1)} %values.1) | copy-start | bytes 6291460
  0.0 21.1 %copy-start.2 = (bf16[4,2,1024,128]{3,2,1,0:T(8,128)(2,1)S(1)}, bf16[4,2,1024,128]{3,2,1,0:T(8,128)(2,1)}, u32[]{:S(2)}) copy-start(bf16[4,2,1024,128]{3,2,1,0:T(8,128)(2,1)} %keys.1) | copy-start | bytes 6291460
  0.0 33.5 %copy-start = (bf16[4096,2048]{1,0:T(8,128)(2,1)S(1)}, bf16[4096,2048]{1,0:T(8,128)(2,1)}, u32[]{:S(2)}) copy-start(bf16[4096,2048]{1,0:T(8,128)(2,1)} %w_ref.1) | copy-start | bytes 50331652
  7.2 6.7 %collective-permute-start = (bf16[288,128]{1,0:T(8,128)(2,1)S(1)}, bf16[288,128]{1,0:T(8,128)(2,1)S(1)}, u32[]{:S(2)}, u32[]{:S(2)}) collective-permute-start(bf16[288,128]{1,0:T(8,128)(2,1)S(1)} %get-tuple-element.14), channel_id=1, source_target_pairs={{0,6},{2,4},{4,2},{6,0},{8,14},{10,12},{12,10},{14,8},{1,7},{3,5},... | collective-permute-start | bytes 221192 | tf_op jit(solution)/shard_map/ppermute | solution.py:220
  11.3 4.4 %collective-permute-start.1 = (bf16[288,128]{1,0:T(8,128)(2,1)S(1)}, bf16[288,128]{1,0:T(8,128)(2,1)S(1)}, u32[]{:S(2)}, u32[]{:S(2)}) collective-permute-start(bf16[288,128]{1,0:T(8,128)(2,1)S(1)} %get-tuple-element.15), channel_id=1, source_target_pairs={{0,4},{2,6},{4,0},{6,2},{8,12},{10,14},{12,8},{14,10},{1,5},{3,7},... | collective-permute-start | bytes 221192 | tf_op jit(solution)/shard_map/ppermute | solution.py:220
  11.7 4.4 %collective-permute-start.2 = (bf16[288,128]{1,0:T(8,128)(2,1)S(1)}, bf16[288,128]{1,0:T(8,128)(2,1)S(1)}, u32[]{:S(2)}, u32[]{:S(2)}) collective-permute-start(bf16[288,128]{1,0:T(8,128)(2,1)S(1)} %get-tuple-element.16), channel_id=1, source_target_pairs={{0,2},{2,0},{4,6},{6,4},{8,10},{10,8},{12,14},{14,12},{1,3},{3,1},... | collective-permute-start | bytes 221192 | tf_op jit(solution)/shard_map/ppermute | solution.py:220
  16.2 4.9 %collective-permute-start.3 = (bf16[144,128]{1,0:T(8,128)(2,1)S(1)}, bf16[144,128]{1,0:T(8,128)(2,1)S(1)}, u32[]{:S(2)}, u32[]{:S(2)}) collective-permute-start(bf16[144,128]{1,0:T(8,128)(2,1)S(1)} %get-tuple-element.18), channel_id=1, source_target_pairs={{0,8},{2,10},{4,12},{6,14},{8,0},{10,2},{12,4},{14,6},{1,9},{3,11}... | collective-permute-start | bytes 110600 | tf_op jit(solution)/shard_map/ppermute | solution.py:225
  22.1 4.9 %collective-permute-start.4 = (bf16[128,128]{1,0:T(8,128)(2,1)S(1)}, bf16[128,128]{1,0:T(8,128)(2,1)S(1)}, u32[]{:S(2)}, u32[]{:S(2)}) collective-permute-start(bf16[128,128]{1,0:T(8,128)(2,1)S(1)} %attend.1), channel_id=1, source_target_pairs={{0,8},{2,10},{4,12},{6,14},{8,0},{10,2},{12,4},{14,6},{1,9},{3,11}... | collective-permute-start | bytes 98312 | tf_op jit(solution)/shard_map/ppermute | solution.py:225
  27.0 5.2 %collective-permute-start.5 = (bf16[2,128,128]{2,1,0:T(8,128)(2,1)S(1)}, bf16[2,128,128]{2,1,0:T(8,128)(2,1)S(1)}, u32[]{:S(2)}, u32[]{:S(2)}) collective-permute-start(bf16[2,128,128]{2,1,0:T(8,128)(2,1)S(1)} %pad_maximum_fusion.refs_0_), channel_id=1, source_target_pairs={{0,6},{2,4},{4,2},{6,0},{8,14},{10,12},{12,10},{14,8},{1,7},{3,5},... | collective-permute-start | bytes 196616 | tf_op jit(solution)/shard_map/ppermute | solution.py:220
  28.8 4.3 %collective-permute-start.6 = (bf16[2,128,128]{2,1,0:T(8,128)(2,1)S(1)}, bf16[2,128,128]{2,1,0:T(8,128)(2,1)S(1)}, u32[]{:S(2)}, u32[]{:S(2)}) collective-permute-start(bf16[2,128,128]{2,1,0:T(8,128)(2,1)S(1)} %pad_maximum_fusion.refs_0_), channel_id=1, source_target_pairs={{0,4},{2,6},{4,0},{6,2},{8,12},{10,14},{12,8},{14,10},{1,5},{3,7},... | collective-permute-start | bytes 196616 | tf_op jit(solution)/shard_map/ppermute | solution.py:220
  29.2 4.3 %collective-permute-start.7 = (bf16[2,128,128]{2,1,0:T(8,128)(2,1)S(1)}, bf16[2,128,128]{2,1,0:T(8,128)(2,1)S(1)}, u32[]{:S(2)}, u32[]{:S(2)}) collective-permute-start(bf16[2,128,128]{2,1,0:T(8,128)(2,1)S(1)} %pad_maximum_fusion.refs_0_), channel_id=1, source_target_pairs={{0,2},{2,0},{4,6},{6,4},{8,10},{10,8},{12,14},{14,12},{1,3},{3,1},... | collective-permute-start | bytes 196616 | tf_op jit(solution)/shard_map/ppermute | solution.py:220
  35.9 1.3 %collective-permute-start.8 = (bf16[16,2048]{1,0:T(8,128)(2,1)S(1)}, bf16[16,2048]{1,0:T(8,128)(2,1)S(1)}, u32[]{:S(2)}, u32[]{:S(2)}) collective-permute-start(bf16[16,2048]{1,0:T(8,128)(2,1)S(1)} %bitcast.4), channel_id=1, source_target_pairs={{0,1},{1,0},{2,3},{3,2},{4,5},{5,4},{6,7},{7,6},{8,9},{9,8},{10,11... | collective-permute-start | bytes 196616 | tf_op jit(solution)/shard_map/ppermute | solution.py:336

commit v7 on v6

--- a/solution.py
+++ b/solution.py
@@ -88,7 +88,7 @@
     total = keep_ref[...]
     for part in received:
         total = total + part[...].astype(jnp.float32)
-    total_ref[...] = total
+    total_ref[: total.shape[0], :] = total
     own = outs[0].shape[0] // (heads + 2 * kv_heads)
     group = steps * own
 
@@ -113,9 +113,10 @@
     total = parts[0][...].astype(jnp.float32)
     for part in parts[1:]:
         total = total + part[...].astype(jnp.float32)
-    cosine = table_ref[:rows]
-    sine = table_ref[rows : 2 * rows]
-    filled = table_ref[2 * rows :]
+    tile = table_ref.shape[0] // 3
+    cosine = table_ref[:tile][:rows]
+    sine = table_ref[tile : 2 * tile][:rows]
+    filled = table_ref[2 * tile :][:rows]
 
     def rotated(vectors, count):
         per_row = (rows, count, head_dim)
@@ -270,7 +271,7 @@
         ],
         in_specs=[vmem] * (2 + len(received)),
         out_specs=[vmem] * high,
-        scratch_shapes=[pltpu.VMEM((all_heads * high * own_rows, head_dim), jnp.float32)],
+        scratch_shapes=[pltpu.VMEM(((all_heads + 8) * high * own_rows, head_dim), jnp.float32)],
         compiler_params=pltpu.CompilerParams(vmem_limit_bytes=12 * MIB),
         cost_estimate=pl.CostEstimate(flops=0, bytes_accessed=16 * MIB, transcendentals=0),
         name="combine",
@@ -280,7 +281,7 @@
 
     half = head_dim // 2
     freqs = rope_base ** (-2.0 * jnp.arange(half).astype(jnp.float32) / (2.0 * half))
-    positions = lengths.astype(jnp.float32)[:, None]
+    positions = jnp.pad(lengths.astype(jnp.float32), (0, -own_rows % 8))[:, None]
     angles = positions * freqs[None, :]
     cosine = jnp.cos(angles)
     sine = jnp.sin(angles)
@@ -288,7 +289,7 @@
         [
             jnp.concatenate([cosine, cosine], axis=1),
             jnp.concatenate([-sine, sine], axis=1),
-            jnp.broadcast_to(positions, (own_rows, head_dim)),
+            jnp.broadcast_to(positions, (positions.shape[0], head_dim)),
         ],
         axis=0,
     )
@@ -319,7 +320,7 @@
         in_specs=[vmem] * (1 + low),
         out_specs=(vmem, vmem),
         scratch_shapes=[
-            pltpu.VMEM((rows * heads, head_dim), jnp.float32),
+            pltpu.VMEM(((rows + 1) * heads, head_dim), jnp.float32),
             pltpu.VMEM((rows, q_cols), jnp.bfloat16),
         ],
         compiler_params=pltpu.CompilerParams(vmem_limit_bytes=12 * MIB),

time: 38 us -> 38 us (level)
  no operation moved by 1% of the time
where the time goes in v7:
time: 38 us; the launch traced here: 37.9 us
  starting transfers between devices  13.7 us (36%)
  waiting for transfers between devices  12.5 us (33%)
  Pallas kernels  10.7 us (28%)
  other arithmetic  0.84 us (2%)
    ppermute x6, starting transfers between devices, to_low(): lax.ppermute(x, 'gx', [(h * low + i, h * low + int(partner(i, k, low))) f...  8.25 us
    pallas_call x1, Pallas kernels, on_device(): pl.pallas_call(functools.partial(project_kernel, low, high, device_at, ow...  7.22 us
    ppermute x6, waiting for transfers between devices, to_low(): lax.ppermute(x, 'gx', [(h * low + i, h * low + int(partner(i, k, low))) f...  6.83 us
    ppermute x2, starting transfers between devices, to_high(): lax.ppermute(x, 'gx', [(h * low + i, int(partner(h, k, high)) * low + i)...  5.34 us
    ppermute x2, waiting for transfers between devices, to_high(): lax.ppermute(x, 'gx', [(h * low + i, int(partner(h, k, high)) * low + i)...  4.42 us
    pallas_call x1, Pallas kernels, on_device(): pl.pallas_call(functools.partial(output_kernel, gy, (0, *order)), out_sha...  2.43 us
    ppermute x1, waiting for transfers between devices, on_device(): lax.ppermute(other[j - 1], 'gy', [(i, (i + j) % gy) for i in range(gy)])  1.24 us
    pallas_call x1, Pallas kernels, on_device(): pl.pallas_call(attend_kernel, out_shape=jax.ShapeDtypeStruct((own_rows *...  1 us
  transfers between devices with their start and end apart: 9, of which 9 were waited for; matrix products, arithmetic and copies ran while one was open for 1% of the time, Pallas kernels for 0%

profile of v7, /device:TPU:0, one launch (start us, length us, event | category | flops | bytes accessed | tf_op | source)
XLA Modules:
  0.0 37.9 jit_solution(5357263655899513943)
XLA Ops:
  0.0 0.0 copy-start.3
  0.0 0.0 copy-start.1
  0.0 7.2 %project.1 = (f32[288,128]{1,0:T(8,128)S(1)}, bf16[288,128]{1,0:T(8,128)(2,1)S(1)}, bf16[288,128]{1,0:T(8,128)(2,1)S(1)}, bf16[288,128]{1,0:T(8,128)(2,1)S(1)}) custom-call(bf16[32,2048]{1,0:T(8,128)(2,1)} %tokens_ref.1, bf16[2048,4096]{1,0:T(8,128)(2,1)} %wq_ref.1, bf16[2048,256]{1,0:T(8,128)(2,1)} %wk_ref.1, bf16[2048,256]{1,0:T(8,128)(2,1)} %wv_ref.1), custom_call_target="tpu_custom_call" | custom-call | flops 603979776 | bytes 18874368 | tf_op jit(solution)/shard_map/project/pallas_call | solution.py:237
  7.2 4.1 %collective-permute-start = (bf16[288,128]{1,0:T(8,128)(2,1)S(1)}, bf16[288,128]{1,0:T(8,128)(2,1)S(1)}, u32[]{:S(2)}, u32[]{:S(2)}) collective-permute-start(bf16[288,128]{1,0:T(8,128)(2,1)S(1)} %get-tuple-element.14), channel_id=1, source_target_pairs={{0,6},{2,4},{4,2},{6,0},{8,14},{10,12},{12,10},{14,8},{1,7},{3,5},... | collective-permute-start | bytes 221192 | tf_op jit(solution)/shard_map/ppermute | solution.py:221
  11.3 0.5 %collective-permute-start.1 = (bf16[288,128]{1,0:T(8,128)(2,1)S(1)}, bf16[288,128]{1,0:T(8,128)(2,1)S(1)}, u32[]{:S(2)}, u32[]{:S(2)}) collective-permute-start(bf16[288,128]{1,0:T(8,128)(2,1)S(1)} %get-tuple-element.15), channel_id=1, source_target_pairs={{0,4},{2,6},{4,0},{6,2},{8,12},{10,14},{12,8},{14,10},{1,5},{3,7},... | collective-permute-start | bytes 221192 | tf_op jit(solution)/shard_map/ppermute | solution.py:221
  11.7 0.2 collective-permute-start.2
  11.9 0.0 copy-done.3
  12.0 0.1 multiply_cosine_fusion
  12.1 0.1 pad.11.clone
  12.2 1.8 %collective-permute-done.refs_0_ = bf16[288,128]{1,0:T(8,128)(2,1)S(1)} collective-permute-done((bf16[288,128]{1,0:T(8,128)(2,1)S(1)}, bf16[288,128]{1,0:T(8,128)(2,1)S(1)}, u32[]{:S(2)}, u32[]{:S(2)}) %collective-permute-start) | collective-permute-done | bytes 73760 | tf_op jit(solution)/shard_map/ppermute | solution.py:221
  13.9 1.7 %collective-permute-done.1.refs_1_ = bf16[288,128]{1,0:T(8,128)(2,1)S(1)} collective-permute-done((bf16[288,128]{1,0:T(8,128)(2,1)S(1)}, bf16[288,128]{1,0:T(8,128)(2,1)S(1)}, u32[]{:S(2)}, u32[]{:S(2)}) %collective-permute-start.1) | collective-permute-done | bytes 73760 | tf_op jit(solution)/shard_map/ppermute | solution.py:221
  15.7 0.4 %collective-permute-done.2.refs_2_ = bf16[288,128]{1,0:T(8,128)(2,1)S(1)} collective-permute-done((bf16[288,128]{1,0:T(8,128)(2,1)S(1)}, bf16[288,128]{1,0:T(8,128)(2,1)S(1)}, u32[]{:S(2)}, u32[]{:S(2)}) %collective-permute-start.2) | collective-permute-done | bytes 73760 | tf_op jit(solution)/shard_map/ppermute | solution.py:221
  16.1 0.0 copy-done.1
  16.1 0.1 combine.1
  16.2 2.7 %collective-permute-start.3 = (bf16[144,128]{1,0:T(8,128)(2,1)S(1)}, bf16[144,128]{1,0:T(8,128)(2,1)S(1)}, u32[]{:S(2)}, u32[]{:S(2)}) collective-permute-start(bf16[144,128]{1,0:T(8,128)(2,1)S(1)} %get-tuple-element.18), channel_id=1, source_target_pairs={{0,8},{2,10},{4,12},{6,14},{8,0},{10,2},{12,4},{14,6},{1,9},{3,11}... | collective-permute-start | bytes 110600 | tf_op jit(solution)/shard_map/ppermute | solution.py:226
  18.8 0.1 maximum_maximum_fusion.table_ref
  18.9 2.2 %collective-permute-done.3.refs_1_ = bf16[144,128]{1,0:T(8,128)(2,1)S(1)} collective-permute-done((bf16[144,128]{1,0:T(8,128)(2,1)S(1)}, bf16[144,128]{1,0:T(8,128)(2,1)S(1)}, u32[]{:S(2)}, u32[]{:S(2)}) %collective-permute-start.3) | collective-permute-done | bytes 36896 | tf_op jit(solution)/shard_map/ppermute | solution.py:226
  21.1 0.0 copy-done.2
  21.1 1.0 %attend.1 = bf16[128,128]{1,0:T(8,128)(2,1)S(1)} custom-call(f32[24,128]{1,0:T(8,128)S(1)} %maximum_maximum_fusion.table_ref, bf16[4,2,1024,128]{3,2,1,0:T(8,128)(2,1)S(1)} %copy-done.2, bf16[4,2,1024,128]{3,2,1,0:T(8,128)(2,1)S(1)} %copy-done.1, f32[144,128]{1,0:T(8,128)S(1)} %get-tuple-element.17.refs_0_, bf16[144,128]{1,0:T(8,128)(2,1)S(1)} %collective-permute-done.3.refs_1_), custom_call_target="tpu_custom_call" | custom-call | flops 67108864 | bytes 4194304 | tf_op jit(solution)/shard_map/attend/pallas_call | solution.py:297
  22.1 2.7 %collective-permute-start.4 = (bf16[128,128]{1,0:T(8,128)(2,1)S(1)}, bf16[128,128]{1,0:T(8,128)(2,1)S(1)}, u32[]{:S(2)}, u32[]{:S(2)}) collective-permute-start(bf16[128,128]{1,0:T(8,128)(2,1)S(1)} %attend.1), channel_id=1, source_target_pairs={{0,8},{2,10},{4,12},{6,14},{8,0},{10,2},{12,4},{14,6},{1,9},{3,11}... | collective-permute-start | bytes 98312 | tf_op jit(solution)/shard_map/ppermute | solution.py:226
  24.8 2.2 %collective-permute-done.4 = bf16[128,128]{1,0:T(8,128)(2,1)S(1)} collective-permute-done((bf16[128,128]{1,0:T(8,128)(2,1)S(1)}, bf16[128,128]{1,0:T(8,128)(2,1)S(1)}, u32[]{:S(2)}, u32[]{:S(2)}) %collective-permute-start.4) | collective-permute-done | bytes 32800 | tf_op jit(solution)/shard_map/ppermute | solution.py:226
  27.0 1.7 %collective-permute-start.5 = (bf16[2,128,128]{2,1,0:T(8,128)(2,1)S(1)}, bf16[2,128,128]{2,1,0:T(8,128)(2,1)S(1)}, u32[]{:S(2)}, u32[]{:S(2)}) collective-permute-start(bf16[2,128,128]{2,1,0:T(8,128)(2,1)S(1)} %pad_maximum_fusion.refs_0_), channel_id=1, source_target_pairs={{0,6},{2,4},{4,2},{6,0},{8,14},{10,12},{12,10},{14,8},{1,7},{3,5},... | collective-permute-start | bytes 196616 | tf_op jit(solution)/shard_map/ppermute | solution.py:221
  28.8 0.4 %collective-permute-start.6 = (bf16[2,128,128]{2,1,0:T(8,128)(2,1)S(1)}, bf16[2,128,128]{2,1,0:T(8,128)(2,1)S(1)}, u32[]{:S(2)}, u32[]{:S(2)}) collective-permute-start(bf16[2,128,128]{2,1,0:T(8,128)(2,1)S(1)} %pad_maximum_fusion.refs_0_), channel_id=1, source_target_pairs={{0,4},{2,6},{4,0},{6,2},{8,12},{10,14},{12,8},{14,10},{1,5},{3,7},... | collective-permute-start | bytes 196616 | tf_op jit(solution)/shard_map/ppermute | solution.py:221
  29.2 1.4 %collective-permute-start.7 = (bf16[2,128,128]{2,1,0:T(8,128)(2,1)S(1)}, bf16[2,128,128]{2,1,0:T(8,128)(2,1)S(1)}, u32[]{:S(2)}, u32[]{:S(2)}) collective-permute-start(bf16[2,128,128]{2,1,0:T(8,128)(2,1)S(1)} %pad_maximum_fusion.refs_0_), channel_id=1, source_target_pairs={{0,2},{2,0},{4,6},{6,4},{8,10},{10,8},{12,14},{14,12},{1,3},{3,1},... | collective-permute-start | bytes 196616 | tf_op jit(solution)/shard_map/ppermute | solution.py:221
  30.6 1.7 %collective-permute-done.5.refs_1_ = bf16[2,128,128]{2,1,0:T(8,128)(2,1)S(1)} collective-permute-done((bf16[2,128,128]{2,1,0:T(8,128)(2,1)S(1)}, bf16[2,128,128]{2,1,0:T(8,128)(2,1)S(1)}, u32[]{:S(2)}, u32[]{:S(2)}) %collective-permute-start.5) | collective-permute-done | bytes 65568 | tf_op jit(solution)/shard_map/ppermute | solution.py:221
  32.3 0.8 %collective-permute-done.6.refs_2_ = bf16[2,128,128]{2,1,0:T(8,128)(2,1)S(1)} collective-permute-done((bf16[2,128,128]{2,1,0:T(8,128)(2,1)S(1)}, bf16[2,128,128]{2,1,0:T(8,128)(2,1)S(1)}, u32[]{:S(2)}, u32[]{:S(2)}) %collective-permute-start.6) | collective-permute-done | bytes 65568 | tf_op jit(solution)/shard_map/ppermute | solution.py:221
  33.0 0.4 %collective-permute-done.7.refs_3_ = bf16[2,128,128]{2,1,0:T(8,128)(2,1)S(1)} collective-permute-done((bf16[2,128,128]{2,1,0:T(8,128)(2,1)S(1)}, bf16[2,128,128]{2,1,0:T(8,128)(2,1)S(1)}, u32[]{:S(2)}, u32[]{:S(2)}) %collective-permute-start.7) | collective-permute-done | bytes 65568 | tf_op jit(solution)/shard_map/ppermute | solution.py:221
  33.5 0.0 copy-done
  33.5 2.4 %output.1 = (f32[16,2048]{1,0:T(8,128)S(1)}, bf16[1,16,2048]{2,1,0:T(8,128)(2,1)S(1)}) custom-call(bf16[4096,2048]{1,0:T(8,128)(2,1)S(1)} %copy-done, bf16[2,128,128]{2,1,0:T(8,128)(2,1)S(1)} %pad_maximum_fusion.refs_0_, bf16[2,128,128]{2,1,0:T(8,128)(2,1)S(1)} %collective-permute-done.5.refs_1_, bf16[2,128,128]{2,1,0:T(8,128)(2,1)S(1)} %collective-permute-done.6.refs_2_, ...), custom_call_target="tpu_custom_call" | custom-call | flops 536870912 | bytes 16777216 | tf_op jit(solution)/shard_map/output/pallas_call | solution.py:314
  35.9 0.1 collective-permute-start.8
  36.0 1.2 %collective-permute-done.8 = bf16[16,2048]{1,0:T(8,128)(2,1)S(1)} collective-permute-done((bf16[16,2048]{1,0:T(8,128)(2,1)S(1)}, bf16[16,2048]{1,0:T(8,128)(2,1)S(1)}, u32[]{:S(2)}, u32[]{:S(2)}) %collective-permute-start.8) | collective-permute-done | bytes 65568 | tf_op jit(solution)/shard_map/ppermute | solution.py:337
  37.2 0.6 %add_convert_fusion = bf16[16,2048]{1,0:T(8,128)(2,1)} fusion(f32[16,2048]{1,0:T(8,128)S(1)} %get-tuple-element.19, bf16[16,2048]{1,0:T(8,128)(2,1)S(1)} %collective-permute-done.8), kind=kLoop, calls=%fused_computation | loop fusion | flops 98304 | bytes 262144 | tf_op jit(solution)/shard_map/convert_element_type | solution.py:339
  (6 shorter events, 0.0 us)
Async XLA Ops:
  0.0 12.0 %copy-start.3 = (s32[4]{0:T(128)S(1)}, s32[4]{0:T(128)}, u32[]{:S(2)}) copy-start(s32[4]{0:T(128)} %param.15) | copy-start | bytes 52
  0.0 16.1 %copy-start.1 = (bf16[4,2,1024,128]{3,2,1,0:T(8,128)(2,1)S(1)}, bf16[4,2,1024,128]{3,2,1,0:T(8,128)(2,1)}, u32[]{:S(2)}) copy-start(bf16[4,2,1024,128]{3,2,1,0:T(8,128)(2,1)} %values.1) | copy-start | bytes 6291460
  0.0 21.1 %copy-start.2 = (bf16[4,2,1024,128]{3,2,1,0:T(8,128)(2,1)S(1)}, bf16[4,2,1024,128]{3,2,1,0:T(8,128)(2,1)}, u32[]{:S(2)}) copy-start(bf16[4,2,1024,128]{3,2,1,0:T(8,128)(2,1)} %keys.1) | copy-start | bytes 6291460
  0.0 33.5 %copy-start = (bf16[4096,2048]{1,0:T(8,128)(2,1)S(1)}, bf16[4096,2048]{1,0:T(8,128)(2,1)}, u32[]{:S(2)}) copy-start(bf16[4096,2048]{1,0:T(8,128)(2,1)} %w_ref.1) | copy-start | bytes 50331652
  7.2 6.7 %collective-permute-start = (bf16[288,128]{1,0:T(8,128)(2,1)S(1)}, bf16[288,128]{1,0:T(8,128)(2,1)S(1)}, u32[]{:S(2)}, u32[]{:S(2)}) collective-permute-start(bf16[288,128]{1,0:T(8,128)(2,1)S(1)} %get-tuple-element.14), channel_id=1, source_target_pairs={{0,6},{2,4},{4,2},{6,0},{8,14},{10,12},{12,10},{14,8},{1,7},{3,5},... | collective-permute-start | bytes 221192 | tf_op jit(solution)/shard_map/ppermute | solution.py:221
  11.3 4.4 %collective-permute-start.1 = (bf16[288,128]{1,0:T(8,128)(2,1)S(1)}, bf16[288,128]{1,0:T(8,128)(2,1)S(1)}, u32[]{:S(2)}, u32[]{:S(2)}) collective-permute-start(bf16[288,128]{1,0:T(8,128)(2,1)S(1)} %get-tuple-element.15), channel_id=1, source_target_pairs={{0,4},{2,6},{4,0},{6,2},{8,12},{10,14},{12,8},{14,10},{1,5},{3,7},... | collective-permute-start | bytes 221192 | tf_op jit(solution)/shard_map/ppermute | solution.py:221
  11.7 4.4 %collective-permute-start.2 = (bf16[288,128]{1,0:T(8,128)(2,1)S(1)}, bf16[288,128]{1,0:T(8,128)(2,1)S(1)}, u32[]{:S(2)}, u32[]{:S(2)}) collective-permute-start(bf16[288,128]{1,0:T(8,128)(2,1)S(1)} %get-tuple-element.16), channel_id=1, source_target_pairs={{0,2},{2,0},{4,6},{6,4},{8,10},{10,8},{12,14},{14,12},{1,3},{3,1},... | collective-permute-start | bytes 221192 | tf_op jit(solution)/shard_map/ppermute | solution.py:221
  16.2 4.9 %collective-permute-start.3 = (bf16[144,128]{1,0:T(8,128)(2,1)S(1)}, bf16[144,128]{1,0:T(8,128)(2,1)S(1)}, u32[]{:S(2)}, u32[]{:S(2)}) collective-permute-start(bf16[144,128]{1,0:T(8,128)(2,1)S(1)} %get-tuple-element.18), channel_id=1, source_target_pairs={{0,8},{2,10},{4,12},{6,14},{8,0},{10,2},{12,4},{14,6},{1,9},{3,11}... | collective-permute-start | bytes 110600 | tf_op jit(solution)/shard_map/ppermute | solution.py:226
  22.1 4.9 %collective-permute-start.4 = (bf16[128,128]{1,0:T(8,128)(2,1)S(1)}, bf16[128,128]{1,0:T(8,128)(2,1)S(1)}, u32[]{:S(2)}, u32[]{:S(2)}) collective-permute-start(bf16[128,128]{1,0:T(8,128)(2,1)S(1)} %attend.1), channel_id=1, source_target_pairs={{0,8},{2,10},{4,12},{6,14},{8,0},{10,2},{12,4},{14,6},{1,9},{3,11}... | collective-permute-start | bytes 98312 | tf_op jit(solution)/shard_map/ppermute | solution.py:226
  27.0 5.2 %collective-permute-start.5 = (bf16[2,128,128]{2,1,0:T(8,128)(2,1)S(1)}, bf16[2,128,128]{2,1,0:T(8,128)(2,1)S(1)}, u32[]{:S(2)}, u32[]{:S(2)}) collective-permute-start(bf16[2,128,128]{2,1,0:T(8,128)(2,1)S(1)} %pad_maximum_fusion.refs_0_), channel_id=1, source_target_pairs={{0,6},{2,4},{4,2},{6,0},{8,14},{10,12},{12,10},{14,8},{1,7},{3,5},... | collective-permute-start | bytes 196616 | tf_op jit(solution)/shard_map/ppermute | solution.py:221
  28.8 4.3 %collective-permute-start.6 = (bf16[2,128,128]{2,1,0:T(8,128)(2,1)S(1)}, bf16[2,128,128]{2,1,0:T(8,128)(2,1)S(1)}, u32[]{:S(2)}, u32[]{:S(2)}) collective-permute-start(bf16[2,128,128]{2,1,0:T(8,128)(2,1)S(1)} %pad_maximum_fusion.refs_0_), channel_id=1, source_target_pairs={{0,4},{2,6},{4,0},{6,2},{8,12},{10,14},{12,8},{14,10},{1,5},{3,7},... | collective-permute-start | bytes 196616 | tf_op jit(solution)/shard_map/ppermute | solution.py:221
  29.2 4.3 %collective-permute-start.7 = (bf16[2,128,128]{2,1,0:T(8,128)(2,1)S(1)}, bf16[2,128,128]{2,1,0:T(8,128)(2,1)S(1)}, u32[]{:S(2)}, u32[]{:S(2)}) collective-permute-start(bf16[2,128,128]{2,1,0:T(8,128)(2,1)S(1)} %pad_maximum_fusion.refs_0_), channel_id=1, source_target_pairs={{0,2},{2,0},{4,6},{6,4},{8,10},{10,8},{12,14},{14,12},{1,3},{3,1},... | collective-permute-start | bytes 196616 | tf_op jit(solution)/shard_map/ppermute | solution.py:221
  35.9 1.3 %collective-permute-start.8 = (bf16[16,2048]{1,0:T(8,128)(2,1)S(1)}, bf16[16,2048]{1,0:T(8,128)(2,1)S(1)}, u32[]{:S(2)}, u32[]{:S(2)}) collective-permute-start(bf16[16,2048]{1,0:T(8,128)(2,1)S(1)} %bitcast.4), channel_id=1, source_target_pairs={{0,1},{1,0},{2,3},{3,2},{4,5},{5,4},{6,7},{7,6},{8,9},{9,8},{10,11... | collective-permute-start | bytes 196616 | tf_op jit(solution)/shard_map/ppermute | solution.py:337

commit v8 on v7

--- a/solution.py
+++ b/solution.py
@@ -22,14 +22,14 @@
     t_copy = pltpu.make_async_copy(tokens_ref, t_buf, sems.at[0])
     k_copy = pltpu.make_async_copy(wk_ref, k_buf, sems.at[1])
     v_copy = pltpu.make_async_copy(wv_ref, v_buf, sems.at[2])
-    t_copy.start()
-    k_copy.start()
-    v_copy.start()
+    t_copy.start(priority=1)
+    k_copy.start(priority=1)
+    v_copy.start(priority=1)
     q_copies = []
     for c in range(depth // slab):
         at = slice(c * slab, (c + 1) * slab)
         q_copies.append((pltpu.make_async_copy(wq_ref.at[at, :], q_buf.at[at, :], sems.at[3 + c]), at))
-        q_copies[-1][0].start()
+        q_copies[-1][0].start(priority=1)
 
     row = lax.broadcasted_iota(jnp.int32, (rows, rows), 0)
     column = lax.broadcasted_iota(jnp.int32, (rows, rows), 1)
@@ -227,7 +227,7 @@
             x, "gx", [(h * low + i, int(partner(h, k, high)) * low + i) for h in range(high) for i in range(low)]
         )
 
-    slab = 256 if depth % 256 == 0 else depth
+    slab = 128 if depth % 128 == 0 else depth
 
     def device_at(p, q):
         me = lax.axis_index("gx")

time: 38 us -> 37.8 us (level)
  no operation moved by 1% of the time
where the time goes in v8:
time: 37.8 us; the launch traced here: 37.7 us
  starting transfers between devices  13.7 us (36%)
  waiting for transfers between devices  12.5 us (33%)
  Pallas kernels  10.5 us (28%)
  other arithmetic  0.84 us (2%)
    ppermute x6, starting transfers between devices, to_low(): lax.ppermute(x, 'gx', [(h * low + i, h * low + int(partner(i, k, low))) f...  8.25 us
    pallas_call x1, Pallas kernels, on_device(): pl.pallas_call(functools.partial(project_kernel, low, high, device_at, ow...  7.03 us
    ppermute x6, waiting for transfers between devices, to_low(): lax.ppermute(x, 'gx', [(h * low + i, h * low + int(partner(i, k, low))) f...  6.84 us
    ppermute x2, starting transfers between devices, to_high(): lax.ppermute(x, 'gx', [(h * low + i, int(partner(h, k, high)) * low + i)...  5.34 us
    ppermute x2, waiting for transfers between devices, to_high(): lax.ppermute(x, 'gx', [(h * low + i, int(partner(h, k, high)) * low + i)...  4.4 us
    pallas_call x1, Pallas kernels, on_device(): pl.pallas_call(functools.partial(output_kernel, gy, (0, *order)), out_sha...  2.43 us
    ppermute x1, waiting for transfers between devices, on_device(): lax.ppermute(other[j - 1], 'gy', [(i, (i + j) % gy) for i in range(gy)])  1.24 us
    pallas_call x1, Pallas kernels, on_device(): pl.pallas_call(attend_kernel, out_shape=jax.ShapeDtypeStruct((own_rows *...  1 us
  transfers between devices with their start and end apart: 9, of which 9 were waited for; matrix products, arithmetic and copies ran while one was open for 1% of the time, Pallas kernels for 0%

profile of v8, /device:TPU:0, one launch (start us, length us, event | category | flops | bytes accessed | tf_op | source)
XLA Modules:
  0.0 37.7 jit_solution(1182429914275256471)
XLA Ops:
  0.0 0.0 copy-start.3
  0.0 0.0 copy-start.1
  0.0 7.0 %project.1 = (f32[288,128]{1,0:T(8,128)S(1)}, bf16[288,128]{1,0:T(8,128)(2,1)S(1)}, bf16[288,128]{1,0:T(8,128)(2,1)S(1)}, bf16[288,128]{1,0:T(8,128)(2,1)S(1)}) custom-call(bf16[32,2048]{1,0:T(8,128)(2,1)} %tokens_ref.1, bf16[2048,4096]{1,0:T(8,128)(2,1)} %wq_ref.1, bf16[2048,256]{1,0:T(8,128)(2,1)} %wk_ref.1, bf16[2048,256]{1,0:T(8,128)(2,1)} %wv_ref.1), custom_call_target="tpu_custom_call" | custom-call | flops 603979776 | bytes 18874368 | tf_op jit(solution)/shard_map/project/pallas_call | solution.py:237
  7.0 4.1 %collective-permute-start = (bf16[288,128]{1,0:T(8,128)(2,1)S(1)}, bf16[288,128]{1,0:T(8,128)(2,1)S(1)}, u32[]{:S(2)}, u32[]{:S(2)}) collective-permute-start(bf16[288,128]{1,0:T(8,128)(2,1)S(1)} %get-tuple-element.14), channel_id=1, source_target_pairs={{0,6},{2,4},{4,2},{6,0},{8,14},{10,12},{12,10},{14,8},{1,7},{3,5},... | collective-permute-start | bytes 221192 | tf_op jit(solution)/shard_map/ppermute | solution.py:221
  11.1 0.4 %collective-permute-start.1 = (bf16[288,128]{1,0:T(8,128)(2,1)S(1)}, bf16[288,128]{1,0:T(8,128)(2,1)S(1)}, u32[]{:S(2)}, u32[]{:S(2)}) collective-permute-start(bf16[288,128]{1,0:T(8,128)(2,1)S(1)} %get-tuple-element.15), channel_id=1, source_target_pairs={{0,4},{2,6},{4,0},{6,2},{8,12},{10,14},{12,8},{14,10},{1,5},{3,7},... | collective-permute-start | bytes 221192 | tf_op jit(solution)/shard_map/ppermute | solution.py:221
  11.6 0.2 collective-permute-start.2
  11.8 0.0 copy-done.3
  11.8 0.1 multiply_cosine_fusion
  11.9 0.1 pad.11.clone
  12.0 1.8 %collective-permute-done.refs_0_ = bf16[288,128]{1,0:T(8,128)(2,1)S(1)} collective-permute-done((bf16[288,128]{1,0:T(8,128)(2,1)S(1)}, bf16[288,128]{1,0:T(8,128)(2,1)S(1)}, u32[]{:S(2)}, u32[]{:S(2)}) %collective-permute-start) | collective-permute-done | bytes 73760 | tf_op jit(solution)/shard_map/ppermute | solution.py:221
  13.7 1.7 %collective-permute-done.1.refs_1_ = bf16[288,128]{1,0:T(8,128)(2,1)S(1)} collective-permute-done((bf16[288,128]{1,0:T(8,128)(2,1)S(1)}, bf16[288,128]{1,0:T(8,128)(2,1)S(1)}, u32[]{:S(2)}, u32[]{:S(2)}) %collective-permute-start.1) | collective-permute-done | bytes 73760 | tf_op jit(solution)/shard_map/ppermute | solution.py:221
  15.5 0.4 %collective-permute-done.2.refs_2_ = bf16[288,128]{1,0:T(8,128)(2,1)S(1)} collective-permute-done((bf16[288,128]{1,0:T(8,128)(2,1)S(1)}, bf16[288,128]{1,0:T(8,128)(2,1)S(1)}, u32[]{:S(2)}, u32[]{:S(2)}) %collective-permute-start.2) | collective-permute-done | bytes 73760 | tf_op jit(solution)/shard_map/ppermute | solution.py:221
  15.9 0.0 copy-done.1
  15.9 0.1 combine.1
  16.0 2.7 %collective-permute-start.3 = (bf16[144,128]{1,0:T(8,128)(2,1)S(1)}, bf16[144,128]{1,0:T(8,128)(2,1)S(1)}, u32[]{:S(2)}, u32[]{:S(2)}) collective-permute-start(bf16[144,128]{1,0:T(8,128)(2,1)S(1)} %get-tuple-element.18), channel_id=1, source_target_pairs={{0,8},{2,10},{4,12},{6,14},{8,0},{10,2},{12,4},{14,6},{1,9},{3,11}... | collective-permute-start | bytes 110600 | tf_op jit(solution)/shard_map/ppermute | solution.py:226
  18.6 0.1 maximum_maximum_fusion.table_ref
  18.7 2.2 %collective-permute-done.3.refs_1_ = bf16[144,128]{1,0:T(8,128)(2,1)S(1)} collective-permute-done((bf16[144,128]{1,0:T(8,128)(2,1)S(1)}, bf16[144,128]{1,0:T(8,128)(2,1)S(1)}, u32[]{:S(2)}, u32[]{:S(2)}) %collective-permute-start.3) | collective-permute-done | bytes 36896 | tf_op jit(solution)/shard_map/ppermute | solution.py:226
  20.9 0.0 copy-done.2
  20.9 1.0 %attend.1 = bf16[128,128]{1,0:T(8,128)(2,1)S(1)} custom-call(f32[24,128]{1,0:T(8,128)S(1)} %maximum_maximum_fusion.table_ref, bf16[4,2,1024,128]{3,2,1,0:T(8,128)(2,1)S(1)} %copy-done.2, bf16[4,2,1024,128]{3,2,1,0:T(8,128)(2,1)S(1)} %copy-done.1, f32[144,128]{1,0:T(8,128)S(1)} %get-tuple-element.17.refs_0_, bf16[144,128]{1,0:T(8,128)(2,1)S(1)} %collective-permute-done.3.refs_1_), custom_call_target="tpu_custom_call" | custom-call | flops 67108864 | bytes 4194304 | tf_op jit(solution)/shard_map/attend/pallas_call | solution.py:297
  21.9 2.7 %collective-permute-start.4 = (bf16[128,128]{1,0:T(8,128)(2,1)S(1)}, bf16[128,128]{1,0:T(8,128)(2,1)S(1)}, u32[]{:S(2)}, u32[]{:S(2)}) collective-permute-start(bf16[128,128]{1,0:T(8,128)(2,1)S(1)} %attend.1), channel_id=1, source_target_pairs={{0,8},{2,10},{4,12},{6,14},{8,0},{10,2},{12,4},{14,6},{1,9},{3,11}... | collective-permute-start | bytes 98312 | tf_op jit(solution)/shard_map/ppermute | solution.py:226
  24.6 2.2 %collective-permute-done.4 = bf16[128,128]{1,0:T(8,128)(2,1)S(1)} collective-permute-done((bf16[128,128]{1,0:T(8,128)(2,1)S(1)}, bf16[128,128]{1,0:T(8,128)(2,1)S(1)}, u32[]{:S(2)}, u32[]{:S(2)}) %collective-permute-start.4) | collective-permute-done | bytes 32800 | tf_op jit(solution)/shard_map/ppermute | solution.py:226
  26.8 1.7 %collective-permute-start.5 = (bf16[2,128,128]{2,1,0:T(8,128)(2,1)S(1)}, bf16[2,128,128]{2,1,0:T(8,128)(2,1)S(1)}, u32[]{:S(2)}, u32[]{:S(2)}) collective-permute-start(bf16[2,128,128]{2,1,0:T(8,128)(2,1)S(1)} %pad_maximum_fusion.refs_0_), channel_id=1, source_target_pairs={{0,6},{2,4},{4,2},{6,0},{8,14},{10,12},{12,10},{14,8},{1,7},{3,5},... | collective-permute-start | bytes 196616 | tf_op jit(solution)/shard_map/ppermute | solution.py:221
  28.6 0.4 %collective-permute-start.6 = (bf16[2,128,128]{2,1,0:T(8,128)(2,1)S(1)}, bf16[2,128,128]{2,1,0:T(8,128)(2,1)S(1)}, u32[]{:S(2)}, u32[]{:S(2)}) collective-permute-start(bf16[2,128,128]{2,1,0:T(8,128)(2,1)S(1)} %pad_maximum_fusion.refs_0_), channel_id=1, source_target_pairs={{0,4},{2,6},{4,0},{6,2},{8,12},{10,14},{12,8},{14,10},{1,5},{3,7},... | collective-permute-start | bytes 196616 | tf_op jit(solution)/shard_map/ppermute | solution.py:221
  29.0 1.4 %collective-permute-start.7 = (bf16[2,128,128]{2,1,0:T(8,128)(2,1)S(1)}, bf16[2,128,128]{2,1,0:T(8,128)(2,1)S(1)}, u32[]{:S(2)}, u32[]{:S(2)}) collective-permute-start(bf16[2,128,128]{2,1,0:T(8,128)(2,1)S(1)} %pad_maximum_fusion.refs_0_), channel_id=1, source_target_pairs={{0,2},{2,0},{4,6},{6,4},{8,10},{10,8},{12,14},{14,12},{1,3},{3,1},... | collective-permute-start | bytes 196616 | tf_op jit(solution)/shard_map/ppermute | solution.py:221
  30.4 1.7 %collective-permute-done.5.refs_1_ = bf16[2,128,128]{2,1,0:T(8,128)(2,1)S(1)} collective-permute-done((bf16[2,128,128]{2,1,0:T(8,128)(2,1)S(1)}, bf16[2,128,128]{2,1,0:T(8,128)(2,1)S(1)}, u32[]{:S(2)}, u32[]{:S(2)}) %collective-permute-start.5) | collective-permute-done | bytes 65568 | tf_op jit(solution)/shard_map/ppermute | solution.py:221
  32.1 0.8 %collective-permute-done.6.refs_2_ = bf16[2,128,128]{2,1,0:T(8,128)(2,1)S(1)} collective-permute-done((bf16[2,128,128]{2,1,0:T(8,128)(2,1)S(1)}, bf16[2,128,128]{2,1,0:T(8,128)(2,1)S(1)}, u32[]{:S(2)}, u32[]{:S(2)}) %collective-permute-start.6) | collective-permute-done | bytes 65568 | tf_op jit(solution)/shard_map/ppermute | solution.py:221
  32.8 0.4 %collective-permute-done.7.refs_3_ = bf16[2,128,128]{2,1,0:T(8,128)(2,1)S(1)} collective-permute-done((bf16[2,128,128]{2,1,0:T(8,128)(2,1)S(1)}, bf16[2,128,128]{2,1,0:T(8,128)(2,1)S(1)}, u32[]{:S(2)}, u32[]{:S(2)}) %collective-permute-start.7) | collective-permute-done | bytes 65568 | tf_op jit(solution)/shard_map/ppermute | solution.py:221
  33.3 0.0 copy-done
  33.3 2.4 %output.1 = (f32[16,2048]{1,0:T(8,128)S(1)}, bf16[1,16,2048]{2,1,0:T(8,128)(2,1)S(1)}) custom-call(bf16[4096,2048]{1,0:T(8,128)(2,1)S(1)} %copy-done, bf16[2,128,128]{2,1,0:T(8,128)(2,1)S(1)} %pad_maximum_fusion.refs_0_, bf16[2,128,128]{2,1,0:T(8,128)(2,1)S(1)} %collective-permute-done.5.refs_1_, bf16[2,128,128]{2,1,0:T(8,128)(2,1)S(1)} %collective-permute-done.6.refs_2_, ...), custom_call_target="tpu_custom_call" | custom-call | flops 536870912 | bytes 16777216 | tf_op jit(solution)/shard_map/output/pallas_call | solution.py:314
  35.7 0.1 collective-permute-start.8
  35.8 1.2 %collective-permute-done.8 = bf16[16,2048]{1,0:T(8,128)(2,1)S(1)} collective-permute-done((bf16[16,2048]{1,0:T(8,128)(2,1)S(1)}, bf16[16,2048]{1,0:T(8,128)(2,1)S(1)}, u32[]{:S(2)}, u32[]{:S(2)}) %collective-permute-start.8) | collective-permute-done | bytes 65568 | tf_op jit(solution)/shard_map/ppermute | solution.py:337
  37.0 0.6 %add_convert_fusion = bf16[16,2048]{1,0:T(8,128)(2,1)} fusion(f32[16,2048]{1,0:T(8,128)S(1)} %get-tuple-element.19, bf16[16,2048]{1,0:T(8,128)(2,1)S(1)} %collective-permute-done.8), kind=kLoop, calls=%fused_computation | loop fusion | flops 98304 | bytes 262144 | tf_op jit(solution)/shard_map/convert_element_type | solution.py:339
  (6 shorter events, 0.0 us)
Async XLA Ops:
  0.0 11.8 %copy-start.3 = (s32[4]{0:T(128)S(1)}, s32[4]{0:T(128)}, u32[]{:S(2)}) copy-start(s32[4]{0:T(128)} %param.15) | copy-start | bytes 52
  0.0 15.9 %copy-start.1 = (bf16[4,2,1024,128]{3,2,1,0:T(8,128)(2,1)S(1)}, bf16[4,2,1024,128]{3,2,1,0:T(8,128)(2,1)}, u32[]{:S(2)}) copy-start(bf16[4,2,1024,128]{3,2,1,0:T(8,128)(2,1)} %values.1) | copy-start | bytes 6291460
  0.0 20.9 %copy-start.2 = (bf16[4,2,1024,128]{3,2,1,0:T(8,128)(2,1)S(1)}, bf16[4,2,1024,128]{3,2,1,0:T(8,128)(2,1)}, u32[]{:S(2)}) copy-start(bf16[4,2,1024,128]{3,2,1,0:T(8,128)(2,1)} %keys.1) | copy-start | bytes 6291460
  0.0 33.3 %copy-start = (bf16[4096,2048]{1,0:T(8,128)(2,1)S(1)}, bf16[4096,2048]{1,0:T(8,128)(2,1)}, u32[]{:S(2)}) copy-start(bf16[4096,2048]{1,0:T(8,128)(2,1)} %w_ref.1) | copy-start | bytes 50331652
  7.0 6.7 %collective-permute-start = (bf16[288,128]{1,0:T(8,128)(2,1)S(1)}, bf16[288,128]{1,0:T(8,128)(2,1)S(1)}, u32[]{:S(2)}, u32[]{:S(2)}) collective-permute-start(bf16[288,128]{1,0:T(8,128)(2,1)S(1)} %get-tuple-element.14), channel_id=1, source_target_pairs={{0,6},{2,4},{4,2},{6,0},{8,14},{10,12},{12,10},{14,8},{1,7},{3,5},... | collective-permute-start | bytes 221192 | tf_op jit(solution)/shard_map/ppermute | solution.py:221
  11.1 4.4 %collective-permute-start.1 = (bf16[288,128]{1,0:T(8,128)(2,1)S(1)}, bf16[288,128]{1,0:T(8,128)(2,1)S(1)}, u32[]{:S(2)}, u32[]{:S(2)}) collective-permute-start(bf16[288,128]{1,0:T(8,128)(2,1)S(1)} %get-tuple-element.15), channel_id=1, source_target_pairs={{0,4},{2,6},{4,0},{6,2},{8,12},{10,14},{12,8},{14,10},{1,5},{3,7},... | collective-permute-start | bytes 221192 | tf_op jit(solution)/shard_map/ppermute | solution.py:221
  11.6 4.4 %collective-permute-start.2 = (bf16[288,128]{1,0:T(8,128)(2,1)S(1)}, bf16[288,128]{1,0:T(8,128)(2,1)S(1)}, u32[]{:S(2)}, u32[]{:S(2)}) collective-permute-start(bf16[288,128]{1,0:T(8,128)(2,1)S(1)} %get-tuple-element.16), channel_id=1, source_target_pairs={{0,2},{2,0},{4,6},{6,4},{8,10},{10,8},{12,14},{14,12},{1,3},{3,1},... | collective-permute-start | bytes 221192 | tf_op jit(solution)/shard_map/ppermute | solution.py:221
  16.0 4.9 %collective-permute-start.3 = (bf16[144,128]{1,0:T(8,128)(2,1)S(1)}, bf16[144,128]{1,0:T(8,128)(2,1)S(1)}, u32[]{:S(2)}, u32[]{:S(2)}) collective-permute-start(bf16[144,128]{1,0:T(8,128)(2,1)S(1)} %get-tuple-element.18), channel_id=1, source_target_pairs={{0,8},{2,10},{4,12},{6,14},{8,0},{10,2},{12,4},{14,6},{1,9},{3,11}... | collective-permute-start | bytes 110600 | tf_op jit(solution)/shard_map/ppermute | solution.py:226
  21.9 4.9 %collective-permute-start.4 = (bf16[128,128]{1,0:T(8,128)(2,1)S(1)}, bf16[128,128]{1,0:T(8,128)(2,1)S(1)}, u32[]{:S(2)}, u32[]{:S(2)}) collective-permute-start(bf16[128,128]{1,0:T(8,128)(2,1)S(1)} %attend.1), channel_id=1, source_target_pairs={{0,8},{2,10},{4,12},{6,14},{8,0},{10,2},{12,4},{14,6},{1,9},{3,11}... | collective-permute-start | bytes 98312 | tf_op jit(solution)/shard_map/ppermute | solution.py:226
  26.8 5.2 %collective-permute-start.5 = (bf16[2,128,128]{2,1,0:T(8,128)(2,1)S(1)}, bf16[2,128,128]{2,1,0:T(8,128)(2,1)S(1)}, u32[]{:S(2)}, u32[]{:S(2)}) collective-permute-start(bf16[2,128,128]{2,1,0:T(8,128)(2,1)S(1)} %pad_maximum_fusion.refs_0_), channel_id=1, source_target_pairs={{0,6},{2,4},{4,2},{6,0},{8,14},{10,12},{12,10},{14,8},{1,7},{3,5},... | collective-permute-start | bytes 196616 | tf_op jit(solution)/shard_map/ppermute | solution.py:221
  28.6 4.3 %collective-permute-start.6 = (bf16[2,128,128]{2,1,0:T(8,128)(2,1)S(1)}, bf16[2,128,128]{2,1,0:T(8,128)(2,1)S(1)}, u32[]{:S(2)}, u32[]{:S(2)}) collective-permute-start(bf16[2,128,128]{2,1,0:T(8,128)(2,1)S(1)} %pad_maximum_fusion.refs_0_), channel_id=1, source_target_pairs={{0,4},{2,6},{4,0},{6,2},{8,12},{10,14},{12,8},{14,10},{1,5},{3,7},... | collective-permute-start | bytes 196616 | tf_op jit(solution)/shard_map/ppermute | solution.py:221
  29.0 4.3 %collective-permute-start.7 = (bf16[2,128,128]{2,1,0:T(8,128)(2,1)S(1)}, bf16[2,128,128]{2,1,0:T(8,128)(2,1)S(1)}, u32[]{:S(2)}, u32[]{:S(2)}) collective-permute-start(bf16[2,128,128]{2,1,0:T(8,128)(2,1)S(1)} %pad_maximum_fusion.refs_0_), channel_id=1, source_target_pairs={{0,2},{2,0},{4,6},{6,4},{8,10},{10,8},{12,14},{14,12},{1,3},{3,1},... | collective-permute-start | bytes 196616 | tf_op jit(solution)/shard_map/ppermute | solution.py:221
  35.7 1.3 %collective-permute-start.8 = (bf16[16,2048]{1,0:T(8,128)(2,1)S(1)}, bf16[16,2048]{1,0:T(8,128)(2,1)S(1)}, u32[]{:S(2)}, u32[]{:S(2)}) collective-permute-start(bf16[16,2048]{1,0:T(8,128)(2,1)S(1)} %bitcast.4), channel_id=1, source_target_pairs={{0,1},{1,0},{2,3},{3,2},{4,5},{5,4},{6,7},{7,6},{8,9},{9,8},{10,11... | collective-permute-start | bytes 196616 | tf_op jit(solution)/shard_map/ppermute | solution.py:337
